TPU v7x, 256 devices: a whole 4x4x8 slice. The times are simulated.
256 devices in a mesh: fsdp: 16 (over y_lo, z), sample: 16 (over y_hi, x, core).
Axes of the slice: x: 4, y: 4 (y_hi: 2, y_lo: 2; y = y_hi * 2 + y_lo), z: 8, core: 2. Of those that a mesh axis runs over, the one named last changes fastest.
Arguments:
- hidden: bfloat16 [4, 256, 16, 5120], P(None, 'fsdp', 'sample'), may hold values from -6 to 6
- norm_gain: float32 [5120], replicated, may hold values from 0.5 to 1.5
- w_qkv: bfloat16 [5120, 5120], P(None, 'fsdp'), may hold values from -0.078125 to 0.078125
- query_gain: float32 [128], replicated, may hold values from 0.5 to 5
- key_gain: float32 [128], replicated, may hold values from 0.5 to 4
- prompt_kv: bfloat16 [16, 128, 64, 1024], P('fsdp', 'sample')
- block_table: int32 [16, 16, 8], P('fsdp', 'sample'), may hold values from 0 to 7, as said below
- prompt_slot: int32 [16, 16], P('fsdp'), may hold values from 0 to 15, each once within a row
- prompt_len: int32 [16, 16], P('fsdp'), may hold values from 1 to 512
- resp_kv: bfloat16 [256, 16, 128, 1024], P('fsdp', 'sample')
- resp_len: int32 [256, 16], P('fsdp', 'sample'), may hold values from 1 to 128
Outputs:
- attention: bfloat16 [4, 256, 16, 4096], P(None, 'fsdp', 'sample')
Inputs may be any that keep to these rules, and one draw needn't show every extreme that they name: `block_table`: the rows of slots j * 1 to (j + 1) - 1 of a group, together, name each of the 8 pages of pool rows j * 8 onward exactly once.
All inputs are finite; a program needn't handle non-finite values.
Results may differ from a plain program's by a relative error of at most 0.019.
The roundings to bfloat16 on the way count: a program that leaves them out, or rounds other values in their place, can miss the bound.
Values may be sent and summed in bfloat16 or wider, within the bound.
No kernel may reach another device: no remote copies, remote signals or barrier semaphores. Data moves between devices by JAX's collectives and lax.ppermute only.
A program may use at most 128 MiB of HBM per device.

v0:
```python
import jax
import jax.numpy as jnp
from jax import lax
from jax.sharding import PartitionSpec as P

D = 5120
HD = 128
HEADS = 32
KV_HEADS = 4
QD = 4096
KVD = 512


def rms_scale(values_in, scale_gain):
    return (
        values_in
        * lax.rsqrt(jnp.mean(values_in * values_in, axis=-1, keepdims=True) + 1e-06)
        * scale_gain
    )


def rotary(values_in, positions):
    width = values_in.shape[-1]
    half_width = width // 2
    inv_freq = jnp.exp(
        -jnp.log(1000000.0) * jnp.arange(half_width, dtype=jnp.float32) * 2.0 / width
    )
    angles = positions.astype(jnp.float32)[..., None, None] * inv_freq
    cosine = jnp.cos(angles)
    sine = jnp.sin(angles)
    first = values_in[..., :half_width]
    second = values_in[..., half_width:]
    return jnp.concatenate(
        [first * cosine - second * sine, second * cosine + first * sine], axis=-1
    )


def attend(queries, key_vals, valid_mask):
    feature = key_vals.shape[-1] // 2
    count, length = (key_vals.shape[0], key_vals.shape[1])
    head_dim = queries.shape[-1]
    key_part = key_vals[..., :feature].reshape(count, length, KV_HEADS, head_dim)
    value_part = key_vals[..., feature:].reshape(count, length, KV_HEADS, head_dim)
    scores = jnp.einsum(
        "nrkgd,nlkd->nrkgl", queries, key_part, preferred_element_type=jnp.float32
    ) * head_dim ** (-0.5)
    scores = jnp.where(valid_mask[:, :, None, None, :], scores, -1e30)
    row_max = jnp.max(scores, axis=-1)
    weights = jnp.exp(scores - row_max[..., None])
    row_sum = jnp.sum(weights, axis=-1)
    mixed = jnp.einsum(
        "nrkgl,nlkd->nrkgd",
        weights.astype(jnp.bfloat16),
        value_part,
        preferred_element_type=jnp.float32,
    )
    return (row_max, row_sum, mixed)


def combine(first, second):
    max_one, sum_one, mix_one = first
    max_two, sum_two, mix_two = second
    peak = jnp.maximum(max_one, max_two)
    factor_one = jnp.exp(max_one - peak)
    factor_two = jnp.exp(max_two - peak)
    numer = mix_one * factor_one[..., None] + mix_two * factor_two[..., None]
    denom = sum_one * factor_one + sum_two * factor_two
    return (numer / denom[..., None]).astype(jnp.bfloat16)


def per_device(
    hidden,
    norm_gain,
    w_qkv,
    query_gain,
    key_gain,
    prompt_kv,
    block_table,
    prompt_slot,
    prompt_len,
    resp_kv,
    resp_len,
):
    step_count, prompt_count = (hidden.shape[0], hidden.shape[1])
    group_size = HEADS // KV_HEADS
    wide = hidden.reshape(step_count * prompt_count, D).astype(jnp.float32)
    normed = rms_scale(wide, norm_gain).astype(jnp.bfloat16)
    own_columns = jnp.dot(
        lax.all_gather(normed, "fsdp", axis=0, tiled=True),
        w_qkv,
        preferred_element_type=jnp.float32,
    ).astype(jnp.bfloat16)
    projected = lax.all_to_all(own_columns, "fsdp", split_axis=0, concat_axis=1, tiled=True)
    projected = projected.reshape(step_count, prompt_count, QD + 2 * KVD)
    lengths = prompt_len[0]
    cache_len = resp_len[:, 0]
    positions = (
        lengths[None, :] + cache_len[None, :] + jnp.arange(step_count, dtype=jnp.int32)[:, None]
    )
    query_raw = projected[..., :QD].astype(jnp.float32).reshape(step_count, prompt_count, HEADS, HD)
    key_raw = (
        projected[..., QD : QD + KVD]
        .astype(jnp.float32)
        .reshape(step_count, prompt_count, KV_HEADS, HD)
    )
    queries = rotary(rms_scale(query_raw, query_gain), positions).astype(jnp.bfloat16)
    queries = queries.reshape(step_count, prompt_count, KV_HEADS, group_size, HD).transpose(
        1, 0, 2, 3, 4
    )
    key_new = rotary(rms_scale(key_raw, key_gain), positions).astype(jnp.bfloat16)
    new_kv = jnp.concatenate(
        [key_new.reshape(step_count, prompt_count, KVD), projected[..., QD + KVD :]], axis=-1
    )
    new_kv = new_kv.transpose(1, 0, 2)
    joined = jnp.concatenate([resp_kv[:, 0], new_kv], axis=1)
    cache_room = resp_kv.shape[2]
    spots = jnp.arange(cache_room + step_count, dtype=jnp.int32)[None, None, :]
    step_ids = jnp.arange(step_count, dtype=jnp.int32)[None, :, None]
    resp_mask = jnp.where(
        spots < cache_room, spots < cache_len[:, None, None], spots - cache_room <= step_ids
    )
    response_stats = attend(queries, joined, resp_mask)
    slot_of = prompt_slot[0]
    own_count = block_table.shape[1]
    pool_pages = prompt_kv.shape[1]
    prefix_room = block_table.shape[2] * prompt_kv.shape[2]
    feature_pair = prompt_kv.shape[3]
    pool, tables = (
        lax.all_gather(prompt_kv[0], "sample", axis=0, tiled=True),
        lax.all_gather(block_table[0], "sample", axis=0, tiled=True),
    )
    page_rows = jnp.take(tables, slot_of, axis=0) + (slot_of // own_count * pool_pages)[:, None]
    prefix_kv = jnp.take(pool, page_rows, axis=0).reshape(prompt_count, prefix_room, feature_pair)
    prefix_mask = (jnp.arange(prefix_room, dtype=jnp.int32)[None, :] < lengths[:, None])[:, None, :]
    prefix_stats = attend(queries, prefix_kv, prefix_mask)
    mixed = combine(prefix_stats, response_stats)
    return mixed.transpose(1, 0, 2, 3, 4).reshape(step_count, prompt_count, 1, QD)


def solution(mesh):
    placed = (
        P(None, "fsdp", "sample", None),
        P(),
        P(None, "fsdp"),
        P(),
        P(),
        P("fsdp", "sample", None, None),
        P("fsdp", "sample", None),
        P("fsdp", None),
        P("fsdp", None),
        P("fsdp", "sample", None, None),
        P("fsdp", "sample"),
    )
    return jax.shard_map(
        per_device,
        mesh=mesh,
        in_specs=placed,
        out_specs=P(None, "fsdp", "sample", None),
        check_vma=False,
    )
```

profile of v0, /device:TPU:1, one launch (start us, length us, event | category | flops | bytes accessed | tf_op | source)
XLA Modules:
  0.0 341.6 jit_solution(14728971865391097929)
XLA Ops:
  6.5 1.4 multiply_reduce_fusion
  8.1 2.2 fusion.34
  10.4 0.7 all-gather.7.cloned.1.call-update
  11.1 25.7 %all-gather = s32[16,1,8]{2,1,0:T(1,128)S(1)} all-gather(s32[1,1,8]{2,1,0:T(1,128)} %param.17), channel_id=2, replica_groups=mesh['fsdp'=16,'sample'=16] {'sample'}, dimensions={0}, use_global_device_ids=true | all-gather | bytes 544 | tf_op jit(solution)/shard_map/all_gather | solution.py:130
  36.7 0.7 fusion.56
  37.4 0.6 gather_fusion
  38.0 0.7 bitcast_multiply_fusion.5
  38.7 0.7 compare_and_fusion.1
  39.9 0.7 fusion.57
  40.6 95.8 %all-gather.5.cloned.1.call-done = bf16[1024,5120]{1,0:T(8,128)(2,1)} async-done(((bf16[64,5120]{1,0:T(8,128)(2,1)}), bf16[1024,5120]{1,0:T(8,128)(2,1)}) %all-gather.5.cloned.1.call-update) | async-done | bytes 10485776 | tf_op jit(solution)/shard_map/all_gather | solution.py:89
  136.3 7.2 %convolution_convert_fusion = bf16[1024,320]{0,1:T(8,128)(2,1)} fusion(bf16[1024,5120]{1,0:T(8,128)(2,1)} %all-gather.5.cloned.1.call-done, bf16[5120,320]{0,1:T(8,128)(2,1)S(1)} %copy-done), kind=kOutput, calls=%fused_computation.30 | convolution fusion | flops 3355770880 | bytes 14417920 | tf_op jit(solution)/shard_map/dot_general | solution.py:88
  143.6 2.3 copy.59
  145.8 4.1 %all-to-all-start = ((bf16[16,64,320]{2,1,0:T(8,128)(2,1)}), bf16[16,64,320]{2,1,0:T(8,128)(2,1)S(1)}, u32[]{:S(2)}, u32[]{:S(2)}) async-start(bf16[16,64,320]{2,1,0:T(8,128)(2,1)} %bitcast.14), calls=%async_computation | async-start | bytes 1572864 | tf_op jit(solution)/shard_map/all_to_all | solution.py:93
  150.4 19.3 %all-to-all-done = bf16[16,64,320]{2,1,0:T(8,128)(2,1)S(1)} async-done(((bf16[16,64,320]{2,1,0:T(8,128)(2,1)}), bf16[16,64,320]{2,1,0:T(8,128)(2,1)S(1)}, u32[]{:S(2)}, u32[]{:S(2)}) %all-to-all-start) | async-done | bytes 655392 | tf_op jit(solution)/shard_map/all_to_all | solution.py:93
  170.2 0.6 reshape.348
  172.0 3.5 %pad_maximum_fusion = (bf16[16,132,512]{2,1,0:T(8,128)(2,1)S(1)}, bf16[16,132,512]{2,1,0:T(8,128)(2,1)}) fusion(bf16[16,4,1024]{2,1,0:T(4,128)(2,1)S(1)} %copy.65, bf16[16,128,1024]{2,1,0:T(8,128)(2,1)} %bitcast.138), kind=kLoop, calls=%fused_computation.12 | loop fusion | flops 8650752 | bytes 8650752 | tf_op jit(solution)/shard_map/concatenate | solution.py:115
  175.5 4.1 %reshape.385 = bf16[16,132,4,128]{3,2,1,0:T(4,128)(2,1)} reshape(bf16[16,132,512]{2,1,0:T(8,128)(2,1)} %get-tuple-element.11) | data formatting | bytes 4325376 | tf_op jit(solution)/shard_map/reshape | solution.py:42
  179.6 2.2 reshape.386
  183.4 1.7 fusion.63
  185.1 0.8 fusion.14
  185.9 74.5 %all-gather.7.cloned.1.call-done = bf16[1,128,64,1024]{3,2,0,1:T(8,128)(2,1)} async-done(((bf16[1,8,64,1024]{3,2,0,1:T(8,128)(2,1)}), bf16[1,128,64,1024]{3,2,0,1:T(8,128)(2,1)}) %all-gather.7.cloned.1.call-update) | async-done | bytes 16777232 | tf_op jit(solution)/shard_map/all_gather | solution.py:129
  260.4 14.1 %gather_fusion.1 = bf16[128,64,1024]{2,1,0:T(8,128)(2,1)} fusion(bf16[128,64,1024]{2,1,0:T(8,128)(2,1)} %bitcast.133, s32[1024]{0:T(1024)S(1)} %pad_clamp_fusion), kind=kCustom, calls=%fused_computation.1 | custom fusion | bytes 33554944 | tf_op jit(solution)/shard_map/jit(_take)/gather | solution.py:133
  274.5 8.6 %bitcast_select_fusion = bf16[16,512,1024]{2,1,0:T(8,128)(2,1)S(1)} fusion(pred[16,512]{1,0:T(8,128)(4,1)S(1)} %broadcast_in_dim.100, bf16[16,512,1024]{2,1,0:T(8,128)(2,1)} %bitcast.132), kind=kLoop, calls=%fused_computation.2 | loop fusion | flops 8388608 | bytes 33562624 | tf_op jit(solution)/shard_map/jit(_take)/select_n | solution.py:133
  283.1 6.3 %fusion.62 = (bf16[16,512,512]{2,1,0:T(8,128)(2,1)}, bf16[16,512,512]{2,1,0:T(8,128)(2,1)}) fusion(bf16[16,512,1024]{2,1,0:T(8,128)(2,1)S(1)} %bitcast_select_fusion), kind=kLoop, calls=%fused_computation.97 | loop fusion | bytes 33554432 | tf_op jit(solution)/shard_map/slice | solution.py:42
  289.4 12.3 %copy.57 = bf16[16,512,512]{1,2,0:T(8,128)(2,1)} copy(bf16[16,512,512]{2,1,0:T(8,128)(2,1)} %get-tuple-element.9) | data formatting | bytes 16777216 | tf_op jit(solution)/shard_map/slice | solution.py:43
  301.7 12.3 %copy.58 = bf16[16,512,512]{1,2,0:T(8,128)(2,1)} copy(bf16[16,512,512]{2,1,0:T(8,128)(2,1)} %get-tuple-element.8) | data formatting | bytes 16777216 | tf_op jit(solution)/shard_map/slice | solution.py:42
  314.0 5.0 %bitcast_reduce_fusion = (f32[16,4,4,8]{3,1,2,0:T(4,128)S(1)}, f32[16,4,512,4,8]{2,4,3,1,0:T(8,128)S(1)}) fusion(pred[16,512]{1,0:T(8,128)(4,1)S(1)} %iota_compare_fusion, bf16[16,512,4,128,1]{1,3,4,2,0:T(8,128)(2,1)} %bitcast.137, bf16[4,16,4,8,64]{4,3,2,1,0:T(8,128)(2,1)S(1)} %get-tuple-element.13, bf16[4,16,4,8,64]{4,3,2,1,0:T(8,128)(2,1)S(1)} %get-tuple-element.12), kind=kOutput, calls=%fused_computation.6 | convolution fusion | flops 272627712 | bytes 13123584 | tf_op jit(solution)/shard_map/nrkgd,nlkd->nrkgl/dot_general | solution.py:44
  319.0 2.0 fusion.1
  321.2 7.6 %fusion.30 = f32[4,16,4,8,128]{4,3,0,2,1:T(8,128)} fusion(bf16[16,512,4,128,1]{1,3,4,2,0:T(8,128)(2,1)} %bitcast.136, f32[16,4,512,4,8]{2,4,3,1,0:T(8,128)S(1)} %get-tuple-element.21, f32[16,4,4,8]{3,1,2,0:T(4,128)S(1)} %get-tuple-element.20, pred[16,512]{1,0:T(8,128)(4,1)S(1)} %iota_compare_fusion, f32[4,16,4,8]{3,0,2,1:T(4,128)S(1)} %get-tuple-element.7), kind=kOutput, calls=%fused_computation.31 | convolution fusion | flops 272891904 | bytes 13656064 | tf_op jit(solution)/shard_map/nrkgl,nlkd->nrkgd/dot_general | solution.py:51
  328.8 3.0 fusion.38
  331.8 0.9 copy.70
  332.7 2.1 reshape.355
  (59 shorter events, 4.3 us)
Async XLA Ops:
  6.5 129.8 %copy-start = (bf16[5120,320]{0,1:T(8,128)(2,1)S(1)}, bf16[5120,320]{0,1:T(8,128)(2,1)}, u32[]{:S(2)}) copy-start(bf16[5120,320]{0,1:T(8,128)(2,1)} %param.13) | copy-start | bytes 9830404
  6.5 129.8 %all-gather.5.cloned.1.call-start = ((), (), s32[]{:S(2)}) async-start(), calls=%async_computation.1 | async-start | bytes 11141120 | tf_op jit(solution)/shard_map/all_gather | solution.py:89
  10.3 250.1 %all-gather.7.cloned.1.call-start = ((), (), s32[]{:S(2)}) async-start(), calls=%async_computation.2 | async-start | bytes 17825792 | tf_op jit(solution)/shard_map/all_gather | solution.py:129
  40.5 109.5 %copy-start.7 = (s32[16,1]{0,1:T(1,128)S(1)}, s32[16,1]{0,1:T(1,128)}, u32[]{:S(2)}) copy-start(s32[16,1]{0,1:T(1,128)} %param.21) | copy-start | bytes 196
  40.5 109.6 %copy-start.8 = (s32[1,16]{1,0:T(1,128)S(1)}, s32[1,16]{1,0:T(1,128)}, u32[]{:S(2)}) copy-start(s32[1,16]{1,0:T(1,128)} %param.19) | copy-start | bytes 196
  145.8 23.9 %all-to-all-start = ((bf16[16,64,320]{2,1,0:T(8,128)(2,1)}), bf16[16,64,320]{2,1,0:T(8,128)(2,1)S(1)}, u32[]{:S(2)}, u32[]{:S(2)}) async-start(bf16[16,64,320]{2,1,0:T(8,128)(2,1)} %bitcast.14), calls=%async_computation | async-start | bytes 1572864 | tf_op jit(solution)/shard_map/all_to_all | solution.py:93
  150.0 21.4 %copy-start.5 = (f32[128]{0:T(128)S(1)}, f32[128]{0:T(128)}, u32[]{:S(2)}) copy-start(f32[128]{0:T(128)} %param.15) | copy-start | bytes 1540
  175.5 6.7 %copy-start.6 = (f32[128]{0:T(128)S(1)}, f32[128]{0:T(128)}, u32[]{:S(2)}) copy-start(f32[128]{0:T(128)} %param.14) | copy-start | bytes 1540
  181.8 1.6 copy-start.3
  185.1 89.4 %copy-start.4 = (f32[16,4,4,8,132]{4,3,1,2,0:T(8,128)}, f32[16,4,4,8,132]{4,3,1,2,0:T(8,128)S(1)}, u32[]{:S(2)}) copy-start(f32[16,4,4,8,132]{4,3,1,2,0:T(8,128)S(1)} %get-tuple-element.23) | copy-start | bytes 3244036
  321.2 7.6 %copy-start.2 = (bf16[16,132,4,128]{3,2,1,0:T(4,128)(2,1)S(1)}, bf16[16,132,4,128]{3,2,1,0:T(4,128)(2,1)}, u32[]{:S(2)}) copy-start(bf16[16,132,4,128]{3,2,1,0:T(4,128)(2,1)} %reshape.386) | copy-start | bytes 6488068
  328.8 6.0 %copy-start.1 = (bf16[5120,320]{0,1:T(8,128)(2,1)S(1)}, bf16[5120,320]{0,1:T(8,128)(2,1)}, u32[]{:S(2)}) copy-start(bf16[5120,320]{0,1:T(8,128)(2,1)} %param.13) | copy-start | bytes 9830404
Sparse Core Ops, SparseCore 0:
  10.4 125.8 all-gather.4
  139.1 121.3 all-gather.6
where the time goes:
time: 343 us; the launch traced here: 342 us
  waiting for transfers between devices  190 us (55%)
  local copies, waits for them, and re-layouts  59.4 us (17%)
  blocking collectives  25.7 us (7%)
  matrix products  24.6 us (7%)
  other arithmetic  23.6 us (7%)
  between operations  13.7 us (4%)
  starting transfers between devices  4.18 us (1%)
    all_gather x1, waiting for transfers between devices, per_device(): lax.all_gather(normed, 'fsdp', axis=0, tiled=True)  95.8 us
    all_gather x1, waiting for transfers between devices, per_device(): lax.all_gather(prompt_kv[0], 'sample', axis=0, tiled=True)  74.5 us
    all_gather x1, blocking collectives, per_device(): lax.all_gather(block_table[0], 'sample', axis=0, tiled=True)  25.7 us
    all_to_all x1, waiting for transfers between devices, per_device(): lax.all_to_all(own_columns, 'fsdp', split_axis=0, concat_axis=1, tiled=True)  19.3 us
    slice x2, local copies, waits for them, and re-layouts, attend(): key_vals[..., :feature].reshape(count, length, KV_HEADS, head_dim)  18.6 us
    gather x1, local copies, waits for them, and re-layouts, per_device(): jnp.take(pool, page_rows, axis=0)  14.1 us
    slice x1, local copies, waits for them, and re-layouts, attend(): key_vals[..., feature:].reshape(count, length, KV_HEADS, head_dim)  12.3 us
    dot_general x2, matrix products, attend(): jnp.einsum('nrkgl,nlkd->nrkgd', weights.astype(jnp.bfloat16), value_part,...  10.6 us
  transfers between devices with their start and end apart: 3, of which 3 were waited for; matrix products, arithmetic and copies ran while one was open for 9% of the time, Pallas kernels for 0%

commit v1 on v0

v1 whole, which is shorter than its diff:
```python
import functools

import jax
import jax.numpy as jnp
import numpy as np
from jax import lax
from jax.experimental import pallas as pl
from jax.experimental.pallas import tpu as pltpu
from jax.sharding import Mesh, PartitionSpec as P

D = 5120
HD = 128
HEADS = 32
KV_HEADS = 4
GROUP = HEADS // KV_HEADS
QD = 4096
KVD = 512
STEPS = 4
SLOTS = 16
ROWS = STEPS * SLOTS
PLEN = 512
RL = 128
NEW = 16
RK = RL + NEW
SCALE = HD**-0.5
FSDP = ("yl", "z")
SAMPLE = ("yh", "x", "c")


def slot_of(j, yh, x, c):
    return ((j // 8) ^ yh) * 8 + ((x + (j // 2) % 4) % 4) * 2 + ((j % 2) ^ c)


def norm_kernel(place_ref, slots_ref, gain_ref, hidden_ref, normed_ref, perm_ref):
    row = lax.broadcasted_iota(jnp.int32, (ROWS, ROWS), 0)
    col = lax.broadcasted_iota(jnp.int32, (ROWS, ROWS), 1)
    want = slot_of(row // STEPS, place_ref[0], place_ref[1], place_ref[2])
    have = jnp.concatenate([slots_ref[...]] * STEPS, axis=1)
    hit = (want == have) & (row % STEPS == col // SLOTS)
    perm = jnp.where(hit, 1.0, 0.0).astype(jnp.bfloat16)
    perm_ref[...] = perm
    wide = hidden_ref[...].astype(jnp.float32)
    mean = jnp.mean(wide * wide, axis=-1, keepdims=True)
    normed = (wide * lax.rsqrt(mean + 1e-6) * gain_ref[...]).astype(jnp.bfloat16)
    normed_ref[...] = jnp.dot(perm, normed, preferred_element_type=jnp.float32).astype(jnp.bfloat16)


def norm_rows(place, slots, gain, hidden):
    vmem = pl.BlockSpec(memory_space=pltpu.VMEM)
    return pl.pallas_call(
        norm_kernel,
        out_shape=(
            jax.ShapeDtypeStruct((ROWS, D), jnp.bfloat16),
            jax.ShapeDtypeStruct((ROWS, ROWS), jnp.bfloat16),
        ),
        in_specs=[pl.BlockSpec(memory_space=pltpu.SMEM), vmem, vmem, vmem],
        out_specs=(vmem, vmem),
        compiler_params=pltpu.CompilerParams(vmem_limit_bytes=16 * 2**20),
        cost_estimate=pl.CostEstimate(flops=2 * ROWS * ROWS * D, bytes_accessed=4 * ROWS * D, transcendentals=0),
    )(place, slots, gain, hidden)


KSTEP = 640


def project_kernel(place_ref, rows_ref, own_ref, near_ref, far_ref, out_ref, weights, acc):
    step = pl.program_id(0)
    yl, odd = place_ref[0], place_ref[1]
    side = pl.multiple_of(odd * 64, 64)
    tail = pl.multiple_of((1 - odd) * 256, 64)

    def put(which, block):
        weights[pl.ds(pl.multiple_of(which * 256, 256), 256), :] = block[pl.ds(side, 256), :]
        weights[pl.ds(pl.multiple_of(512 + which * 64, 64), 64), :] = block[pl.ds(tail, 64), :]

    put(yl, own_ref)

    @pl.when(step < 4)
    def _():
        put(1 - yl, near_ref)

    @pl.when(step >= 4)
    def _():
        put(1 - yl, far_ref)

    @pl.when(step == 0)
    def _():
        acc[...] = jnp.zeros_like(acc)

    acc[...] += lax.dot_general(
        rows_ref[...], weights[...], (((1,), (1,)), ((), ())), preferred_element_type=jnp.float32
    )

    @pl.when(step == 7)
    def _():
        out_ref[...] = acc[...].astype(jnp.bfloat16)


def project(place, rows, own_w, near, far):
    count, width = rows.shape[0], own_w.shape[0]

    def slab(step, place_ref):
        return (0, ((step // 4) ^ place_ref[2]) * 4 + step % 4)

    return pl.pallas_call(
        project_kernel,
        out_shape=jax.ShapeDtypeStruct((count, 2 * width), jnp.bfloat16),
        grid_spec=pltpu.PrefetchScalarGridSpec(
            num_scalar_prefetch=1,
            grid=(8,),
            in_specs=[
                pl.BlockSpec((count, KSTEP), slab),
                pl.BlockSpec((width, KSTEP), slab),
                pl.BlockSpec((width, KSTEP), lambda step, place_ref: (0, jnp.minimum(step, 3))),
                pl.BlockSpec((width, KSTEP), lambda step, place_ref: (0, jnp.maximum(step - 4, 0))),
            ],
            out_specs=pl.BlockSpec((count, 2 * width), lambda step, place_ref: (0, 0)),
            scratch_shapes=[
                pltpu.VMEM((2 * width, KSTEP), jnp.bfloat16),
                pltpu.VMEM((count, 2 * width), jnp.float32),
            ],
        ),
        compiler_params=pltpu.CompilerParams(vmem_limit_bytes=24 * 2**20),
        cost_estimate=pl.CostEstimate(
            flops=4 * count * width * D, bytes_accessed=2 * D * (count + 2 * width), transcendentals=0
        ),
    )(place, rows, own_w, near, far)


PIECES = ((0, 0, 512), (1, 0, 512), (2, 0, 256), (2, 256, 256), (3, 0, 512))


def attend_kernel(*refs):
    (order, plen, rlen, cols, cosf, sinf, qgain, kgain, perm) = refs[:9]
    pages = refs[9:29]
    resp = refs[29]
    out = refs[30]
    kv, rkv, queries, mixed, sem_kv, sem_r = refs[31:]
    n = 0
    for dy in range(2):
        for dc in range(2):
            for dx, start, size in PIECES:
                j = dy * 8 + dx * 2 + dc
                pltpu.make_async_copy(pages[n], kv.at[j, pl.ds(start, size)], sem_kv.at[j]).start()
                n += 1
    for j in range(SLOTS):
        pltpu.make_async_copy(resp.at[order[j]], rkv.at[j, pl.ds(0, RL)], sem_r.at[j]).start()

    low = lax.broadcasted_iota(jnp.int32, (ROWS, HD), 1) < 64

    def head_of(hh):
        half, even, n = hh // 20, hh % 20 // 5 * 2, hh % 5
        if n < 2:
            return cols[even, :, half * 256 + n * HD : half * 256 + (n + 1) * HD].astype(jnp.float32)
        if n > 2:
            return cols[even + 1, :, half * 256 + (n - 3) * HD : half * 256 + (n - 2) * HD].astype(jnp.float32)
        left = cols[even, :, 512:640].astype(jnp.float32)
        right = cols[even + 1, :, 512:640].astype(jnp.float32)
        if half == 0:
            return jnp.where(low, left, pltpu.roll(right, 64, 1))
        return jnp.where(low, pltpu.roll(left, 64, 1), right)

    cosine, sine = cosf[...], sinf[...]

    def turned(hh, gain):
        head = head_of(hh)
        mean = jnp.mean(head * head, axis=-1, keepdims=True)
        head = head * lax.rsqrt(mean + 1e-6) * gain
        return (head * cosine + pltpu.roll(head, 64, 1) * sine).astype(jnp.bfloat16)

    fresh = [turned(HEADS + k, kgain[...]) for k in range(KV_HEADS)]
    fresh += [head_of(HEADS + KV_HEADS + k).astype(jnp.bfloat16) for k in range(KV_HEADS)]
    for k in range(2 * KV_HEADS):
        for j in range(SLOTS):
            rkv[j, RL:RK, k * HD : (k + 1) * HD] = fresh[k][j // 4 * NEW : (j // 4 + 1) * NEW]
    for h in range(HEADS):
        queries[:, h, :] = turned(h, qgain[...]).astype(jnp.float32)

    key_p = lax.broadcasted_iota(jnp.int32, (PLEN, HD), 0)
    key_r = lax.broadcasted_iota(jnp.int32, (RK, HD), 0)
    spot = key_r - RL
    step = lax.broadcasted_iota(jnp.int32, (RK, HD), 1) % 32 // GROUP
    seen = (spot >= 0) & (spot % STEPS <= step)
    turn = spot // STEPS
    across = (((1,), (1,)), ((), ()))
    down = (((0,), (0,)), ((), ()))
    factor = SCALE * 1.4426950408889634

    def one_slot(j, carry):
        pltpu.make_async_copy(kv.at[j], kv.at[j], sem_kv.at[j]).wait()
        pltpu.make_async_copy(rkv.at[j, pl.ds(0, RL)], rkv.at[j, pl.ds(0, RL)], sem_r.at[j]).wait()
        mine = queries[pl.ds(j * STEPS, STEPS)]
        zero = jnp.zeros((32, HD), jnp.float32)
        spread = []
        for k in range(KV_HEADS):
            q = mine[:, k * GROUP : (k + 1) * GROUP, :].reshape(32, HD)
            spread.append(jnp.concatenate([q if n == k else zero for n in range(KV_HEADS)], axis=1))
        q = jnp.concatenate(spread, axis=0).astype(jnp.bfloat16)
        s_p = lax.dot_general(kv[j, :, :KVD], q, across, preferred_element_type=jnp.float32)
        s_r = lax.dot_general(rkv[j, :, :KVD], q, across, preferred_element_type=jnp.float32)
        s_p = jnp.where(key_p < plen[j], s_p, -1e30)
        s_r = jnp.where((key_r < rlen[j]) | (seen & (turn == j % 4)), s_r, -1e30)
        peak = jnp.maximum(jnp.max(s_p, axis=0, keepdims=True), jnp.max(s_r, axis=0, keepdims=True))
        w_p = jnp.exp2((s_p - peak) * factor)
        w_r = jnp.exp2((s_r - peak) * factor)
        share = 1.0 / (jnp.sum(w_p, axis=0, keepdims=True) + jnp.sum(w_r, axis=0, keepdims=True))
        mix = lax.dot_general(
            (w_p * share).astype(jnp.bfloat16), kv[j, :, KVD:], down, preferred_element_type=jnp.float32
        )
        mix += lax.dot_general(
            (w_r * share).astype(jnp.bfloat16), rkv[j, :, KVD:], down, preferred_element_type=jnp.float32
        )
        for k in range(KV_HEADS):
            block = mix[k * 32 : (k + 1) * 32, k * HD : (k + 1) * HD]
            mixed[pl.ds(j * STEPS, STEPS), k * GROUP : (k + 1) * GROUP, :] = block.reshape(STEPS, GROUP, HD)
        return carry

    lax.fori_loop(0, SLOTS, one_slot, 0)
    back = perm[...]
    for h in range(HEADS):
        head = mixed[:, h, :].astype(jnp.bfloat16)
        out[:, h * HD : (h + 1) * HD] = lax.dot_general(
            back, head, (((0,), (0,)), ((), ())), preferred_element_type=jnp.float32
        ).astype(jnp.bfloat16)


def attend_all(order, plen, rlen, cols, cosf, sinf, qgain, kgain, perm, pages, resp):
    vmem = pl.BlockSpec(memory_space=pltpu.VMEM)
    smem = pl.BlockSpec(memory_space=pltpu.SMEM)
    hbm = pl.BlockSpec(memory_space=pl.ANY)
    return pl.pallas_call(
        attend_kernel,
        out_shape=jax.ShapeDtypeStruct((ROWS, QD), jnp.bfloat16),
        in_specs=[smem] * 3 + [vmem] * 6 + [hbm] * 21,
        out_specs=vmem,
        scratch_shapes=[
            pltpu.VMEM((SLOTS, PLEN, 2 * KVD), jnp.bfloat16),
            pltpu.VMEM((SLOTS, RK, 2 * KVD), jnp.bfloat16),
            pltpu.VMEM((ROWS, HEADS, HD), jnp.float32),
            pltpu.VMEM((ROWS, HEADS, HD), jnp.float32),
            pltpu.SemaphoreType.DMA((SLOTS,)),
            pltpu.SemaphoreType.DMA((SLOTS,)),
        ],
        compiler_params=pltpu.CompilerParams(vmem_limit_bytes=44 * 2**20),
        cost_estimate=pl.CostEstimate(
            flops=4 * ROWS * QD * (PLEN + RK), bytes_accessed=21 * 2**20, transcendentals=ROWS * HEADS * (PLEN + RK)
        ),
    )(order, plen, rlen, cols, cosf, sinf, qgain, kgain, perm, *pages, resp)


def shift(array, axis, size, by):
    return lax.ppermute(array, axis, [(i, (i + by) % size) for i in range(size)])


def ring(base):
    return shift(base, "x", 4, 1), shift(base, "x", 4, -1)


def far_side(up, down):
    return shift(up[:256], "x", 4, 1), shift(down[256:], "x", 4, -1)


def with_core(pieces):
    return pieces + [shift(piece, "c", 2, 1) for piece in pieces]


def swap_block(part):
    pairs = []
    for yl in range(2):
        for yh in range(2):
            for c in range(2):
                pairs.append((yl * 4 + yh * 2 + c, (1 - yl) * 4 + (yh ^ c) * 2 + c))
    return lax.ppermute(part, ("yl", "yh", "c"), pairs)


def per_device(
    hidden,
    norm_gain,
    w_qkv,
    query_gain,
    key_gain,
    prompt_kv,
    block_table,
    prompt_slot,
    prompt_len,
    resp_kv,
    resp_len,
):
    yl, z, yh, x, c = (lax.axis_index(name) for name in FSDP + SAMPLE)
    place = jnp.stack([yh, x, c]).astype(jnp.int32)
    normed, perm = norm_rows(place, prompt_slot, norm_gain.reshape(1, D), hidden.reshape(ROWS, D))
    rows = lax.all_gather(normed, "z", axis=0, tiled=True)

    own = jnp.take(prompt_kv[0], block_table[0, 0], axis=0).reshape(PLEN, 2 * KVD)
    other = shift(own, "yh", 2, 1)

    own_w = w_qkv.T
    half = D // 2
    part = lax.dynamic_slice_in_dim(own_w, c * half, half, 1)
    near = swap_block(part)
    far = shift(near, "c", 2, 1)
    up, down = ring(own)
    far_a, far_b = far_side(up, down)
    pages = with_core([own, down, far_a, far_b, up])
    up, down = ring(other)

    where = jnp.stack([yl, z % 2, c]).astype(jnp.int32)
    projected = project(where, rows, own_w, near, far)
    up, down, projected = lax.optimization_barrier((up, down, projected))
    far_a, far_b = far_side(up, down)
    pages += with_core([other, down, far_a, far_b, up])
    projected = projected.reshape(8, ROWS, 2 * own_w.shape[0])
    cols = lax.all_to_all(projected, "z", split_axis=0, concat_axis=0, tiled=True)

    want = slot_of(jnp.arange(SLOTS, dtype=jnp.int32), yh, x, c)
    hit = (prompt_slot == want[:, None]).astype(jnp.int32)
    order = jnp.sum(hit * jnp.arange(SLOTS, dtype=jnp.int32)[None, :], axis=1)
    plen = jnp.sum(hit * prompt_len, axis=1)
    rlen = jnp.sum(hit * resp_len.reshape(1, SLOTS), axis=1)
    positions = (plen + rlen)[:, None] + jnp.arange(STEPS, dtype=jnp.int32)[None, :]
    inv_freq = jnp.exp(-jnp.log(1000000.0) * jnp.arange(HD // 2, dtype=jnp.float32) * 2.0 / HD)
    angles = positions.reshape(ROWS, 1).astype(jnp.float32) * inv_freq[None, :]
    cosine, sine = jnp.cos(angles), jnp.sin(angles)
    cosf = jnp.concatenate([cosine, cosine], axis=1)
    sinf = jnp.concatenate([-sine, sine], axis=1)

    mixed = attend_all(
        order,
        plen,
        rlen,
        cols,
        cosf,
        sinf,
        query_gain.reshape(1, HD),
        key_gain.reshape(1, HD),
        perm,
        pages,
        resp_kv.reshape(SLOTS, RL, 2 * KVD),
    )
    return mixed.reshape(STEPS, SLOTS, 1, QD)


def solution(mesh):
    fine = Mesh(np.asarray(mesh.devices).reshape(2, 8, 2, 4, 2), FSDP + SAMPLE)
    placed = (
        P(None, FSDP, SAMPLE, None),
        P(),
        P(None, FSDP),
        P(),
        P(),
        P(FSDP, SAMPLE, None, None),
        P(FSDP, SAMPLE, None),
        P(FSDP, None),
        P(FSDP, None),
        P(FSDP, SAMPLE, None, None),
        P(FSDP, SAMPLE),
    )
    return jax.shard_map(
        per_device,
        mesh=fine,
        in_specs=placed,
        out_specs=P(None, FSDP, SAMPLE, None),
        check_vma=False,
    )
```

time: 343 us -> 183 us (0.53)
  waiting for transfers between devices: 190 us -> 71.5 us
  local copies, waits for them, and re-layouts: 59.4 us -> 19 us
  starting transfers between devices: 4.18 us -> 42 us
  Pallas kernels: 0 us -> 35 us
  blocking collectives: 25.7 us -> 0 us
  matrix products: 24.6 us -> 0 us
  other arithmetic: 23.6 us -> 0.98 us
    all_gather x2 -> x1, waiting for transfers between devices: 170 us -> 0.01 us  [per_device(): rows = lax.all_gather(normed, 'z', axis=0, tiled=True)]
    ppermute x0 -> x21, waiting for transfers between devices: none -> 59.1 us  [the longest x20 32.9 us: shift(): lax.ppermute(array, axis, [(i, (i + by) % size) for i in range(size)])]
    pallas_call x0 -> x3, Pallas kernels: none -> 35 us  [the longest x1 22.1 us: attend_all(): pl.pallas_call(attend_kernel, out_shape=jax.ShapeDtypeStruct((ROWS, QD),...]
    ppermute x0 -> x21, starting transfers between devices: none -> 33.8 us  [the longest x20 30.3 us: shift(): lax.ppermute(array, axis, [(i, (i + by) % size) for i in range(size)])]
    slice x3 -> x4, local copies, waits for them, and re-layouts: 30.9 us -> 4.91 us  [far_side(): return (shift(up[:256], 'x', 4, 1), shift(down[256:], 'x', 4, -1))]
    all_gather x1 -> x0, blocking collectives: 25.7 us -> none  [per_device(): lax.all_gather(block_table[0], 'sample', axis=0, tiled=True)]
    dot_general x5 -> x0, matrix products: 24.6 us -> none  [the longest x2 10.6 us: attend(): jnp.einsum('nrkgl,nlkd->nrkgd', weights.astype(jnp.bfloat16), value_part,...]
    gather x3 -> x1, local copies, waits for them, and re-layouts: 14.7 us -> 0.61 us  [per_device(): jnp.take(prompt_kv[0], block_table[0, 0], axis=0).reshape(PLEN, 2 * KVD)]
  transfers between devices with their start and end apart: 3 -> 23, of which waited for: 3 -> 7; matrix products, arithmetic and copies ran while one was open for 9% -> 5% of each run, Pallas kernels for 0% -> 6%
where the time goes in v1:
time: 183 us; the launch traced here: 182 us
  waiting for transfers between devices  71.5 us (39%)
  starting transfers between devices  42 us (23%)
  Pallas kernels  35 us (19%)
  local copies, waits for them, and re-layouts  19 us (10%)
  between operations  13.6 us (7%)
    ppermute x20, waiting for transfers between devices, shift(): lax.ppermute(array, axis, [(i, (i + by) % size) for i in range(size)])  32.9 us
    ppermute x20, starting transfers between devices, shift(): lax.ppermute(array, axis, [(i, (i + by) % size) for i in range(size)])  30.3 us
    ppermute x1, waiting for transfers between devices, swap_block(): return lax.ppermute(part, ('yl', 'yh', 'c'), pairs)  26.2 us
    pallas_call x1, Pallas kernels, attend_all(): pl.pallas_call(attend_kernel, out_shape=jax.ShapeDtypeStruct((ROWS, QD),...  22.1 us
    all_to_all x1, waiting for transfers between devices, per_device(): lax.all_to_all(projected, 'z', split_axis=0, concat_axis=0, tiled=True)  12.3 us
    pallas_call x1, Pallas kernels, project(): pl.pallas_call(project_kernel, out_shape=jax.ShapeDtypeStruct((count, 2 *...  10.9 us
    unnamed x32, local copies, waits for them, and re-layouts  10.4 us
    all_to_all x1, starting transfers between devices, per_device(): lax.all_to_all(projected, 'z', split_axis=0, concat_axis=0, tiled=True)  8.17 us
  transfers between devices with their start and end apart: 23, of which 7 were waited for; matrix products, arithmetic and copies ran while one was open for 5% of the time, Pallas kernels for 6%

profile of v1, /device:TPU:1, one launch (start us, length us, event | category | flops | bytes accessed | tf_op | source)
XLA Modules:
  0.0 182.0 jit_solution(1512170368357787069)
XLA Ops:
  6.6 1.2 copy-done.7
  9.2 1.9 %shard_map.109 = (bf16[64,5120]{1,0:T(8,128)(2,1)}, bf16[64,64]{1,0:T(8,128)(2,1)S(1)}) custom-call(s32[3]{0:T(128)S(1)} %add_add_fusion.1.place_ref, s32[1,16]{1,0:T(1,128)S(1)} %copy-done.9, f32[1,5120]{1,0:T(1,128)S(1)} %bitcast.32, bf16[64,5120]{1,0:T(8,128)(2,1)S(1)} %bitcast.31), custom_call_target="tpu_custom_call" | custom-call | flops 41943040 | bytes 1310720 | tf_op jit(solution)/shard_map/pallas_call | solution.py:50
  11.1 2.8 %dynamic-slice_bitcast_fusion = bf16[320,2560]{1,0:T(8,128)(2,1)} fusion(bf16[5120,320]{0,1:T(8,128)(2,1)} %param.13, s32[]{:T(128)S(6)} %select_n.82), kind=kLoop, calls=%fused_computation.1 | loop fusion | bytes 3276804 | tf_op jit(solution)/shard_map/dynamic_slice | solution.py:299
  13.9 3.6 %collective-permute-start.3 = (bf16[320,2560]{1,0:T(8,128)(2,1)}, bf16[320,2560]{1,0:T(8,128)(2,1)}, u32[]{:S(2)}, u32[]{:S(2)}) collective-permute-start(bf16[320,2560]{1,0:T(8,128)(2,1)} %dynamic-slice_bitcast_fusion), channel_id=1, source_target_pairs={{0,128},{1,137},{8,136},{9,129},{128,0},{129,9},{136,8},{137,1},{2... | collective-permute-start | bytes 4915208 | tf_op jit(solution)/shard_map/ppermute | solution.py:273
  19.0 1.2 collective-permute-start.6
  20.2 1.5 collective-permute-start.5
  21.6 26.2 %collective-permute-done.3.near_ref = bf16[320,2560]{1,0:T(8,128)(2,1)} collective-permute-done((bf16[320,2560]{1,0:T(8,128)(2,1)}, bf16[320,2560]{1,0:T(8,128)(2,1)}, u32[]{:S(2)}, u32[]{:S(2)}) %collective-permute-start.3) | collective-permute-done | bytes 1638432 | tf_op jit(solution)/shard_map/ppermute | solution.py:273
  47.8 1.9 %collective-permute-start.4 = (bf16[320,2560]{1,0:T(8,128)(2,1)}, bf16[320,2560]{1,0:T(8,128)(2,1)}, u32[]{:S(2)}, u32[]{:S(2)}) collective-permute-start(bf16[320,2560]{1,0:T(8,128)(2,1)} %collective-permute-done.3.near_ref), channel_id=1, source_target_pairs={{0,1},{1,0},{2,3},{3,2},{4,5},{5,4},{6,7},{7,6},{8,9},{9,8},{10,11... | collective-permute-start | bytes 4915208 | tf_op jit(solution)/shard_map/ppermute | solution.py:252
  49.7 9.9 %collective-permute-start.1 = (bf16[512,1024]{1,0:T(8,128)(2,1)}, bf16[512,1024]{1,0:T(8,128)(2,1)}, u32[]{:S(2)}, u32[]{:S(2)}) collective-permute-start(bf16[512,1024]{1,0:T(8,128)(2,1)} %collective-permute-done.refs_19_), channel_id=1, source_target_pairs={{0,2},{2,4},{4,6},{6,0},{1,3},{3,5},{5,7},{7,1},{8,10},{10,12},{12... | collective-permute-start | bytes 3145736 | tf_op jit(solution)/shard_map/ppermute | solution.py:252
  59.6 1.3 collective-permute-start.7
  60.9 1.4 collective-permute-start.2
  62.4 1.1 slice.19
  63.7 28.3 %collective-permute-done.7.refs_11_ = bf16[256,1024]{1,0:T(8,128)(2,1)} collective-permute-done((bf16[256,1024]{1,0:T(8,128)(2,1)S(1)}, bf16[256,1024]{1,0:T(8,128)(2,1)}, u32[]{:S(2)}, u32[]{:S(2)}) %collective-permute-start.7) | collective-permute-done | bytes 524320 | tf_op jit(solution)/shard_map/ppermute | solution.py:252
  92.0 4.5 %collective-permute-start.9 = (bf16[512,1024]{1,0:T(8,128)(2,1)S(1)}, bf16[512,1024]{1,0:T(8,128)(2,1)S(1)}, u32[]{:S(2)}, u32[]{:S(2)}) collective-permute-start(bf16[512,1024]{1,0:T(8,128)(2,1)S(1)} %bitcast_select_fusion.refs_9_), channel_id=1, source_target_pairs={{0,1},{1,0},{2,3},{3,2},{4,5},{5,4},{6,7},{7,6},{8,9},{9,8},{10,11... | collective-permute-start | bytes 3145736 | tf_op jit(solution)/shard_map/ppermute | solution.py:252
  96.5 1.5 collective-permute-start.16
  98.8 1.9 %copy-done.1 = bf16[5120,320]{0,1:T(8,128)(2,1)S(1)} copy-done((bf16[5120,320]{0,1:T(8,128)(2,1)S(1)}, bf16[5120,320]{0,1:T(8,128)(2,1)}, u32[]{:S(2)}) %copy-start.1) | copy-done | bytes 3276824
  100.7 2.5 %copy-done.2 = bf16[512,5120]{1,0:T(8,128)(2,1)S(1)} copy-done((bf16[512,5120]{1,0:T(8,128)(2,1)S(1)}, bf16[512,5120]{1,0:T(8,128)(2,1)}, u32[]{:S(2)}) %copy-start.2) | copy-done | bytes 5242904
  103.2 10.9 %shard_map.110 = bf16[512,640]{1,0:T(8,128)(2,1)} custom-call(s32[3]{0:T(128)S(1)} %add_add_fusion.place_ref, bf16[512,5120]{1,0:T(8,128)(2,1)S(1)} %copy-done.2, bf16[320,5120]{1,0:T(8,128)(2,1)S(1)} %bitcast.30, bf16[320,2560]{1,0:T(8,128)(2,1)} %collective-permute-done.3.near_ref, bf16[320,2560]{1,0:T(8,128)(2,1)} %collective-permute-done.4.far_ref), custom_call_target="tpu_custom_call" | custom-call | flops 3355443200 | bytes 11796480 | tf_op jit(solution)/shard_map/pallas_call | solution.py:105
  114.1 1.9 %slice.14 = bf16[256,1024]{1,0:T(8,128)(2,1)} slice(bf16[512,1024]{1,0:T(8,128)(2,1)} %collective-permute-done.1.refs_23_), slice={[0:256], [0:1024]} | slice | bytes 1048576 | tf_op jit(solution)/shard_map/slice | solution.py:260
  116.1 1.9 %slice.15 = bf16[256,1024]{1,0:T(8,128)(2,1)} slice(bf16[512,1024]{1,0:T(8,128)(2,1)} %collective-permute-done.2.refs_20_), slice={[256:512], [0:1024]} | slice | bytes 1048576 | tf_op jit(solution)/shard_map/slice | solution.py:260
  117.9 1.0 copy-done.5
  119.8 1.8 collective-permute-start.15
  121.6 8.2 %all-to-all-start = ((bf16[8,64,640]{2,1,0:T(8,128)(2,1)}), bf16[8,64,640]{2,1,0:T(8,128)(2,1)S(1)}, u32[]{:S(2)}, u32[]{:S(2)}) async-start(bf16[8,64,640]{2,1,0:T(8,128)(2,1)} %bitcast.17), calls=%async_computation | async-start | bytes 1310720 | tf_op jit(solution)/shard_map/all_to_all | solution.py:313
  129.8 1.3 collective-permute-start.13
  131.9 1.6 collective-permute-done.14.refs_21_
  133.4 1.2 collective-permute-start.18
  135.2 1.5 collective-permute-done.20.refs_28_
  136.7 1.3 collective-permute-done.18.refs_26_
  138.2 12.3 %all-to-all-done.refs_3_ = bf16[8,64,640]{2,1,0:T(8,128)(2,1)S(1)} async-done(((bf16[8,64,640]{2,1,0:T(8,128)(2,1)}), bf16[8,64,640]{2,1,0:T(8,128)(2,1)S(1)}, u32[]{:S(2)}, u32[]{:S(2)}) %all-to-all-start) | async-done | bytes 655392 | tf_op jit(solution)/shard_map/all_to_all | solution.py:313
  150.5 1.2 copy-done.4
  151.8 1.2 copy-done.6
  153.0 22.1 %shard_map.111 = bf16[64,4096]{1,0:T(8,128)(2,1)} custom-call(s32[16]{0:T(128)S(1)} %get-tuple-element.17.refs_0_, s32[16]{0:T(128)S(1)} %get-tuple-element.16.refs_1_, s32[16]{0:T(128)S(1)} %get-tuple-element.15.refs_2_, bf16[8,64,640]{2,1,0:T(8,128)(2,1)S(1)} %all-to-all-done.refs_3_, f32[64,128]{1,0:T(8,128)S(1)} %get-tuple-element.21.refs_4_, ...), custom_call_target="tpu_custom_call" | custom-call | flops 687865856 | bytes 22020096 | tf_op jit(solution)/shard_map/pallas_call | solution.py:231
  (72 shorter events, 6.3 us)
Async XLA Ops:
  6.5 11.1 %copy-start = (bf16[1,8,64,1024]{3,2,1,0:T(8,128)(2,1)S(1)}, bf16[1,8,64,1024]{3,2,1,0:T(8,128)(2,1)}, u32[]{:S(2)}) copy-start(bf16[1,8,64,1024]{3,2,1,0:T(8,128)(2,1)} %param.16) | copy-start | bytes 3145732
  6.5 10.9 %copy-start.15 = (s32[1,1,8]{2,1,0:T(1,128)S(1)}, s32[1,1,8]{2,1,0:T(1,128)}, u32[]{:S(2)}) copy-start(s32[1,1,8]{2,1,0:T(1,128)} %param.17) | copy-start | bytes 100
  6.5 92.2 %all-gather.2.cloned.1.call-start = ((), (), s32[]{:S(2)}) async-start(), calls=%async_computation.1 | async-start | bytes 5898240 | tf_op jit(solution)/shard_map/all_gather | solution.py:292
  13.9 33.9 %collective-permute-start.3 = (bf16[320,2560]{1,0:T(8,128)(2,1)}, bf16[320,2560]{1,0:T(8,128)(2,1)}, u32[]{:S(2)}, u32[]{:S(2)}) collective-permute-start(bf16[320,2560]{1,0:T(8,128)(2,1)} %dynamic-slice_bitcast_fusion), channel_id=1, source_target_pairs={{0,128},{1,137},{8,136},{9,129},{128,0},{129,9},{136,8},{137,1},{2... | collective-permute-start | bytes 4915208 | tf_op jit(solution)/shard_map/ppermute | solution.py:273
  18.5 31.2 %collective-permute-start = (bf16[512,1024]{1,0:T(8,128)(2,1)S(1)}, bf16[512,1024]{1,0:T(8,128)(2,1)}, u32[]{:S(2)}, u32[]{:S(2)}) collective-permute-start(bf16[512,1024]{1,0:T(8,128)(2,1)S(1)} %bitcast_select_fusion.refs_9_), channel_id=1, source_target_pairs={{0,8},{8,0},{1,9},{9,1},{2,10},{10,2},{3,11},{11,3},{4,12},{12,4},... | collective-permute-start | bytes 3145736 | tf_op jit(solution)/shard_map/ppermute | solution.py:252
  19.0 40.6 %collective-permute-start.6 = (bf16[512,1024]{1,0:T(8,128)(2,1)S(1)}, bf16[512,1024]{1,0:T(8,128)(2,1)S(1)}, u32[]{:S(2)}, u32[]{:S(2)}) collective-permute-start(bf16[512,1024]{1,0:T(8,128)(2,1)S(1)} %bitcast_select_fusion.refs_9_), channel_id=1, source_target_pairs={{0,2},{2,4},{4,6},{6,0},{1,3},{3,5},{5,7},{7,1},{8,10},{10,12},{12... | collective-permute-start | bytes 3145736 | tf_op jit(solution)/shard_map/ppermute | solution.py:252
  20.2 42.2 %collective-permute-start.5 = (bf16[512,1024]{1,0:T(8,128)(2,1)S(1)}, bf16[512,1024]{1,0:T(8,128)(2,1)}, u32[]{:S(2)}, u32[]{:S(2)}) collective-permute-start(bf16[512,1024]{1,0:T(8,128)(2,1)S(1)} %bitcast_select_fusion.refs_9_), channel_id=1, source_target_pairs={{0,6},{2,0},{4,2},{6,4},{1,7},{3,1},{5,3},{7,5},{8,14},{10,8},{12,... | collective-permute-start | bytes 3145736 | tf_op jit(solution)/shard_map/ppermute | solution.py:252
  47.8 50.8 %collective-permute-start.4 = (bf16[320,2560]{1,0:T(8,128)(2,1)}, bf16[320,2560]{1,0:T(8,128)(2,1)}, u32[]{:S(2)}, u32[]{:S(2)}) collective-permute-start(bf16[320,2560]{1,0:T(8,128)(2,1)} %collective-permute-done.3.near_ref), channel_id=1, source_target_pairs={{0,1},{1,0},{2,3},{3,2},{4,5},{5,4},{6,7},{7,6},{8,9},{9,8},{10,11... | collective-permute-start | bytes 4915208 | tf_op jit(solution)/shard_map/ppermute | solution.py:252
  49.7 48.3 %collective-permute-start.1 = (bf16[512,1024]{1,0:T(8,128)(2,1)}, bf16[512,1024]{1,0:T(8,128)(2,1)}, u32[]{:S(2)}, u32[]{:S(2)}) collective-permute-start(bf16[512,1024]{1,0:T(8,128)(2,1)} %collective-permute-done.refs_19_), channel_id=1, source_target_pairs={{0,2},{2,4},{4,6},{6,0},{1,3},{3,5},{5,7},{7,1},{8,10},{10,12},{12... | collective-permute-start | bytes 3145736 | tf_op jit(solution)/shard_map/ppermute | solution.py:252
  59.6 4.1 %copy-start.3 = (bf16[512,1024]{1,0:T(8,128)(2,1)}, bf16[512,1024]{1,0:T(8,128)(2,1)S(1)}, u32[]{:S(2)}) copy-start(bf16[512,1024]{1,0:T(8,128)(2,1)S(1)} %collective-permute-done.6.refs_13_) | copy-start | bytes 3145732
  59.6 32.4 %collective-permute-start.7 = (bf16[256,1024]{1,0:T(8,128)(2,1)S(1)}, bf16[256,1024]{1,0:T(8,128)(2,1)}, u32[]{:S(2)}, u32[]{:S(2)}) collective-permute-start(bf16[256,1024]{1,0:T(8,128)(2,1)S(1)} %slice.18), channel_id=1, source_target_pairs={{0,2},{2,4},{4,6},{6,0},{1,3},{3,5},{5,7},{7,1},{8,10},{10,12},{12... | collective-permute-start | bytes 1572872 | tf_op jit(solution)/shard_map/ppermute | solution.py:252
  60.9 37.1 %collective-permute-start.2 = (bf16[512,1024]{1,0:T(8,128)(2,1)}, bf16[512,1024]{1,0:T(8,128)(2,1)}, u32[]{:S(2)}, u32[]{:S(2)}) collective-permute-start(bf16[512,1024]{1,0:T(8,128)(2,1)} %collective-permute-done.refs_19_), channel_id=1, source_target_pairs={{0,6},{2,0},{4,2},{6,4},{1,7},{3,1},{5,3},{7,5},{8,14},{10,8},{12,... | collective-permute-start | bytes 3145736 | tf_op jit(solution)/shard_map/ppermute | solution.py:252
  63.5 33.0 %collective-permute-start.8 = (bf16[256,1024]{1,0:T(8,128)(2,1)S(1)}, bf16[256,1024]{1,0:T(8,128)(2,1)}, u32[]{:S(2)}, u32[]{:S(2)}) collective-permute-start(bf16[256,1024]{1,0:T(8,128)(2,1)S(1)} %slice.19), channel_id=1, source_target_pairs={{0,6},{2,0},{4,2},{6,4},{1,7},{3,1},{5,3},{7,5},{8,14},{10,8},{12,... | collective-permute-start | bytes 1572872 | tf_op jit(solution)/shard_map/ppermute | solution.py:252
  92.0 25.9 %collective-permute-start.9 = (bf16[512,1024]{1,0:T(8,128)(2,1)S(1)}, bf16[512,1024]{1,0:T(8,128)(2,1)S(1)}, u32[]{:S(2)}, u32[]{:S(2)}) collective-permute-start(bf16[512,1024]{1,0:T(8,128)(2,1)S(1)} %bitcast_select_fusion.refs_9_), channel_id=1, source_target_pairs={{0,1},{1,0},{2,3},{3,2},{4,5},{5,4},{6,7},{7,6},{8,9},{9,8},{10,11... | collective-permute-start | bytes 3145736 | tf_op jit(solution)/shard_map/ppermute | solution.py:252
  96.5 34.6 %collective-permute-start.16 = (bf16[512,1024]{1,0:T(8,128)(2,1)}, bf16[512,1024]{1,0:T(8,128)(2,1)}, u32[]{:S(2)}, u32[]{:S(2)}) collective-permute-start(bf16[512,1024]{1,0:T(8,128)(2,1)} %collective-permute-done.refs_19_), channel_id=1, source_target_pairs={{0,1},{1,0},{2,3},{3,2},{4,5},{5,4},{6,7},{7,6},{8,9},{9,8},{10,11... | collective-permute-start | bytes 3145736 | tf_op jit(solution)/shard_map/ppermute | solution.py:252
  98.1 33.1 %collective-permute-start.10 = (bf16[512,1024]{1,0:T(8,128)(2,1)}, bf16[512,1024]{1,0:T(8,128)(2,1)}, u32[]{:S(2)}, u32[]{:S(2)}) collective-permute-start(bf16[512,1024]{1,0:T(8,128)(2,1)} %collective-permute-done.5.refs_10_), channel_id=1, source_target_pairs={{0,1},{1,0},{2,3},{3,2},{4,5},{5,4},{6,7},{7,6},{8,9},{9,8},{10,11... | collective-permute-start | bytes 3145736 | tf_op jit(solution)/shard_map/ppermute | solution.py:252
  98.1 21.7 %collective-permute-start.11 = (bf16[256,1024]{1,0:T(8,128)(2,1)}, bf16[256,1024]{1,0:T(8,128)(2,1)}, u32[]{:S(2)}, u32[]{:S(2)}) collective-permute-start(bf16[256,1024]{1,0:T(8,128)(2,1)} %collective-permute-done.7.refs_11_), channel_id=1, source_target_pairs={{0,1},{1,0},{2,3},{3,2},{4,5},{5,4},{6,7},{7,6},{8,9},{9,8},{10,11... | collective-permute-start | bytes 1572872 | tf_op jit(solution)/shard_map/ppermute | solution.py:252
  98.6 31.2 %collective-permute-start.12 = (bf16[256,1024]{1,0:T(8,128)(2,1)}, bf16[256,1024]{1,0:T(8,128)(2,1)}, u32[]{:S(2)}, u32[]{:S(2)}) collective-permute-start(bf16[256,1024]{1,0:T(8,128)(2,1)} %collective-permute-done.8.refs_12_), channel_id=1, source_target_pairs={{0,1},{1,0},{2,3},{3,2},{4,5},{5,4},{6,7},{7,6},{8,9},{9,8},{10,11... | collective-permute-start | bytes 1572872 | tf_op jit(solution)/shard_map/ppermute | solution.py:252
  100.7 2.5 %copy-start.2 = (bf16[512,5120]{1,0:T(8,128)(2,1)S(1)}, bf16[512,5120]{1,0:T(8,128)(2,1)}, u32[]{:S(2)}) copy-start(bf16[512,5120]{1,0:T(8,128)(2,1)} %all-gather.2.cloned.1.call-done.rows_ref) | copy-start | bytes 15728644
  114.1 17.5 %copy-start.10 = (s32[1,16]{1,0:T(1,128)S(1)}, s32[1,16]{1,0:T(1,128)}, u32[]{:S(2)}) copy-start(s32[1,16]{1,0:T(1,128)} %slots_ref.1) | copy-start | bytes 196
  114.1 17.5 %copy-start.13 = (s32[16,1]{0,1:T(1,128)S(1)}, s32[16,1]{0,1:T(1,128)}, u32[]{:S(2)}) copy-start(s32[16,1]{0,1:T(1,128)} %param.21) | copy-start | bytes 196
  114.1 17.5 %copy-start.14 = (s32[1,16]{1,0:T(1,128)S(1)}, s32[1,16]{1,0:T(1,128)}, u32[]{:S(2)}) copy-start(s32[1,16]{1,0:T(1,128)} %param.19) | copy-start | bytes 196
  114.1 36.4 %copy-start.11 = (f32[128]{0:T(128)S(1)}, f32[128]{0:T(128)}, u32[]{:S(2)}) copy-start(f32[128]{0:T(128)} %param.14) | copy-start | bytes 1540
  114.1 36.4 %copy-start.12 = (f32[128]{0:T(128)S(1)}, f32[128]{0:T(128)}, u32[]{:S(2)}) copy-start(f32[128]{0:T(128)} %param.15) | copy-start | bytes 1540
  118.9 14.5 %collective-permute-start.14 = (bf16[256,1024]{1,0:T(8,128)(2,1)}, bf16[256,1024]{1,0:T(8,128)(2,1)S(1)}, u32[]{:S(2)}, u32[]{:S(2)}) collective-permute-start(bf16[256,1024]{1,0:T(8,128)(2,1)} %slice.14), channel_id=1, source_target_pairs={{0,2},{2,4},{4,6},{6,0},{1,3},{3,5},{5,7},{7,1},{8,10},{10,12},{12... | collective-permute-start | bytes 1572872 | tf_op jit(solution)/shard_map/ppermute | solution.py:252
  119.8 14.9 %collective-permute-start.15 = (bf16[256,1024]{1,0:T(8,128)(2,1)}, bf16[256,1024]{1,0:T(8,128)(2,1)}, u32[]{:S(2)}, u32[]{:S(2)}) collective-permute-start(bf16[256,1024]{1,0:T(8,128)(2,1)} %slice.15), channel_id=1, source_target_pairs={{0,6},{2,0},{4,2},{6,4},{1,7},{3,1},{5,3},{7,5},{8,14},{10,8},{12,... | collective-permute-start | bytes 1572872 | tf_op jit(solution)/shard_map/ppermute | solution.py:252
  121.6 28.9 %all-to-all-start = ((bf16[8,64,640]{2,1,0:T(8,128)(2,1)}), bf16[8,64,640]{2,1,0:T(8,128)(2,1)S(1)}, u32[]{:S(2)}, u32[]{:S(2)}) async-start(bf16[8,64,640]{2,1,0:T(8,128)(2,1)} %bitcast.17), calls=%async_computation | async-start | bytes 1310720 | tf_op jit(solution)/shard_map/all_to_all | solution.py:313
  129.8 5.4 %collective-permute-start.13 = (bf16[512,1024]{1,0:T(8,128)(2,1)}, bf16[512,1024]{1,0:T(8,128)(2,1)}, u32[]{:S(2)}, u32[]{:S(2)}) collective-permute-start(bf16[512,1024]{1,0:T(8,128)(2,1)} %copy-done.3), channel_id=1, source_target_pairs={{0,1},{1,0},{2,3},{3,2},{4,5},{5,4},{6,7},{7,6},{8,9},{9,8},{10,11... | collective-permute-start | bytes 3145736 | tf_op jit(solution)/shard_map/ppermute | solution.py:252
  131.1 4.1 %collective-permute-start.17 = (bf16[512,1024]{1,0:T(8,128)(2,1)}, bf16[512,1024]{1,0:T(8,128)(2,1)}, u32[]{:S(2)}, u32[]{:S(2)}) collective-permute-start(bf16[512,1024]{1,0:T(8,128)(2,1)} %collective-permute-done.2.refs_20_), channel_id=1, source_target_pairs={{0,1},{1,0},{2,3},{3,2},{4,5},{5,4},{6,7},{7,6},{8,9},{9,8},{10,11... | collective-permute-start | bytes 3145736 | tf_op jit(solution)/shard_map/ppermute | solution.py:252
  131.2 5.5 %collective-permute-start.20 = (bf16[512,1024]{1,0:T(8,128)(2,1)}, bf16[512,1024]{1,0:T(8,128)(2,1)}, u32[]{:S(2)}, u32[]{:S(2)}) collective-permute-start(bf16[512,1024]{1,0:T(8,128)(2,1)} %collective-permute-done.1.refs_23_), channel_id=1, source_target_pairs={{0,1},{1,0},{2,3},{3,2},{4,5},{5,4},{6,7},{7,6},{8,9},{9,8},{10,11... | collective-permute-start | bytes 3145736 | tf_op jit(solution)/shard_map/ppermute | solution.py:252
  133.4 4.6 %collective-permute-start.18 = (bf16[256,1024]{1,0:T(8,128)(2,1)S(1)}, bf16[256,1024]{1,0:T(8,128)(2,1)}, u32[]{:S(2)}, u32[]{:S(2)}) collective-permute-start(bf16[256,1024]{1,0:T(8,128)(2,1)S(1)} %collective-permute-done.14.refs_21_), channel_id=1, source_target_pairs={{0,1},{1,0},{2,3},{3,2},{4,5},{5,4},{6,7},{7,6},{8,9},{9,8},{10,11... | collective-permute-start | bytes 1572872 | tf_op jit(solution)/shard_map/ppermute | solution.py:252
  134.7 3.5 %collective-permute-start.19 = (bf16[256,1024]{1,0:T(8,128)(2,1)}, bf16[256,1024]{1,0:T(8,128)(2,1)}, u32[]{:S(2)}, u32[]{:S(2)}) collective-permute-start(bf16[256,1024]{1,0:T(8,128)(2,1)} %collective-permute-done.15.refs_22_), channel_id=1, source_target_pairs={{0,1},{1,0},{2,3},{3,2},{4,5},{5,4},{6,7},{7,6},{8,9},{9,8},{10,11... | collective-permute-start | bytes 1572872 | tf_op jit(solution)/shard_map/ppermute | solution.py:252
  (7 other events, 7.9 us)
Sparse Core Ops, SparseCore 0:
  11.2 68.4 all-gather.1

commit v2 on v1

v2 whole, which is shorter than its diff:
```python
import functools

import jax
import jax.numpy as jnp
import numpy as np
from jax import lax
from jax.experimental import pallas as pl
from jax.experimental.pallas import tpu as pltpu
from jax.sharding import Mesh, PartitionSpec as P

D = 5120
HD = 128
HEADS = 32
KV_HEADS = 4
GROUP = HEADS // KV_HEADS
QD = 4096
KVD = 512
STEPS = 4
SLOTS = 16
HELD = SLOTS // 2
ROWS = STEPS * SLOTS
PLEN = 512
RL = 128
NEW = 16
RK = RL + NEW
SCALE = HD**-0.5
FSDP = ("yl", "z")
SAMPLE = ("yh", "x", "c")


def slot_of(j, yh, x, c):
    return (((j // 4) ^ yh) * 4 + (x + j % 4) % 4) * 2 + c


def prepare_kernel(
    place_ref, table_ref, slots_ref, gain_ref, mine_ref, mate_ref, weights, pool, normed_ref, part_ref, pages_ref, sem
):
    depth = pl.ds(pl.multiple_of(place_ref[2] * (D // 2), 128), D // 2)
    copies = [pltpu.make_async_copy(weights.at[:, depth], part_ref, sem.at[8])]
    for n in range(8):
        copies.append(pltpu.make_async_copy(pool.at[table_ref[n]], pages_ref.at[pl.ds(n * 64, 64)], sem.at[n]))
    for copy in copies:
        copy.start()
    row = lax.broadcasted_iota(jnp.int32, (2 * ROWS, ROWS), 0)
    col = lax.broadcasted_iota(jnp.int32, (2 * ROWS, ROWS), 1)
    want = slot_of(row % ROWS // (2 * STEPS), place_ref[0], place_ref[1], row // ROWS)
    have = jnp.concatenate([slots_ref[...]] * STEPS, axis=1)
    hit = (want == have) & (row % STEPS == col // SLOTS)
    own = row // STEPS % 2 == place_ref[2]
    mine = jnp.where(hit & own, 1.0, 0.0).astype(jnp.bfloat16)
    mate = jnp.where(hit & ~own, 1.0, 0.0).astype(jnp.bfloat16)
    wide = jnp.dot(mine, mine_ref[...], preferred_element_type=jnp.float32)
    wide += jnp.dot(mate, mate_ref[...], preferred_element_type=jnp.float32)
    mean = jnp.mean(wide * wide, axis=-1, keepdims=True)
    normed_ref[...] = (wide * lax.rsqrt(mean + 1e-6) * gain_ref[...]).astype(jnp.bfloat16)
    for copy in copies:
        copy.wait()


def prepare(place, table, slots, gain, mine, mate, weights, pool):
    vmem = pl.BlockSpec(memory_space=pltpu.VMEM)
    smem = pl.BlockSpec(memory_space=pltpu.SMEM)
    hbm = pl.BlockSpec(memory_space=pl.ANY)
    return pl.pallas_call(
        prepare_kernel,
        out_shape=(
            jax.ShapeDtypeStruct((2 * ROWS, D), jnp.bfloat16),
            jax.ShapeDtypeStruct((weights.shape[0], D // 2), jnp.bfloat16),
            jax.ShapeDtypeStruct((PLEN, 2 * KVD), jnp.bfloat16),
        ),
        in_specs=[smem, smem, vmem, vmem, vmem, vmem, hbm, hbm],
        out_specs=(vmem, vmem, vmem),
        scratch_shapes=[pltpu.SemaphoreType.DMA((9,))],
        compiler_params=pltpu.CompilerParams(vmem_limit_bytes=58 * 2**20),
        cost_estimate=pl.CostEstimate(flops=8 * ROWS * ROWS * D, bytes_accessed=8 * 2**20, transcendentals=0),
    )(place, table, slots, gain, mine, mate, weights, pool)


def back_kernel(place_ref, slots_ref, kept_ref, got_ref, out_ref):
    row = lax.broadcasted_iota(jnp.int32, (ROWS, ROWS), 0)
    col = lax.broadcasted_iota(jnp.int32, (ROWS, ROWS), 1)
    have = jnp.concatenate([slots_ref[...]] * STEPS, axis=1)
    turn = (row % STEPS == col // SLOTS) & (row // STEPS % 2 == place_ref[2])
    down = (((0,), (0,)), ((), ()))
    total = jnp.zeros(out_ref.shape, jnp.float32)
    for core, ref in ((place_ref[2], kept_ref), (1 - place_ref[2], got_ref)):
        want = slot_of(row // (2 * STEPS), place_ref[0], place_ref[1], core)
        hit = jnp.where((want == have) & turn, 1.0, 0.0).astype(jnp.bfloat16)
        total += lax.dot_general(hit, ref[...], down, preferred_element_type=jnp.float32)
    out_ref[...] = total.astype(jnp.bfloat16)


def rows_back(place, slots, kept, got):
    vmem = pl.BlockSpec(memory_space=pltpu.VMEM)
    return pl.pallas_call(
        back_kernel,
        out_shape=jax.ShapeDtypeStruct((ROWS, QD), jnp.bfloat16),
        in_specs=[pl.BlockSpec(memory_space=pltpu.SMEM), vmem, vmem, vmem],
        out_specs=vmem,
        compiler_params=pltpu.CompilerParams(vmem_limit_bytes=58 * 2**20),
        cost_estimate=pl.CostEstimate(flops=4 * ROWS * ROWS * QD, bytes_accessed=4 * ROWS * QD, transcendentals=0),
    )(place, slots, kept, got)


KSTEP = 1280


def join_kernel(place_ref, own, near, far, out, sem):
    yl, odd, c = place_ref[0], place_ref[1], place_ref[2]
    head = pl.ds(pl.multiple_of(odd * 64, 64), 256)
    tail = pl.ds(pl.multiple_of((1 - odd) * 256, 64), 64)

    def to(which, size):
        base = which * 256 if size == 256 else 512 + which * 64
        return pl.ds(pl.multiple_of(base, 64), size)

    copies = []
    for rows in (head, tail):
        size = rows.size
        copies.append((own.at[rows], out.at[to(yl, size)]))
        for block, half in ((near, c), (far, 1 - c)):
            depth = pl.ds(pl.multiple_of(half * (D // 2), 128), D // 2)
            copies.append((block.at[rows], out.at[to(1 - yl, size), depth]))
    copies = [pltpu.make_async_copy(src, dst, sem.at[n]) for n, (src, dst) in enumerate(copies)]
    for copy in copies:
        copy.start()
    for copy in copies:
        copy.wait()


def join_weights(place, own_w, near, far):
    hbm = pl.BlockSpec(memory_space=pl.ANY)
    return pl.pallas_call(
        join_kernel,
        out_shape=jax.ShapeDtypeStruct((2 * own_w.shape[0], D), jnp.bfloat16),
        in_specs=[pl.BlockSpec(memory_space=pltpu.SMEM), hbm, hbm, hbm],
        out_specs=pl.BlockSpec(memory_space=pltpu.VMEM),
        scratch_shapes=[pltpu.SemaphoreType.DMA((6,))],
        compiler_params=pltpu.CompilerParams(vmem_limit_bytes=58 * 2**20),
        cost_estimate=pl.CostEstimate(flops=0, bytes_accessed=8 * D * own_w.shape[0], transcendentals=0),
    )(place, own_w, near, far)


def project_kernel(count, own_rows, *refs):
    place_ref, rows, weights, outs, total = refs[0], refs[1 : 1 + count], refs[1 + count], refs[2 + count : -1], refs[-1]
    step = pl.program_id(0)

    @pl.when(step == 0)
    def _():
        total[...] = jnp.zeros_like(total)

    both = [ref[...] for ref in rows]
    if own_rows:
        both[0] = rows[0][pl.ds(pl.multiple_of(place_ref[0] * ROWS, ROWS), ROWS)]
    total[...] += lax.dot_general(
        jnp.concatenate(both, axis=0), weights[...], (((1,), (1,)), ((), ())), preferred_element_type=jnp.float32
    )

    @pl.when(step == pl.num_programs(0) - 1)
    def _():
        base = 0
        for out in outs:
            out[...] = total[base : base + out.shape[0]].astype(jnp.bfloat16)
            base += out.shape[0]


def project(place, weights, arrays, own_rows=False):
    width = weights.shape[0]
    heights = [array.shape[0] for array in arrays]
    if own_rows:
        heights[0] = ROWS
    return pl.pallas_call(
        functools.partial(project_kernel, len(arrays), own_rows),
        out_shape=[jax.ShapeDtypeStruct((height, width), jnp.bfloat16) for height in heights],
        grid_spec=pltpu.PrefetchScalarGridSpec(
            num_scalar_prefetch=1,
            grid=(D // KSTEP,),
            in_specs=[pl.BlockSpec((array.shape[0], KSTEP), lambda step, _: (0, step)) for array in arrays]
            + [pl.BlockSpec((width, KSTEP), lambda step, _: (0, step))],
            out_specs=[pl.BlockSpec((height, width), lambda step, _: (0, 0)) for height in heights],
            scratch_shapes=[pltpu.VMEM((sum(heights), width), jnp.float32)],
        ),
        compiler_params=pltpu.CompilerParams(vmem_limit_bytes=58 * 2**20),
        cost_estimate=pl.CostEstimate(
            flops=2 * sum(heights) * width * D, bytes_accessed=2 * D * (sum(heights) + width), transcendentals=0
        ),
    )(place, *arrays, weights)


def attend_kernel(*refs):
    (order, plen, rlen, spot_z, cosf, sinf, qgain, kgain) = refs[:8]
    pages = refs[8:16]
    resp = refs[16:18]
    near_cols, far_cols = refs[18], refs[19]
    turned_cols = refs[20:26]
    out = refs[26]
    cols, kv, rkv, queries, mixed, sem_c, sem_kv, sem_r = refs[27:]
    core = spot_z[1]
    mine = pl.ds(pl.multiple_of(core * ROWS, ROWS), ROWS)
    place = spot_z[0]
    pltpu.make_async_copy(near_cols, cols.at[place], sem_c).start()
    pltpu.make_async_copy(far_cols, cols.at[(place + 4) % 8], sem_c).start()
    for k in range(3):
        ahead = (k + 1) * (1 - 2 * core)
        pltpu.make_async_copy(turned_cols[2 * k].at[mine], cols.at[(place + ahead + 8) % 8], sem_c).start()
        pltpu.make_async_copy(turned_cols[2 * k + 1].at[mine], cols.at[(place - ahead + 8) % 8], sem_c).start()
    pltpu.make_async_copy(cols, cols, sem_c).wait()
    for n in range(HELD):
        j = n // 4 * 4 + (0, 3 - 2 * core, 1 + 2 * core, 2)[n % 4]
        pltpu.make_async_copy(pages[n], kv.at[j], sem_kv.at[j]).start()
    for j in range(HELD):
        for a, sample in enumerate((core, 1 - core)):
            pltpu.make_async_copy(resp[a].at[order[j]], rkv.at[2 * j + sample, pl.ds(0, RL)], sem_r.at[j]).start()

    low = lax.broadcasted_iota(jnp.int32, (ROWS, HD), 1) < 64

    def head_of(hh):
        half, even, n = hh // 20, hh % 20 // 5 * 2, hh % 5
        if n < 2:
            return cols[even, :, half * 256 + n * HD : half * 256 + (n + 1) * HD].astype(jnp.float32)
        if n > 2:
            return cols[even + 1, :, half * 256 + (n - 3) * HD : half * 256 + (n - 2) * HD].astype(jnp.float32)
        left = cols[even, :, 512:640].astype(jnp.float32)
        right = cols[even + 1, :, 512:640].astype(jnp.float32)
        if half == 0:
            return jnp.where(low, left, pltpu.roll(right, 64, 1))
        return jnp.where(low, pltpu.roll(left, 64, 1), right)

    cosine, sine = cosf[...], sinf[...]

    def turned(hh, gain):
        head = head_of(hh)
        mean = jnp.mean(head * head, axis=-1, keepdims=True)
        head = head * lax.rsqrt(mean + 1e-6) * gain
        return (head * cosine + pltpu.roll(head, 64, 1) * sine).astype(jnp.bfloat16)

    fresh = [turned(HEADS + k, kgain[...]) for k in range(KV_HEADS)]
    fresh += [head_of(HEADS + KV_HEADS + k).astype(jnp.bfloat16) for k in range(KV_HEADS)]
    for k in range(2 * KV_HEADS):
        for n in range(SLOTS):
            rkv[n, RL:RK, k * HD : (k + 1) * HD] = fresh[k][n // 4 * NEW : (n // 4 + 1) * NEW]
    for h in range(HEADS):
        queries[h] = turned(h, qgain[...]).astype(jnp.float32)

    key_p = lax.broadcasted_iota(jnp.int32, (PLEN, 2 * HD), 0)
    key_r = lax.broadcasted_iota(jnp.int32, (RK, 2 * HD), 0)
    lane = lax.broadcasted_iota(jnp.int32, (RK, 2 * HD), 1)
    first = lane // STEPS % 2 == 0
    spot = key_r - RL
    seen = (spot >= 0) & (spot % STEPS <= lane % STEPS)
    turn = spot // STEPS
    first_row = lax.broadcasted_iota(jnp.int32, (2 * STEPS * GROUP, HD), 0) // STEPS % 2 == 0
    across = (((1,), (1,)), ((), ()))
    down = (((0,), (0,)), ((), ()))
    factor = SCALE * 1.4426950408889634
    wide = 2 * STEPS * GROUP
    zero = jnp.zeros((wide, HD), jnp.float32)

    def one_slot(j):
        rows = pl.ds(j * 2 * STEPS, 2 * STEPS)
        spread = []
        for k in range(KV_HEADS):
            q = queries[k * GROUP : (k + 1) * GROUP, rows, :].reshape(wide, HD)
            spread.append(jnp.concatenate([q if n == k else zero for n in range(KV_HEADS)], axis=1))
        q = jnp.concatenate(spread, axis=0).astype(jnp.bfloat16)
        s_p = lax.dot_general(kv[j, :, :KVD], q, across, preferred_element_type=jnp.float32)
        s_p = jnp.where(key_p < plen[j], s_p, -1e30)
        s_r = []
        for a in range(2):
            one = lax.dot_general(rkv[2 * j + a, :, :KVD], q, across, preferred_element_type=jnp.float32)
            s_r.append(jnp.where((key_r < rlen[2 * j + a]) | (seen & (turn == (2 * j + a) % 4)), one, -1e30))
        s_r = jnp.where(first, s_r[0], s_r[1])
        peak = jnp.maximum(jnp.max(s_p, axis=0, keepdims=True), jnp.max(s_r, axis=0, keepdims=True))
        w_p = jnp.exp2((s_p - peak) * factor)
        w_r = jnp.exp2((s_r - peak) * factor)
        share = 1.0 / (jnp.sum(w_p, axis=0, keepdims=True) + jnp.sum(w_r, axis=0, keepdims=True))
        w_p = (w_p * share).astype(jnp.bfloat16)
        w_r = (w_r * share).astype(jnp.bfloat16)
        mix = lax.dot_general(w_p, kv[j, :, KVD:], down, preferred_element_type=jnp.float32)
        mix_r = [
            lax.dot_general(w_r, rkv[2 * j + a, :, KVD:], down, preferred_element_type=jnp.float32) for a in range(2)
        ]
        for k in range(KV_HEADS):
            block = (slice(k * wide, (k + 1) * wide), slice(k * HD, (k + 1) * HD))
            one = mix[block] + jnp.where(first_row, mix_r[0][block], mix_r[1][block])
            mixed[k * GROUP : (k + 1) * GROUP, rows, :] = one.reshape(GROUP, 2 * STEPS, HD)

    def some_slots(i, carry):
        for n in range(BATCH):
            j = i * BATCH + n
            pltpu.make_async_copy(kv.at[j], kv.at[j], sem_kv.at[j]).wait()
            both = rkv.at[pl.ds(2 * j, 2), pl.ds(0, RL)]
            pltpu.make_async_copy(both, both, sem_r.at[j]).wait()
        for n in range(BATCH):
            one_slot(i * BATCH + n)
        return carry

    lax.fori_loop(0, HELD // BATCH, some_slots, 0)
    for h in range(HEADS):
        out[:, h * HD : (h + 1) * HD] = mixed[h].astype(jnp.bfloat16)


BATCH = 2


def attend_all(order, plen, rlen, spot_z, cosf, sinf, qgain, kgain, pages, resp, pieces):
    vmem = pl.BlockSpec(memory_space=pltpu.VMEM)
    smem = pl.BlockSpec(memory_space=pltpu.SMEM)
    hbm = pl.BlockSpec(memory_space=pl.ANY)
    return pl.pallas_call(
        attend_kernel,
        out_shape=jax.ShapeDtypeStruct((ROWS, QD), jnp.bfloat16),
        in_specs=[smem] * 4 + [vmem] * 4 + [hbm] * 18,
        out_specs=vmem,
        scratch_shapes=[
            pltpu.VMEM((8, ROWS, 640), jnp.bfloat16),
            pltpu.VMEM((HELD, PLEN, 2 * KVD), jnp.bfloat16),
            pltpu.VMEM((SLOTS, RK, 2 * KVD), jnp.bfloat16),
            pltpu.VMEM((HEADS, ROWS, HD), jnp.float32),
            pltpu.VMEM((HEADS, ROWS, HD), jnp.float32),
            pltpu.SemaphoreType.DMA,
            pltpu.SemaphoreType.DMA((HELD,)),
            pltpu.SemaphoreType.DMA((HELD,)),
        ],
        compiler_params=pltpu.CompilerParams(vmem_limit_bytes=58 * 2**20),
        cost_estimate=pl.CostEstimate(
            flops=4 * ROWS * QD * (PLEN + RK), bytes_accessed=13 * 2**20, transcendentals=ROWS * HEADS * (PLEN + RK)
        ),
    )(order, plen, rlen, spot_z, cosf, sinf, qgain, kgain, *pages, *resp, *pieces)


def shift(array, axis, size, by):
    return lax.ppermute(array, axis, [(i, (i + by) % size) for i in range(size)])


def turn(array, axis, size, by):
    pairs = []
    for n in range(size):
        for c in range(2):
            pairs.append((n * 2 + c, (n + (by if c == 0 else -by)) % size * 2 + c))
    return lax.ppermute(array, (axis, "c"), pairs)


def swap_block(part):
    pairs = []
    for yl in range(2):
        for yh in range(2):
            for c in range(2):
                pairs.append((yl * 4 + yh * 2 + c, (1 - yl) * 4 + (yh ^ c) * 2 + c))
    return lax.ppermute(part, ("yl", "yh", "c"), pairs)


def per_device(
    hidden,
    norm_gain,
    w_qkv,
    query_gain,
    key_gain,
    prompt_kv,
    block_table,
    prompt_slot,
    prompt_len,
    resp_kv,
    resp_len,
):
    yl, z, yh, x, c = (lax.axis_index(name) for name in FSDP + SAMPLE)
    place = jnp.stack([yh, x, c]).astype(jnp.int32)
    core = c.reshape(1).astype(jnp.int32)
    step = lax.optimization_barrier
    mine = hidden.reshape(ROWS, D)
    mate = shift(mine, "c", 2, 1)
    mate_len = shift(resp_len, "c", 2, 1)
    own_w = w_qkv.T
    normed, part, own = prepare(
        place, block_table[0, 0], prompt_slot, norm_gain.reshape(1, D), mine, mate, own_w, prompt_kv[0]
    )
    resp = resp_kv.reshape(SLOTS, RL, 2 * KVD)

    normed, part, own, resp, mate_len = step((normed, part, own, resp, mate_len))
    rows_1 = turn(normed, "z", 8, 1)
    near = swap_block(part)
    page_a = turn(own, "x", 4, 1)
    mate_resp = shift(resp, "c", 2, 1)
    want = slot_of(jnp.arange(HELD, dtype=jnp.int32), yh, x, c)
    hit = (prompt_slot == want[:, None]).astype(jnp.int32)
    order = jnp.sum(hit * jnp.arange(SLOTS, dtype=jnp.int32)[None, :], axis=1)
    plen = jnp.sum(hit * prompt_len, axis=1)
    lens = jnp.where(c == 0, jnp.concatenate([resp_len, mate_len], axis=1), jnp.concatenate([mate_len, resp_len], axis=1))
    rlen = jnp.sum(hit[:, :, None] * lens[None], axis=1)
    positions = (plen[:, None] + rlen)[:, :, None] + jnp.arange(STEPS, dtype=jnp.int32)
    rlen = rlen.reshape(SLOTS)
    inv_freq = jnp.exp(-jnp.log(1000000.0) * jnp.arange(HD // 2, dtype=jnp.float32) * 2.0 / HD)
    angles = positions.reshape(ROWS, 1).astype(jnp.float32) * inv_freq[None, :]
    cosine, sine = jnp.cos(angles), jnp.sin(angles)
    cosf = jnp.concatenate([cosine, cosine], axis=1)
    sinf = jnp.concatenate([-sine, sine], axis=1)

    spot = jnp.stack([z, c]).astype(jnp.int32)
    where = jnp.stack([yl, z % 2, c]).astype(jnp.int32)

    rows_1, near, page_a, mate_resp, order, plen, rlen, cosf, sinf, spot, where = step(
        (rows_1, near, page_a, mate_resp, order, plen, rlen, cosf, sinf, spot, where)
    )
    rows_2 = turn(rows_1, "z", 8, 1)
    far = shift(near, "c", 2, 1)
    page_b = turn(own, "x", 4, -1)
    other_a = shift(own[: PLEN // 2], "yh", 2, 1)
    weights = join_weights(where, own_w, near, far)
    own_cols, back_1 = project(core, weights, [normed, rows_1], True)

    rows_2, page_b, page_a, weights, back_1, other_a = step((rows_2, page_b, page_a, weights, back_1, other_a))
    other_b = shift(own[PLEN // 2 :], "yh", 2, 1)
    rows_3 = turn(rows_2, "z", 8, 1)
    page_far = turn(page_a, "x", 4, 1)
    cols_1 = turn(back_1, "z", 8, -1)
    (back_2,) = project(core, weights, [rows_2])

    rows_3, page_far, other_b, back_2, cols_1 = step((rows_3, page_far, other_b, back_2, cols_1))
    other = jnp.concatenate([other_a, other_b], axis=0)
    rows_4 = turn(lax.dynamic_slice_in_dim(rows_3, c * ROWS, ROWS, 0), "z", 8, 1)
    page_c = turn(other, "x", 4, 1)
    page_d = turn(other, "x", 4, -1)
    page_e = shift(page_far, "yh", 2, 1)
    cols_2 = turn(back_2, "z", 8, -2)

    back_3, back_4 = project(core, weights, [rows_3, rows_4])
    cols_3 = turn(back_3, "z", 8, -3)
    cols_4 = turn(back_4, "z", 8, -4)
    turned = []
    for cols in (cols_1, cols_2, cols_3):
        turned += [cols, shift(cols, "c", 2, 1)]

    kept = attend_all(
        order,
        plen,
        rlen,
        spot,
        cosf,
        sinf,
        query_gain.reshape(1, HD),
        key_gain.reshape(1, HD),
        [own, page_a, page_b, page_far, other, page_c, page_d, page_e],
        (resp, mate_resp),
        [own_cols, cols_4] + turned,
    )
    got = shift(kept, "c", 2, 1)
    return rows_back(place, prompt_slot, kept, got).reshape(STEPS, SLOTS, 1, QD)


def solution(mesh):
    fine = Mesh(np.asarray(mesh.devices).reshape(2, 8, 2, 4, 2), FSDP + SAMPLE)
    placed = (
        P(None, FSDP, SAMPLE, None),
        P(),
        P(None, FSDP),
        P(),
        P(),
        P(FSDP, SAMPLE, None, None),
        P(FSDP, SAMPLE, None),
        P(FSDP, None),
        P(FSDP, None),
        P(FSDP, SAMPLE, None, None),
        P(FSDP, SAMPLE),
    )
    return jax.shard_map(
        per_device,
        mesh=fine,
        in_specs=placed,
        out_specs=P(None, FSDP, SAMPLE, None),
        check_vma=False,
    )
```

time: 183 us -> 142 us (0.78)
  waiting for transfers between devices: 71.5 us -> 38.7 us
  between operations: 13.6 us -> 0.25 us
  Pallas kernels: 35 us -> 47.3 us
  local copies, waits for them, and re-layouts: 19 us -> 7.33 us
  other arithmetic: 0.98 us -> 3.89 us
    ppermute x0 -> x13, waiting for transfers between devices: none -> 29.3 us  [turn(): return lax.ppermute(array, (axis, 'c'), pairs)]
    ppermute x1, waiting for transfers between devices: 26.2 us -> 0.01 us  [swap_block(): return lax.ppermute(part, ('yl', 'yh', 'c'), pairs)]
    ppermute x20 -> x11, waiting for transfers between devices: 32.9 us -> 9.42 us  [shift(): lax.ppermute(array, axis, [(i, (i + by) % size) for i in range(size)])]
    ppermute x0 -> x13, starting transfers between devices: none -> 23.3 us  [turn(): return lax.ppermute(array, (axis, 'c'), pairs)]
    pallas_call x2 -> x6, Pallas kernels: 12.9 us -> 32.5 us  [the longest x3 18.6 us: project(): pl.pallas_call(functools.partial(project_kernel, len(arrays), own_rows),...]
    all_to_all x1 -> x0, waiting for transfers between devices: 12.3 us -> none  [per_device(): lax.all_to_all(projected, 'z', split_axis=0, concat_axis=0, tiled=True)]
    ppermute x20 -> x11, starting transfers between devices: 30.3 us -> 19.3 us  [shift(): lax.ppermute(array, axis, [(i, (i + by) % size) for i in range(size)])]
    all_to_all x1 -> x0, starting transfers between devices: 8.17 us -> none  [per_device(): lax.all_to_all(projected, 'z', split_axis=0, concat_axis=0, tiled=True)]
  transfers between devices with their start and end apart: 23 -> 25, of which waited for: 7 -> 9; matrix products, arithmetic and copies ran while one was open for 5% -> 5% of each run, Pallas kernels for 6% -> 21%
where the time goes in v2:
time: 142 us; the launch traced here: 141 us
  Pallas kernels  47.3 us (33%)
  starting transfers between devices  43.7 us (31%)
  waiting for transfers between devices  38.7 us (27%)
  local copies, waits for them, and re-layouts  7.33 us (5%)
  other arithmetic  3.89 us (3%)
    ppermute x13, waiting for transfers between devices, turn(): return lax.ppermute(array, (axis, 'c'), pairs)  29.3 us
    ppermute x13, starting transfers between devices, turn(): return lax.ppermute(array, (axis, 'c'), pairs)  23.3 us
    ppermute x11, starting transfers between devices, shift(): lax.ppermute(array, axis, [(i, (i + by) % size) for i in range(size)])  19.3 us
    pallas_call x3, Pallas kernels, project(): pl.pallas_call(functools.partial(project_kernel, len(arrays), own_rows),...  18.6 us
    pallas_call x1, Pallas kernels, attend_all(): pl.pallas_call(attend_kernel, out_shape=jax.ShapeDtypeStruct((ROWS, QD),...  14.7 us
    ppermute x11, waiting for transfers between devices, shift(): lax.ppermute(array, axis, [(i, (i + by) % size) for i in range(size)])  9.42 us
    pallas_call x1, Pallas kernels, join_weights(): pl.pallas_call(join_kernel, out_shape=jax.ShapeDtypeStruct((2 * own_w.sha...  6.3 us
    pallas_call x1, Pallas kernels, prepare(): pl.pallas_call(prepare_kernel, out_shape=(jax.ShapeDtypeStruct((2 * ROWS,...  5.13 us
  transfers between devices with their start and end apart: 25, of which 9 were waited for; matrix products, arithmetic and copies ran while one was open for 5% of the time, Pallas kernels for 21%

profile of v2, /device:TPU:1, one launch (start us, length us, event | category | flops | bytes accessed | tf_op | source)
XLA Modules:
  0.0 141.2 jit_solution(551757352927942391)
XLA Ops:
  0.0 3.2 %collective-permute-start = (bf16[64,5120]{1,0:T(8,128)(2,1)}, bf16[64,5120]{1,0:T(8,128)(2,1)S(1)}, u32[]{:S(2)}, u32[]{:S(2)}) collective-permute-start(bf16[64,5120]{1,0:T(8,128)(2,1)} %bitcast.22), channel_id=1, source_target_pairs={{0,1},{1,0},{2,3},{3,2},{4,5},{5,4},{6,7},{7,6},{8,9},{9,8},{10,11... | collective-permute-start | bytes 1966088 | tf_op jit(solution)/shard_map/ppermute | solution.py:333
  3.8 1.3 collective-permute-done.mate_ref
  5.2 0.9 copy-done.8
  6.0 5.1 %shard_map.109 = (bf16[128,5120]{1,0:T(8,128)(2,1)}, bf16[320,2560]{1,0:T(8,128)(2,1)}, bf16[512,1024]{1,0:T(8,128)(2,1)}) custom-call(s32[3]{0:T(128)} %add_add_fusion.place_ref, s32[8]{0:T(128)} %bitcast.29, s32[1,16]{1,0:T(1,128)} %slots_ref.3, f32[1,5120]{1,0:T(1,128)} %bitcast.24, bf16[64,5120]{1,0:T(8,128)(2,1)} %bitcast.23, ...), custom_call_target="tpu_custom_call" | custom-call | flops 167772160 | bytes 8388608 | tf_op jit(solution)/shard_map/pallas_call | solution.py:64
  11.7 1.1 collective-permute-start.3
  14.2 5.6 %collective-permute-start.2 = (bf16[128,5120]{1,0:T(8,128)(2,1)}, bf16[128,5120]{1,0:T(8,128)(2,1)S(1)}, u32[]{:S(2)}, u32[]{:S(2)}) collective-permute-start(bf16[128,5120]{1,0:T(8,128)(2,1)} %get-tuple-element.42.refs_1_), channel_id=1, source_target_pairs={{0,16},{1,113},{16,32},{17,1},{32,48},{33,17},{48,64},{49,33},{64,... | collective-permute-start | bytes 3932168 | tf_op jit(solution)/shard_map/ppermute | solution.py:341
  19.8 2.5 %collective-permute-start.4 = (bf16[512,1024]{1,0:T(8,128)(2,1)}, bf16[512,1024]{1,0:T(8,128)(2,1)}, u32[]{:S(2)}, u32[]{:S(2)}) collective-permute-start(bf16[512,1024]{1,0:T(8,128)(2,1)} %get-tuple-element.44.refs_8_), channel_id=1, source_target_pairs={{0,2},{1,7},{2,4},{3,1},{4,6},{5,3},{6,0},{7,5},{8,10},{9,15},{10,... | collective-permute-start | bytes 3145736 | tf_op jit(solution)/shard_map/ppermute | solution.py:341
  25.1 9.3 %collective-permute-done.4.refs_9_ = bf16[512,1024]{1,0:T(8,128)(2,1)} collective-permute-done((bf16[512,1024]{1,0:T(8,128)(2,1)}, bf16[512,1024]{1,0:T(8,128)(2,1)}, u32[]{:S(2)}, u32[]{:S(2)}) %collective-permute-start.4) | collective-permute-done | bytes 1048608 | tf_op jit(solution)/shard_map/ppermute | solution.py:341
  34.9 2.9 %collective-permute-start.6 = (bf16[128,5120]{1,0:T(8,128)(2,1)S(1)}, bf16[128,5120]{1,0:T(8,128)(2,1)}, u32[]{:S(2)}, u32[]{:S(2)}) collective-permute-start(bf16[128,5120]{1,0:T(8,128)(2,1)S(1)} %collective-permute-done.2.refs_2_), channel_id=1, source_target_pairs={{0,16},{1,113},{16,32},{17,1},{32,48},{33,17},{48,64},{49,33},{64,... | collective-permute-start | bytes 3932168 | tf_op jit(solution)/shard_map/ppermute | solution.py:341
  37.8 1.2 collective-permute-start.7
  39.0 2.1 %fusion.10 = (bf16[256,1024]{1,0:T(8,128)(2,1)}, bf16[256,1024]{1,0:T(8,128)(2,1)S(1)}) fusion(bf16[512,1024]{1,0:T(8,128)(2,1)} %get-tuple-element.44.refs_8_), kind=kLoop, calls=%fused_computation.36 | loop fusion | bytes 2097152 | tf_op jit(solution)/shard_map/slice | solution.py:412
  41.1 2.2 %collective-permute-start.9 = (bf16[256,1024]{1,0:T(8,128)(2,1)S(1)}, bf16[256,1024]{1,0:T(8,128)(2,1)S(1)}, u32[]{:S(2)}, u32[]{:S(2)}) collective-permute-start(bf16[256,1024]{1,0:T(8,128)(2,1)S(1)} %get-tuple-element.76), channel_id=1, source_target_pairs={{0,8},{8,0},{1,9},{9,1},{2,10},{10,2},{3,11},{11,3},{4,12},{12,4},... | collective-permute-start | bytes 1572872 | tf_op jit(solution)/shard_map/ppermute | solution.py:333
  43.3 1.2 copy-done.3
  44.4 6.3 %shard_map.110.refs_3_.refs_2_ = bf16[640,5120]{1,0:T(8,128)(2,1)} custom-call(s32[3]{0:T(128)} %add_add_fusion.1.place_ref, bf16[320,5120]{1,0:T(8,128)(2,1)} %bitcast.20, bf16[320,2560]{1,0:T(8,128)(2,1)} %copy-done.2, bf16[320,2560]{1,0:T(8,128)(2,1)} %copy-done.3), custom_call_target="tpu_custom_call" | custom-call | bytes 13107200 | tf_op jit(solution)/shard_map/pallas_call | solution.py:133
  50.7 6.4 %shard_map.111 = (bf16[64,640]{1,0:T(8,128)(2,1)}, bf16[128,640]{1,0:T(8,128)(2,1)}) custom-call(s32[1]{0:T(128)} %bitcast.2.refs_0_, bf16[128,5120]{1,0:T(8,128)(2,1)} %get-tuple-element.42.refs_1_, bf16[128,5120]{1,0:T(8,128)(2,1)} %copy-done.4, bf16[640,5120]{1,0:T(8,128)(2,1)} %shard_map.110.refs_3_.refs_2_), custom_call_target="tpu_custom_call" | custom-call | flops 1258291200 | bytes 8519680 | tf_op jit(solution)/shard_map/pallas_call | solution.py:172
  58.0 1.4 %collective-permute-start.11 = (bf16[512,1024]{1,0:T(8,128)(2,1)}, bf16[512,1024]{1,0:T(8,128)(2,1)S(1)}, u32[]{:S(2)}, u32[]{:S(2)}) collective-permute-start(bf16[512,1024]{1,0:T(8,128)(2,1)} %collective-permute-done.4.refs_9_), channel_id=1, source_target_pairs={{0,2},{1,7},{2,4},{3,1},{4,6},{5,3},{6,0},{7,5},{8,10},{9,15},{10,... | collective-permute-start | bytes 3145736 | tf_op jit(solution)/shard_map/ppermute | solution.py:341
  61.0 5.9 %shard_map.112 = bf16[128,640]{1,0:T(8,128)(2,1)} custom-call(s32[1]{0:T(128)} %bitcast.2.refs_0_, bf16[128,5120]{1,0:T(8,128)(2,1)} %collective-permute-done.6.refs_1_, bf16[640,5120]{1,0:T(8,128)(2,1)} %shard_map.110.refs_3_.refs_2_), custom_call_target="tpu_custom_call" | custom-call | flops 838860800 | bytes 7864320 | tf_op jit(solution)/shard_map/pallas_call | solution.py:172
  66.9 6.3 %collective-permute-done.12 = bf16[256,1024]{1,0:T(8,128)(2,1)S(1)} collective-permute-done((bf16[256,1024]{1,0:T(8,128)(2,1)}, bf16[256,1024]{1,0:T(8,128)(2,1)S(1)}, u32[]{:S(2)}, u32[]{:S(2)}) %collective-permute-start.12) | collective-permute-done | bytes 524320 | tf_op jit(solution)/shard_map/ppermute | solution.py:333
  73.3 2.7 %collective-permute-done.10.refs_1_ = bf16[128,5120]{1,0:T(8,128)(2,1)S(1)} collective-permute-done((bf16[128,5120]{1,0:T(8,128)(2,1)}, bf16[128,5120]{1,0:T(8,128)(2,1)S(1)}, u32[]{:S(2)}, u32[]{:S(2)}) %collective-permute-start.10) | collective-permute-done | bytes 1310752 | tf_op jit(solution)/shard_map/ppermute | solution.py:341
  76.0 1.9 %collective-permute-start.17 = (bf16[64,5120]{1,0:T(8,128)(2,1)S(1)}, bf16[64,5120]{1,0:T(8,128)(2,1)}, u32[]{:S(2)}, u32[]{:S(2)}) collective-permute-start(bf16[64,5120]{1,0:T(8,128)(2,1)S(1)} %constant_dynamic-slice_fusion), channel_id=1, source_target_pairs={{0,16},{1,113},{16,32},{17,1},{32,48},{33,17},{48,64},{49,33},{64,... | collective-permute-start | bytes 1966088 | tf_op jit(solution)/shard_map/ppermute | solution.py:341
  78.0 1.5 %collective-permute-start.14 = (bf16[512,1024]{1,0:T(8,128)(2,1)S(1)}, bf16[512,1024]{1,0:T(8,128)(2,1)S(1)}, u32[]{:S(2)}, u32[]{:S(2)}) collective-permute-start(bf16[512,1024]{1,0:T(8,128)(2,1)S(1)} %constant_dynamic-update-slice_fusion.refs_12_), channel_id=1, source_target_pairs={{0,2},{1,7},{2,4},{3,1},{4,6},{5,3},{6,0},{7,5},{8,10},{9,15},{10,... | collective-permute-start | bytes 3145736 | tf_op jit(solution)/shard_map/ppermute | solution.py:341
  80.3 5.7 %collective-permute-done.17.refs_2_ = bf16[64,5120]{1,0:T(8,128)(2,1)} collective-permute-done((bf16[64,5120]{1,0:T(8,128)(2,1)S(1)}, bf16[64,5120]{1,0:T(8,128)(2,1)}, u32[]{:S(2)}, u32[]{:S(2)}) %collective-permute-start.17) | collective-permute-done | bytes 655392 | tf_op jit(solution)/shard_map/ppermute | solution.py:341
  86.1 7.2 %collective-permute-start.19 = (bf16[128,640]{1,0:T(8,128)(2,1)S(1)}, bf16[128,640]{1,0:T(8,128)(2,1)S(1)}, u32[]{:S(2)}, u32[]{:S(2)}) collective-permute-start(bf16[128,640]{1,0:T(8,128)(2,1)S(1)} %collective-permute-done.13.refs_20_), channel_id=1, source_target_pairs={{0,1},{1,0},{2,3},{3,2},{4,5},{5,4},{6,7},{7,6},{8,9},{9,8},{10,11... | collective-permute-start | bytes 491528 | tf_op jit(solution)/shard_map/ppermute | solution.py:333
  93.3 6.3 %shard_map.113 = (bf16[128,640]{1,0:T(8,128)(2,1)}, bf16[64,640]{1,0:T(8,128)(2,1)}) custom-call(s32[1]{0:T(128)} %bitcast.2.refs_0_, bf16[128,5120]{1,0:T(8,128)(2,1)} %copy-done, bf16[64,5120]{1,0:T(8,128)(2,1)} %collective-permute-done.17.refs_2_, bf16[640,5120]{1,0:T(8,128)(2,1)} %shard_map.110.refs_3_.refs_2_), custom_call_target="tpu_custom_call" | custom-call | flops 1258291200 | bytes 8519680 | tf_op jit(solution)/shard_map/pallas_call | solution.py:172
  100.3 1.7 %collective-permute-start.21 = (bf16[128,640]{1,0:T(8,128)(2,1)S(1)}, bf16[128,640]{1,0:T(8,128)(2,1)S(1)}, u32[]{:S(2)}, u32[]{:S(2)}) collective-permute-start(bf16[128,640]{1,0:T(8,128)(2,1)S(1)} %collective-permute-done.20.refs_22_), channel_id=1, source_target_pairs={{0,1},{1,0},{2,3},{3,2},{4,5},{5,4},{6,7},{7,6},{8,9},{9,8},{10,11... | collective-permute-start | bytes 491528 | tf_op jit(solution)/shard_map/ppermute | solution.py:333
  102.0 7.4 %collective-permute-done.22.refs_24_ = bf16[128,640]{1,0:T(8,128)(2,1)S(1)} collective-permute-done((bf16[128,640]{1,0:T(8,128)(2,1)}, bf16[128,640]{1,0:T(8,128)(2,1)S(1)}, u32[]{:S(2)}, u32[]{:S(2)}) %collective-permute-start.22) | collective-permute-done | bytes 163872 | tf_op jit(solution)/shard_map/ppermute | solution.py:341
  109.5 4.0 %collective-permute-start.18 = (bf16[64,640]{1,0:T(8,128)(2,1)}, bf16[64,640]{1,0:T(8,128)(2,1)S(1)}, u32[]{:S(2)}, u32[]{:S(2)}) collective-permute-start(bf16[64,640]{1,0:T(8,128)(2,1)} %get-tuple-element.69), channel_id=1, source_target_pairs={{0,64},{1,65},{16,80},{17,81},{32,96},{33,97},{48,112},{49,113},{6... | collective-permute-start | bytes 245768 | tf_op jit(solution)/shard_map/ppermute | solution.py:341
  113.5 3.8 %collective-permute-done.18.refs_19_ = bf16[64,640]{1,0:T(8,128)(2,1)S(1)} collective-permute-done((bf16[64,640]{1,0:T(8,128)(2,1)}, bf16[64,640]{1,0:T(8,128)(2,1)S(1)}, u32[]{:S(2)}, u32[]{:S(2)}) %collective-permute-start.18) | collective-permute-done | bytes 81952 | tf_op jit(solution)/shard_map/ppermute | solution.py:341
  118.7 14.7 %shard_map.114.kept_ref = bf16[64,4096]{1,0:T(8,128)(2,1)} custom-call(s32[8]{0:T(128)} %get-tuple-element.47.refs_0_, s32[8]{0:T(128)} %copy-done.18, s32[16]{0:T(128)} %reshape.160.refs_2_, s32[2]{0:T(128)} %pad_add_fusion.refs_3_, f32[64,128]{1,0:T(8,128)} %get-tuple-element.51.refs_4_, f32[64,128]{1,0:T(8,128)} %get-tuple-element.52.refs_5_, ...), custom_call_target="tpu_custom_call" | custom-call | flops 687865856 | bytes 13631488 | tf_op jit(solution)/shard_map/pallas_call | solution.py:310
  133.5 2.6 %collective-permute-start.24 = (bf16[64,4096]{1,0:T(8,128)(2,1)}, bf16[64,4096]{1,0:T(8,128)(2,1)S(1)}, u32[]{:S(2)}, u32[]{:S(2)}) collective-permute-start(bf16[64,4096]{1,0:T(8,128)(2,1)} %shard_map.114.kept_ref), channel_id=1, source_target_pairs={{0,1},{1,0},{2,3},{3,2},{4,5},{5,4},{6,7},{7,6},{8,9},{9,8},{10,11... | collective-permute-start | bytes 1572872 | tf_op jit(solution)/shard_map/ppermute | solution.py:333
  136.1 1.7 %collective-permute-done.24.got_ref = bf16[64,4096]{1,0:T(8,128)(2,1)S(1)} collective-permute-done((bf16[64,4096]{1,0:T(8,128)(2,1)}, bf16[64,4096]{1,0:T(8,128)(2,1)S(1)}, u32[]{:S(2)}, u32[]{:S(2)}) %collective-permute-start.24) | collective-permute-done | bytes 524320 | tf_op jit(solution)/shard_map/ppermute | solution.py:333
  138.6 2.5 %shard_map.115 = bf16[64,4096]{1,0:T(8,128)(2,1)} custom-call(s32[3]{0:T(128)} %add_add_fusion.place_ref, s32[1,16]{1,0:T(1,128)} %slots_ref.3, bf16[64,4096]{1,0:T(8,128)(2,1)} %shard_map.114.kept_ref, bf16[64,4096]{1,0:T(8,128)(2,1)} %copy-done.9), custom_call_target="tpu_custom_call" | custom-call | flops 67108864 | bytes 1048576 | tf_op jit(solution)/shard_map/pallas_call | solution.py:95
  (88 shorter events, 12.1 us)
Async XLA Ops:
  0.0 5.2 %collective-permute-start = (bf16[64,5120]{1,0:T(8,128)(2,1)}, bf16[64,5120]{1,0:T(8,128)(2,1)S(1)}, u32[]{:S(2)}, u32[]{:S(2)}) collective-permute-start(bf16[64,5120]{1,0:T(8,128)(2,1)} %bitcast.22), channel_id=1, source_target_pairs={{0,1},{1,0},{2,3},{3,2},{4,5},{5,4},{6,7},{7,6},{8,9},{9,8},{10,11... | collective-permute-start | bytes 1966088 | tf_op jit(solution)/shard_map/ppermute | solution.py:333
  3.2 7.9 %collective-permute-start.1 = (s32[16,1]{0,1:T(1,128)}, s32[16,1]{0,1:T(1,128)S(1)}, u32[]{:S(2)}, u32[]{:S(2)}) collective-permute-start(s32[16,1]{0,1:T(1,128)} %param.21), channel_id=1, source_target_pairs={{0,1},{1,0},{2,3},{3,2},{4,5},{5,4},{6,7},{7,6},{8,9},{9,8},{10,11... | collective-permute-start | bytes 200 | tf_op jit(solution)/shard_map/ppermute | solution.py:333
  11.2 23.4 %collective-permute-start.5 = (bf16[16,128,1024]{2,1,0:T(8,128)(2,1)}, bf16[16,128,1024]{2,1,0:T(8,128)(2,1)}, u32[]{:S(2)}, u32[]{:S(2)}) collective-permute-start(bf16[16,128,1024]{2,1,0:T(8,128)(2,1)} %bitcast.8.refs_16_), channel_id=1, source_target_pairs={{0,1},{1,0},{2,3},{3,2},{4,5},{5,4},{6,7},{7,6},{8,9},{9,8},{10,11... | collective-permute-start | bytes 12582920 | tf_op jit(solution)/shard_map/ppermute | solution.py:333
  11.7 23.0 %collective-permute-start.3 = (bf16[320,2560]{1,0:T(8,128)(2,1)}, bf16[320,2560]{1,0:T(8,128)(2,1)S(1)}, u32[]{:S(2)}, u32[]{:S(2)}) collective-permute-start(bf16[320,2560]{1,0:T(8,128)(2,1)} %get-tuple-element.43), channel_id=1, source_target_pairs={{0,128},{1,137},{8,136},{9,129},{128,0},{129,9},{136,8},{137,1},{2... | collective-permute-start | bytes 4915208 | tf_op jit(solution)/shard_map/ppermute | solution.py:350
  14.2 36.6 %copy-start.18 = (s32[8]{0:T(128)}, s32[8]{0:T(128)S(1)}, u32[]{:S(2)}) copy-start(s32[8]{0:T(128)S(1)} %get-tuple-element.48.refs_1_) | copy-start | bytes 100
  14.2 20.4 %collective-permute-start.2 = (bf16[128,5120]{1,0:T(8,128)(2,1)}, bf16[128,5120]{1,0:T(8,128)(2,1)S(1)}, u32[]{:S(2)}, u32[]{:S(2)}) collective-permute-start(bf16[128,5120]{1,0:T(8,128)(2,1)} %get-tuple-element.42.refs_1_), channel_id=1, source_target_pairs={{0,16},{1,113},{16,32},{17,1},{32,48},{33,17},{48,64},{49,33},{64,... | collective-permute-start | bytes 3932168 | tf_op jit(solution)/shard_map/ppermute | solution.py:341
  19.8 14.5 %collective-permute-start.4 = (bf16[512,1024]{1,0:T(8,128)(2,1)}, bf16[512,1024]{1,0:T(8,128)(2,1)}, u32[]{:S(2)}, u32[]{:S(2)}) collective-permute-start(bf16[512,1024]{1,0:T(8,128)(2,1)} %get-tuple-element.44.refs_8_), channel_id=1, source_target_pairs={{0,2},{1,7},{2,4},{3,1},{4,6},{5,3},{6,0},{7,5},{8,10},{9,15},{10,... | collective-permute-start | bytes 3145736 | tf_op jit(solution)/shard_map/ppermute | solution.py:341
  34.6 8.6 %collective-permute-start.8 = (bf16[320,2560]{1,0:T(8,128)(2,1)S(1)}, bf16[320,2560]{1,0:T(8,128)(2,1)S(1)}, u32[]{:S(2)}, u32[]{:S(2)}) collective-permute-start(bf16[320,2560]{1,0:T(8,128)(2,1)S(1)} %collective-permute-done.3.near), channel_id=1, source_target_pairs={{0,1},{1,0},{2,3},{3,2},{4,5},{5,4},{6,7},{7,6},{8,9},{9,8},{10,11... | collective-permute-start | bytes 4915208 | tf_op jit(solution)/shard_map/ppermute | solution.py:333
  34.9 22.2 %collective-permute-start.6 = (bf16[128,5120]{1,0:T(8,128)(2,1)S(1)}, bf16[128,5120]{1,0:T(8,128)(2,1)}, u32[]{:S(2)}, u32[]{:S(2)}) collective-permute-start(bf16[128,5120]{1,0:T(8,128)(2,1)S(1)} %collective-permute-done.2.refs_2_), channel_id=1, source_target_pairs={{0,16},{1,113},{16,32},{17,1},{32,48},{33,17},{48,64},{49,33},{64,... | collective-permute-start | bytes 3932168 | tf_op jit(solution)/shard_map/ppermute | solution.py:341
  37.8 19.3 %collective-permute-start.7 = (bf16[512,1024]{1,0:T(8,128)(2,1)}, bf16[512,1024]{1,0:T(8,128)(2,1)}, u32[]{:S(2)}, u32[]{:S(2)}) collective-permute-start(bf16[512,1024]{1,0:T(8,128)(2,1)} %get-tuple-element.44.refs_8_), channel_id=1, source_target_pairs={{0,6},{1,3},{2,0},{3,5},{4,2},{5,7},{6,4},{7,1},{8,14},{9,11},{10,... | collective-permute-start | bytes 3145736 | tf_op jit(solution)/shard_map/ppermute | solution.py:341
  41.1 16.0 %collective-permute-start.9 = (bf16[256,1024]{1,0:T(8,128)(2,1)S(1)}, bf16[256,1024]{1,0:T(8,128)(2,1)S(1)}, u32[]{:S(2)}, u32[]{:S(2)}) collective-permute-start(bf16[256,1024]{1,0:T(8,128)(2,1)S(1)} %get-tuple-element.76), channel_id=1, source_target_pairs={{0,8},{8,0},{1,9},{9,1},{2,10},{10,2},{3,11},{11,3},{4,12},{12,4},... | collective-permute-start | bytes 1572872 | tf_op jit(solution)/shard_map/ppermute | solution.py:333
  57.2 18.8 %collective-permute-start.10 = (bf16[128,5120]{1,0:T(8,128)(2,1)}, bf16[128,5120]{1,0:T(8,128)(2,1)S(1)}, u32[]{:S(2)}, u32[]{:S(2)}) collective-permute-start(bf16[128,5120]{1,0:T(8,128)(2,1)} %collective-permute-done.6.refs_1_), channel_id=1, source_target_pairs={{0,16},{1,113},{16,32},{17,1},{32,48},{33,17},{48,64},{49,33},{64,... | collective-permute-start | bytes 3932168 | tf_op jit(solution)/shard_map/ppermute | solution.py:341
  58.0 15.3 %collective-permute-start.11 = (bf16[512,1024]{1,0:T(8,128)(2,1)}, bf16[512,1024]{1,0:T(8,128)(2,1)S(1)}, u32[]{:S(2)}, u32[]{:S(2)}) collective-permute-start(bf16[512,1024]{1,0:T(8,128)(2,1)} %collective-permute-done.4.refs_9_), channel_id=1, source_target_pairs={{0,2},{1,7},{2,4},{3,1},{4,6},{5,3},{6,0},{7,5},{8,10},{9,15},{10,... | collective-permute-start | bytes 3145736 | tf_op jit(solution)/shard_map/ppermute | solution.py:341
  59.4 13.8 %collective-permute-start.12 = (bf16[256,1024]{1,0:T(8,128)(2,1)}, bf16[256,1024]{1,0:T(8,128)(2,1)S(1)}, u32[]{:S(2)}, u32[]{:S(2)}) collective-permute-start(bf16[256,1024]{1,0:T(8,128)(2,1)} %get-tuple-element.75), channel_id=1, source_target_pairs={{0,8},{8,0},{1,9},{9,1},{2,10},{10,2},{3,11},{11,3},{4,12},{12,4},... | collective-permute-start | bytes 1572872 | tf_op jit(solution)/shard_map/ppermute | solution.py:333
  60.3 13.0 %collective-permute-start.13 = (bf16[128,640]{1,0:T(8,128)(2,1)}, bf16[128,640]{1,0:T(8,128)(2,1)S(1)}, u32[]{:S(2)}, u32[]{:S(2)}) collective-permute-start(bf16[128,640]{1,0:T(8,128)(2,1)} %get-tuple-element.62), channel_id=1, source_target_pairs={{0,112},{1,17},{16,0},{17,33},{32,16},{33,49},{48,32},{49,65},{64,... | collective-permute-start | bytes 491528 | tf_op jit(solution)/shard_map/ppermute | solution.py:341
  73.2 26.3 %copy-start.10 = (bf16[128,640]{1,0:T(8,128)(2,1)}, bf16[128,640]{1,0:T(8,128)(2,1)S(1)}, u32[]{:S(2)}) copy-start(bf16[128,640]{1,0:T(8,128)(2,1)S(1)} %collective-permute-done.13.refs_20_) | copy-start | bytes 491524
  73.2 26.3 %copy-start.5 = (bf16[512,1024]{1,0:T(8,128)(2,1)}, bf16[512,1024]{1,0:T(8,128)(2,1)S(1)}, u32[]{:S(2)}) copy-start(bf16[512,1024]{1,0:T(8,128)(2,1)S(1)} %collective-permute-done.11.refs_11_) | copy-start | bytes 3145732
  76.0 17.3 %copy-start = (bf16[128,5120]{1,0:T(8,128)(2,1)}, bf16[128,5120]{1,0:T(8,128)(2,1)S(1)}, u32[]{:S(2)}) copy-start(bf16[128,5120]{1,0:T(8,128)(2,1)S(1)} %collective-permute-done.10.refs_1_) | copy-start | bytes 3932164
  76.0 10.1 %collective-permute-start.17 = (bf16[64,5120]{1,0:T(8,128)(2,1)S(1)}, bf16[64,5120]{1,0:T(8,128)(2,1)}, u32[]{:S(2)}, u32[]{:S(2)}) collective-permute-start(bf16[64,5120]{1,0:T(8,128)(2,1)S(1)} %constant_dynamic-slice_fusion), channel_id=1, source_target_pairs={{0,16},{1,113},{16,32},{17,1},{32,48},{33,17},{48,64},{49,33},{64,... | collective-permute-start | bytes 1966088 | tf_op jit(solution)/shard_map/ppermute | solution.py:341
  77.9 21.6 %copy-start.1 = (bf16[512,1024]{1,0:T(8,128)(2,1)}, bf16[512,1024]{1,0:T(8,128)(2,1)S(1)}, u32[]{:S(2)}) copy-start(bf16[512,1024]{1,0:T(8,128)(2,1)S(1)} %constant_dynamic-update-slice_fusion.refs_12_) | copy-start | bytes 3145732
  78.0 39.4 %collective-permute-start.14 = (bf16[512,1024]{1,0:T(8,128)(2,1)S(1)}, bf16[512,1024]{1,0:T(8,128)(2,1)S(1)}, u32[]{:S(2)}, u32[]{:S(2)}) collective-permute-start(bf16[512,1024]{1,0:T(8,128)(2,1)S(1)} %constant_dynamic-update-slice_fusion.refs_12_), channel_id=1, source_target_pairs={{0,2},{1,7},{2,4},{3,1},{4,6},{5,3},{6,0},{7,5},{8,10},{9,15},{10,... | collective-permute-start | bytes 3145736 | tf_op jit(solution)/shard_map/ppermute | solution.py:341
  79.5 37.9 %collective-permute-start.15 = (bf16[512,1024]{1,0:T(8,128)(2,1)S(1)}, bf16[512,1024]{1,0:T(8,128)(2,1)S(1)}, u32[]{:S(2)}, u32[]{:S(2)}) collective-permute-start(bf16[512,1024]{1,0:T(8,128)(2,1)S(1)} %constant_dynamic-update-slice_fusion.refs_12_), channel_id=1, source_target_pairs={{0,6},{1,3},{2,0},{3,5},{4,2},{5,7},{6,4},{7,1},{8,14},{9,11},{10,... | collective-permute-start | bytes 3145736 | tf_op jit(solution)/shard_map/ppermute | solution.py:341
  79.5 37.8 %collective-permute-start.16 = (bf16[512,1024]{1,0:T(8,128)(2,1)S(1)}, bf16[512,1024]{1,0:T(8,128)(2,1)}, u32[]{:S(2)}, u32[]{:S(2)}) collective-permute-start(bf16[512,1024]{1,0:T(8,128)(2,1)S(1)} %collective-permute-done.11.refs_11_), channel_id=1, source_target_pairs={{0,8},{8,0},{1,9},{9,1},{2,10},{10,2},{3,11},{11,3},{4,12},{12,4},... | collective-permute-start | bytes 3145736 | tf_op jit(solution)/shard_map/ppermute | solution.py:333
  80.3 19.2 %collective-permute-start.20 = (bf16[128,640]{1,0:T(8,128)(2,1)}, bf16[128,640]{1,0:T(8,128)(2,1)S(1)}, u32[]{:S(2)}, u32[]{:S(2)}) collective-permute-start(bf16[128,640]{1,0:T(8,128)(2,1)} %shard_map.112), channel_id=1, source_target_pairs={{0,96},{1,33},{16,112},{17,49},{32,0},{33,65},{48,16},{49,81},{64,... | collective-permute-start | bytes 491528 | tf_op jit(solution)/shard_map/ppermute | solution.py:341
  86.1 14.2 %collective-permute-start.19 = (bf16[128,640]{1,0:T(8,128)(2,1)S(1)}, bf16[128,640]{1,0:T(8,128)(2,1)S(1)}, u32[]{:S(2)}, u32[]{:S(2)}) collective-permute-start(bf16[128,640]{1,0:T(8,128)(2,1)S(1)} %collective-permute-done.13.refs_20_), channel_id=1, source_target_pairs={{0,1},{1,0},{2,3},{3,2},{4,5},{5,4},{6,7},{7,6},{8,9},{9,8},{10,11... | collective-permute-start | bytes 491528 | tf_op jit(solution)/shard_map/ppermute | solution.py:333
  99.6 17.8 %copy-start.11 = (bf16[128,640]{1,0:T(8,128)(2,1)}, bf16[128,640]{1,0:T(8,128)(2,1)S(1)}, u32[]{:S(2)}) copy-start(bf16[128,640]{1,0:T(8,128)(2,1)S(1)} %collective-permute-done.20.refs_22_) | copy-start | bytes 491524
  99.6 9.9 %collective-permute-start.22 = (bf16[128,640]{1,0:T(8,128)(2,1)}, bf16[128,640]{1,0:T(8,128)(2,1)S(1)}, u32[]{:S(2)}, u32[]{:S(2)}) collective-permute-start(bf16[128,640]{1,0:T(8,128)(2,1)} %get-tuple-element.72), channel_id=1, source_target_pairs={{0,80},{1,49},{16,96},{17,65},{32,112},{33,81},{48,0},{49,97},{64,... | collective-permute-start | bytes 491528 | tf_op jit(solution)/shard_map/ppermute | solution.py:341
  100.3 17.0 %copy-start.12 = (bf16[128,640]{1,0:T(8,128)(2,1)}, bf16[128,640]{1,0:T(8,128)(2,1)S(1)}, u32[]{:S(2)}) copy-start(bf16[128,640]{1,0:T(8,128)(2,1)S(1)} %collective-permute-done.19.refs_21_) | copy-start | bytes 491524
  100.3 9.1 %collective-permute-start.21 = (bf16[128,640]{1,0:T(8,128)(2,1)S(1)}, bf16[128,640]{1,0:T(8,128)(2,1)S(1)}, u32[]{:S(2)}, u32[]{:S(2)}) collective-permute-start(bf16[128,640]{1,0:T(8,128)(2,1)S(1)} %collective-permute-done.20.refs_22_), channel_id=1, source_target_pairs={{0,1},{1,0},{2,3},{3,2},{4,5},{5,4},{6,7},{7,6},{8,9},{9,8},{10,11... | collective-permute-start | bytes 491528 | tf_op jit(solution)/shard_map/ppermute | solution.py:333
  109.5 7.8 %collective-permute-start.23 = (bf16[128,640]{1,0:T(8,128)(2,1)S(1)}, bf16[128,640]{1,0:T(8,128)(2,1)S(1)}, u32[]{:S(2)}, u32[]{:S(2)}) collective-permute-start(bf16[128,640]{1,0:T(8,128)(2,1)S(1)} %collective-permute-done.22.refs_24_), channel_id=1, source_target_pairs={{0,1},{1,0},{2,3},{3,2},{4,5},{5,4},{6,7},{7,6},{8,9},{9,8},{10,11... | collective-permute-start | bytes 491528 | tf_op jit(solution)/shard_map/ppermute | solution.py:333
  109.5 7.8 %collective-permute-start.18 = (bf16[64,640]{1,0:T(8,128)(2,1)}, bf16[64,640]{1,0:T(8,128)(2,1)S(1)}, u32[]{:S(2)}, u32[]{:S(2)}) collective-permute-start(bf16[64,640]{1,0:T(8,128)(2,1)} %get-tuple-element.69), channel_id=1, source_target_pairs={{0,64},{1,65},{16,80},{17,81},{32,96},{33,97},{48,112},{49,113},{6... | collective-permute-start | bytes 245768 | tf_op jit(solution)/shard_map/ppermute | solution.py:341
  133.5 4.3 %collective-permute-start.24 = (bf16[64,4096]{1,0:T(8,128)(2,1)}, bf16[64,4096]{1,0:T(8,128)(2,1)S(1)}, u32[]{:S(2)}, u32[]{:S(2)}) collective-permute-start(bf16[64,4096]{1,0:T(8,128)(2,1)} %shard_map.114.kept_ref), channel_id=1, source_target_pairs={{0,1},{1,0},{2,3},{3,2},{4,5},{5,4},{6,7},{7,6},{8,9},{9,8},{10,11... | collective-permute-start | bytes 1572872 | tf_op jit(solution)/shard_map/ppermute | solution.py:333
  (14 other events, 78.9 us)

commit v3 on v2

--- a/solution.py
+++ b/solution.py
@@ -47,10 +47,9 @@
     have = jnp.concatenate([slots_ref[...]] * STEPS, axis=1)
     hit = (want == have) & (row % STEPS == col // SLOTS)
     own = row // STEPS % 2 == place_ref[2]
-    mine = jnp.where(hit & own, 1.0, 0.0).astype(jnp.bfloat16)
-    mate = jnp.where(hit & ~own, 1.0, 0.0).astype(jnp.bfloat16)
-    wide = jnp.dot(mine, mine_ref[...], preferred_element_type=jnp.float32)
-    wide += jnp.dot(mate, mate_ref[...], preferred_element_type=jnp.float32)
+    pick = jnp.concatenate([jnp.where(hit & own, 1.0, 0.0), jnp.where(hit & ~own, 1.0, 0.0)], axis=1)
+    both = jnp.concatenate([mine_ref[...], mate_ref[...]], axis=0)
+    wide = jnp.dot(pick.astype(jnp.bfloat16), both, preferred_element_type=jnp.float32)
     mean = jnp.mean(wide * wide, axis=-1, keepdims=True)
     normed_ref[...] = (wide * lax.rsqrt(mean + 1e-6) * gain_ref[...]).astype(jnp.bfloat16)
     for copy in copies:
@@ -71,7 +70,7 @@
         in_specs=[smem, smem, vmem, vmem, vmem, vmem, hbm, hbm],
         out_specs=(vmem, vmem, vmem),
         scratch_shapes=[pltpu.SemaphoreType.DMA((9,))],
-        compiler_params=pltpu.CompilerParams(vmem_limit_bytes=58 * 2**20),
+        compiler_params=pltpu.CompilerParams(vmem_limit_bytes=62 * 2**20),
         cost_estimate=pl.CostEstimate(flops=8 * ROWS * ROWS * D, bytes_accessed=8 * 2**20, transcendentals=0),
     )(place, table, slots, gain, mine, mate, weights, pool)
 
@@ -97,16 +96,16 @@
         out_shape=jax.ShapeDtypeStruct((ROWS, QD), jnp.bfloat16),
         in_specs=[pl.BlockSpec(memory_space=pltpu.SMEM), vmem, vmem, vmem],
         out_specs=vmem,
-        compiler_params=pltpu.CompilerParams(vmem_limit_bytes=58 * 2**20),
+        compiler_params=pltpu.CompilerParams(vmem_limit_bytes=62 * 2**20),
         cost_estimate=pl.CostEstimate(flops=4 * ROWS * ROWS * QD, bytes_accessed=4 * ROWS * QD, transcendentals=0),
     )(place, slots, kept, got)
 
 
-KSTEP = 1280
+KSTEP = 2560
 
 
 def join_kernel(place_ref, own, near, far, out, sem):
-    yl, odd, c = place_ref[0], place_ref[1], place_ref[2]
+    c, yl, odd = place_ref[2], place_ref[3], place_ref[4]
     head = pl.ds(pl.multiple_of(odd * 64, 64), 256)
     tail = pl.ds(pl.multiple_of((1 - odd) * 256, 64), 64)
 
@@ -136,7 +135,7 @@
         in_specs=[pl.BlockSpec(memory_space=pltpu.SMEM), hbm, hbm, hbm],
         out_specs=pl.BlockSpec(memory_space=pltpu.VMEM),
         scratch_shapes=[pltpu.SemaphoreType.DMA((6,))],
-        compiler_params=pltpu.CompilerParams(vmem_limit_bytes=58 * 2**20),
+        compiler_params=pltpu.CompilerParams(vmem_limit_bytes=62 * 2**20),
         cost_estimate=pl.CostEstimate(flops=0, bytes_accessed=8 * D * own_w.shape[0], transcendentals=0),
     )(place, own_w, near, far)
 
@@ -151,7 +150,7 @@
 
     both = [ref[...] for ref in rows]
     if own_rows:
-        both[0] = rows[0][pl.ds(pl.multiple_of(place_ref[0] * ROWS, ROWS), ROWS)]
+        both[0] = rows[0][pl.ds(pl.multiple_of(place_ref[2] * ROWS, ROWS), ROWS)]
     total[...] += lax.dot_general(
         jnp.concatenate(both, axis=0), weights[...], (((1,), (1,)), ((), ())), preferred_element_type=jnp.float32
     )
@@ -180,7 +179,7 @@
             out_specs=[pl.BlockSpec((height, width), lambda step, _: (0, 0)) for height in heights],
             scratch_shapes=[pltpu.VMEM((sum(heights), width), jnp.float32)],
         ),
-        compiler_params=pltpu.CompilerParams(vmem_limit_bytes=58 * 2**20),
+        compiler_params=pltpu.CompilerParams(vmem_limit_bytes=62 * 2**20),
         cost_estimate=pl.CostEstimate(
             flops=2 * sum(heights) * width * D, bytes_accessed=2 * D * (sum(heights) + width), transcendentals=0
         ),
@@ -195,9 +194,9 @@
     turned_cols = refs[20:26]
     out = refs[26]
     cols, kv, rkv, queries, mixed, sem_c, sem_kv, sem_r = refs[27:]
-    core = spot_z[1]
+    core = spot_z[2]
     mine = pl.ds(pl.multiple_of(core * ROWS, ROWS), ROWS)
-    place = spot_z[0]
+    place = spot_z[5]
     pltpu.make_async_copy(near_cols, cols.at[place], sem_c).start()
     pltpu.make_async_copy(far_cols, cols.at[(place + 4) % 8], sem_c).start()
     for k in range(3):
@@ -322,7 +321,7 @@
             pltpu.SemaphoreType.DMA((HELD,)),
             pltpu.SemaphoreType.DMA((HELD,)),
         ],
-        compiler_params=pltpu.CompilerParams(vmem_limit_bytes=58 * 2**20),
+        compiler_params=pltpu.CompilerParams(vmem_limit_bytes=62 * 2**20),
         cost_estimate=pl.CostEstimate(
             flops=4 * ROWS * QD * (PLEN + RK), bytes_accessed=13 * 2**20, transcendentals=ROWS * HEADS * (PLEN + RK)
         ),
@@ -364,8 +363,7 @@
     resp_len,
 ):
     yl, z, yh, x, c = (lax.axis_index(name) for name in FSDP + SAMPLE)
-    place = jnp.stack([yh, x, c]).astype(jnp.int32)
-    core = c.reshape(1).astype(jnp.int32)
+    place = jnp.stack([yh, x, c, yl, z % 2, z]).astype(jnp.int32)
     step = lax.optimization_barrier
     mine = hidden.reshape(ROWS, D)
     mate = shift(mine, "c", 2, 1)
@@ -381,8 +379,27 @@
     near = swap_block(part)
     page_a = turn(own, "x", 4, 1)
     mate_resp = shift(resp, "c", 2, 1)
+
+    rows_1, near, page_a, mate_resp = step((rows_1, near, page_a, mate_resp))
+    rows_2 = turn(rows_1, "z", 8, 1)
+    far = shift(near, "c", 2, 1)
+    page_far = turn(page_a, "x", 4, 1)
+    other_a = shift(own[: PLEN // 2], "yh", 2, 1)
+    weights = join_weights(place, own_w, near, far)
+    own_cols, back_1 = project(place, weights, [normed, rows_1], True)
+
+    rows_2, page_far, weights, back_1, other_a, slots, own = step(
+        (rows_2, page_far, weights, back_1, other_a, prompt_slot, own)
+    )
+    other_b = shift(own[PLEN // 2 :], "yh", 2, 1)
+    rows_3 = turn(rows_2, "z", 8, 1)
+    page_b = turn(own, "x", 4, -1)
+    page_e = shift(page_far, "yh", 2, 1)
+    cols_1 = turn(back_1, "z", 8, -1)
+    (back_2,) = project(place, weights, [rows_2])
+
     want = slot_of(jnp.arange(HELD, dtype=jnp.int32), yh, x, c)
-    hit = (prompt_slot == want[:, None]).astype(jnp.int32)
+    hit = (slots == want[:, None]).astype(jnp.int32)
     order = jnp.sum(hit * jnp.arange(SLOTS, dtype=jnp.int32)[None, :], axis=1)
     plen = jnp.sum(hit * prompt_len, axis=1)
     lens = jnp.where(c == 0, jnp.concatenate([resp_len, mate_len], axis=1), jnp.concatenate([mate_len, resp_len], axis=1))
@@ -395,37 +412,20 @@
     cosf = jnp.concatenate([cosine, cosine], axis=1)
     sinf = jnp.concatenate([-sine, sine], axis=1)
 
-    spot = jnp.stack([z, c]).astype(jnp.int32)
-    where = jnp.stack([yl, z % 2, c]).astype(jnp.int32)
-
-    rows_1, near, page_a, mate_resp, order, plen, rlen, cosf, sinf, spot, where = step(
-        (rows_1, near, page_a, mate_resp, order, plen, rlen, cosf, sinf, spot, where)
-    )
-    rows_2 = turn(rows_1, "z", 8, 1)
-    far = shift(near, "c", 2, 1)
-    page_b = turn(own, "x", 4, -1)
-    other_a = shift(own[: PLEN // 2], "yh", 2, 1)
-    weights = join_weights(where, own_w, near, far)
-    own_cols, back_1 = project(core, weights, [normed, rows_1], True)
-
-    rows_2, page_b, page_a, weights, back_1, other_a = step((rows_2, page_b, page_a, weights, back_1, other_a))
-    other_b = shift(own[PLEN // 2 :], "yh", 2, 1)
-    rows_3 = turn(rows_2, "z", 8, 1)
-    page_far = turn(page_a, "x", 4, 1)
-    cols_1 = turn(back_1, "z", 8, -1)
-    (back_2,) = project(core, weights, [rows_2])
-
-    rows_3, page_far, other_b, back_2, cols_1 = step((rows_3, page_far, other_b, back_2, cols_1))
+
+    rows_3, page_b, other_b, back_2, cols_1, order, plen, rlen, cosf, sinf = step(
+        (rows_3, page_b, other_b, back_2, cols_1, order, plen, rlen, cosf, sinf)
+    )
     other = jnp.concatenate([other_a, other_b], axis=0)
     rows_4 = turn(lax.dynamic_slice_in_dim(rows_3, c * ROWS, ROWS, 0), "z", 8, 1)
     page_c = turn(other, "x", 4, 1)
     page_d = turn(other, "x", 4, -1)
-    page_e = shift(page_far, "yh", 2, 1)
     cols_2 = turn(back_2, "z", 8, -2)
 
-    back_3, back_4 = project(core, weights, [rows_3, rows_4])
+    back_3, back_4 = project(place, weights, [rows_3, rows_4])
     cols_3 = turn(back_3, "z", 8, -3)
     cols_4 = turn(back_4, "z", 8, -4)
+    cols_3, cols_4 = step((cols_3, cols_4))
     turned = []
     for cols in (cols_1, cols_2, cols_3):
         turned += [cols, shift(cols, "c", 2, 1)]
@@ -434,7 +434,7 @@
         order,
         plen,
         rlen,
-        spot,
+        place,
         cosf,
         sinf,
         query_gain.reshape(1, HD),

time: 142 us -> 139 us (0.979); the launches traced: 141 us -> 137 us
  waiting for transfers between devices: 38.7 us -> 31.4 us
  local copies, waits for them, and re-layouts: 7.33 us -> 13.5 us
  other arithmetic: 3.89 us -> 1.95 us
    ppermute x13, waiting for transfers between devices: 29.3 us -> 23.8 us  [turn(): return lax.ppermute(array, (axis, 'c'), pairs)]
    ppermute x11, starting transfers between devices: 19.3 us -> 17.1 us  [shift(): lax.ppermute(array, axis, [(i, (i + by) % size) for i in range(size)])]
    another operation x3 -> x0, other arithmetic: 1.91 us -> none  [the longest x1 0.66 us: per_device(): where = jnp.stack([yl, z % 2, c]).astype(jnp.int32)]
    unnamed x43 -> x35, local copies, waits for them, and re-layouts: 4.25 us -> 6.14 us
    slice x0 -> x1, local copies, waits for them, and re-layouts: none -> 1.87 us  [per_device(): other_a = shift(own[:PLEN // 2], 'yh', 2, 1)]
    concatenate x1, local copies, waits for them, and re-layouts: 0.03 us -> 1.9 us  [per_device(): other = jnp.concatenate([other_a, other_b], axis=0)]
    ppermute x11, waiting for transfers between devices: 9.42 us -> 7.57 us  [shift(): lax.ppermute(array, axis, [(i, (i + by) % size) for i in range(size)])]
  transfers between devices with their start and end apart: 25 -> 25, of which waited for: 9 -> 10; matrix products, arithmetic and copies ran while one was open for 5% -> 8% of each run, Pallas kernels for 21% -> 22%
where the time goes in v3:
time: 139 us; the launch traced here: 137 us
  Pallas kernels  47.1 us (34%)
  starting transfers between devices  42.5 us (31%)
  waiting for transfers between devices  31.4 us (23%)
  local copies, waits for them, and re-layouts  13.5 us (10%)
  other arithmetic  1.95 us (1%)
    ppermute x13, starting transfers between devices, turn(): return lax.ppermute(array, (axis, 'c'), pairs)  24.4 us
    ppermute x13, waiting for transfers between devices, turn(): return lax.ppermute(array, (axis, 'c'), pairs)  23.8 us
    pallas_call x3, Pallas kernels, project(): pl.pallas_call(functools.partial(project_kernel, len(arrays), own_rows),...  18.5 us
    ppermute x11, starting transfers between devices, shift(): lax.ppermute(array, axis, [(i, (i + by) % size) for i in range(size)])  17.1 us
    pallas_call x1, Pallas kernels, attend_all(): pl.pallas_call(attend_kernel, out_shape=jax.ShapeDtypeStruct((ROWS, QD),...  14.7 us
    ppermute x11, waiting for transfers between devices, shift(): lax.ppermute(array, axis, [(i, (i + by) % size) for i in range(size)])  7.57 us
    pallas_call x1, Pallas kernels, join_weights(): pl.pallas_call(join_kernel, out_shape=jax.ShapeDtypeStruct((2 * own_w.sha...  6.3 us
    unnamed x35, local copies, waits for them, and re-layouts  6.14 us
  transfers between devices with their start and end apart: 25, of which 10 were waited for; matrix products, arithmetic and copies ran while one was open for 8% of the time, Pallas kernels for 22%

profile of v3, /device:TPU:1, one launch (start us, length us, event | category | flops | bytes accessed | tf_op | source)
XLA Modules:
  0.0 136.6 jit_solution(18391291149970345108)
XLA Ops:
  0.0 3.2 %collective-permute-start = (bf16[64,5120]{1,0:T(8,128)(2,1)}, bf16[64,5120]{1,0:T(8,128)(2,1)S(1)}, u32[]{:S(2)}, u32[]{:S(2)}) collective-permute-start(bf16[64,5120]{1,0:T(8,128)(2,1)} %bitcast.24), channel_id=1, source_target_pairs={{0,1},{1,0},{2,3},{3,2},{4,5},{5,4},{6,7},{7,6},{8,9},{9,8},{10,11... | collective-permute-start | bytes 1966088 | tf_op jit(solution)/shard_map/ppermute | solution.py:332
  3.9 1.3 collective-permute-done.mate_ref
  6.0 5.0 %shard_map.109 = (bf16[128,5120]{1,0:T(8,128)(2,1)}, bf16[320,2560]{1,0:T(8,128)(2,1)}, bf16[512,1024]{1,0:T(8,128)(2,1)}) custom-call(s32[6]{0:T(128)} %stack.27.place_ref.refs_0_.refs_3_, s32[8]{0:T(128)} %bitcast.31, s32[1,16]{1,0:T(1,128)} %slots_ref.3, f32[1,5120]{1,0:T(1,128)} %bitcast.26, bf16[64,5120]{1,0:T(8,128)(2,1)} %bitcast.25, ...), custom_call_target="tpu_custom_call" | custom-call | flops 167772160 | bytes 8388608 | tf_op jit(solution)/shard_map/pallas_call | solution.py:63
  11.5 1.0 collective-permute-start.3
  12.5 5.6 %collective-permute-start.2 = (bf16[128,5120]{1,0:T(8,128)(2,1)}, bf16[128,5120]{1,0:T(8,128)(2,1)}, u32[]{:S(2)}, u32[]{:S(2)}) collective-permute-start(bf16[128,5120]{1,0:T(8,128)(2,1)} %get-tuple-element.43.refs_1_), channel_id=1, source_target_pairs={{0,16},{1,113},{16,32},{17,1},{32,48},{33,17},{48,64},{49,33},{64,... | collective-permute-start | bytes 3932168 | tf_op jit(solution)/shard_map/ppermute | solution.py:340
  18.1 2.5 %collective-permute-start.4 = (bf16[512,1024]{1,0:T(8,128)(2,1)}, bf16[512,1024]{1,0:T(8,128)(2,1)}, u32[]{:S(2)}, u32[]{:S(2)}) collective-permute-start(bf16[512,1024]{1,0:T(8,128)(2,1)} %get-tuple-element.52.refs_8_), channel_id=1, source_target_pairs={{0,2},{1,7},{2,4},{3,1},{4,6},{5,3},{6,0},{7,5},{8,10},{9,15},{10,... | collective-permute-start | bytes 3145736 | tf_op jit(solution)/shard_map/ppermute | solution.py:340
  20.6 12.1 %collective-permute-done.4.refs_9_ = bf16[512,1024]{1,0:T(8,128)(2,1)} collective-permute-done((bf16[512,1024]{1,0:T(8,128)(2,1)}, bf16[512,1024]{1,0:T(8,128)(2,1)}, u32[]{:S(2)}, u32[]{:S(2)}) %collective-permute-start.4) | collective-permute-done | bytes 1048608 | tf_op jit(solution)/shard_map/ppermute | solution.py:340
  33.3 3.5 %collective-permute-start.6 = (bf16[128,5120]{1,0:T(8,128)(2,1)}, bf16[128,5120]{1,0:T(8,128)(2,1)}, u32[]{:S(2)}, u32[]{:S(2)}) collective-permute-start(bf16[128,5120]{1,0:T(8,128)(2,1)} %collective-permute-done.2.refs_2_), channel_id=1, source_target_pairs={{0,16},{1,113},{16,32},{17,1},{32,48},{33,17},{48,64},{49,33},{64,... | collective-permute-start | bytes 3932168 | tf_op jit(solution)/shard_map/ppermute | solution.py:340
  36.9 2.5 %collective-permute-start.7 = (bf16[512,1024]{1,0:T(8,128)(2,1)}, bf16[512,1024]{1,0:T(8,128)(2,1)}, u32[]{:S(2)}, u32[]{:S(2)}) collective-permute-start(bf16[512,1024]{1,0:T(8,128)(2,1)} %collective-permute-done.4.refs_9_), channel_id=1, source_target_pairs={{0,2},{1,7},{2,4},{3,1},{4,6},{5,3},{6,0},{7,5},{8,10},{9,15},{10,... | collective-permute-start | bytes 3145736 | tf_op jit(solution)/shard_map/ppermute | solution.py:340
  39.4 1.9 %slice.6 = bf16[256,1024]{1,0:T(8,128)(2,1)} slice(bf16[512,1024]{1,0:T(8,128)(2,1)} %get-tuple-element.52.refs_8_), slice={[0:256], [0:1024]} | slice | bytes 1048576 | tf_op jit(solution)/shard_map/slice | solution.py:387
  41.2 2.8 %collective-permute-start.9 = (bf16[256,1024]{1,0:T(8,128)(2,1)}, bf16[256,1024]{1,0:T(8,128)(2,1)}, u32[]{:S(2)}, u32[]{:S(2)}) collective-permute-start(bf16[256,1024]{1,0:T(8,128)(2,1)} %slice.6), channel_id=1, source_target_pairs={{0,8},{8,0},{1,9},{9,1},{2,10},{10,2},{3,11},{11,3},{4,12},{12,4},... | collective-permute-start | bytes 1572872 | tf_op jit(solution)/shard_map/ppermute | solution.py:332
  44.1 6.3 %shard_map.110.refs_3_.refs_2_ = bf16[640,5120]{1,0:T(8,128)(2,1)} custom-call(s32[6]{0:T(128)} %stack.27.place_ref.refs_0_.refs_3_, bf16[320,5120]{1,0:T(8,128)(2,1)} %bitcast.20, bf16[320,2560]{1,0:T(8,128)(2,1)} %copy-done.1, bf16[320,2560]{1,0:T(8,128)(2,1)} %collective-permute-done.8.far), custom_call_target="tpu_custom_call" | custom-call | bytes 13107200 | tf_op jit(solution)/shard_map/pallas_call | solution.py:132
  50.5 6.5 %shard_map.111 = (bf16[64,640]{1,0:T(8,128)(2,1)}, bf16[128,640]{1,0:T(8,128)(2,1)}) custom-call(s32[6]{0:T(128)} %stack.27.place_ref.refs_0_.refs_3_, bf16[128,5120]{1,0:T(8,128)(2,1)} %get-tuple-element.43.refs_1_, bf16[128,5120]{1,0:T(8,128)(2,1)} %collective-permute-done.2.refs_2_, bf16[640,5120]{1,0:T(8,128)(2,1)} %shard_map.110.refs_3_.refs_2_), custom_call_target="tpu_custom_call" | custom-call | flops 1258291200 | bytes 8519680 | tf_op jit(solution)/shard_map/pallas_call | solution.py:171
  60.6 1.4 %collective-permute-start.12 = (bf16[256,1024]{1,0:T(8,128)(2,1)}, bf16[256,1024]{1,0:T(8,128)(2,1)S(1)}, u32[]{:S(2)}, u32[]{:S(2)}) collective-permute-start(bf16[256,1024]{1,0:T(8,128)(2,1)} %slice.7), channel_id=1, source_target_pairs={{0,8},{8,0},{1,9},{9,1},{2,10},{10,2},{3,11},{11,3},{4,12},{12,4},... | collective-permute-start | bytes 1572872 | tf_op jit(solution)/shard_map/ppermute | solution.py:332
  62.0 2.3 %collective-permute-start.16 = (bf16[512,1024]{1,0:T(8,128)(2,1)}, bf16[512,1024]{1,0:T(8,128)(2,1)}, u32[]{:S(2)}, u32[]{:S(2)}) collective-permute-start(bf16[512,1024]{1,0:T(8,128)(2,1)} %collective-permute-done.7.refs_11_), channel_id=1, source_target_pairs={{0,8},{8,0},{1,9},{9,1},{2,10},{10,2},{3,11},{11,3},{4,12},{12,4},... | collective-permute-start | bytes 3145736 | tf_op jit(solution)/shard_map/ppermute | solution.py:332
  64.3 5.8 %shard_map.112 = bf16[128,640]{1,0:T(8,128)(2,1)} custom-call(s32[6]{0:T(128)} %stack.27.place_ref.refs_0_.refs_3_, bf16[128,5120]{1,0:T(8,128)(2,1)} %collective-permute-done.6.refs_1_, bf16[640,5120]{1,0:T(8,128)(2,1)} %shard_map.110.refs_3_.refs_2_), custom_call_target="tpu_custom_call" | custom-call | flops 838860800 | bytes 7864320 | tf_op jit(solution)/shard_map/pallas_call | solution.py:171
  71.1 1.9 %constant_dynamic-update-slice_fusion.1 = bf16[512,1024]{1,0:T(8,128)(2,1)} fusion(bf16[256,1024]{1,0:T(8,128)(2,1)} %collective-permute-done.9), kind=kLoop, calls=%fused_computation.11 | loop fusion | bytes 1048576
  73.0 3.4 %collective-permute-done.12 = bf16[256,1024]{1,0:T(8,128)(2,1)S(1)} collective-permute-done((bf16[256,1024]{1,0:T(8,128)(2,1)}, bf16[256,1024]{1,0:T(8,128)(2,1)S(1)}, u32[]{:S(2)}, u32[]{:S(2)}) %collective-permute-start.12) | collective-permute-done | bytes 524320 | tf_op jit(solution)/shard_map/ppermute | solution.py:332
  77.2 1.1 constant_dynamic-slice_fusion
  79.0 1.9 %constant_dynamic-update-slice_fusion.refs_12_ = bf16[512,1024]{1,0:T(8,128)(2,1)} fusion(bf16[512,1024]{1,0:T(8,128)(2,1)} %constant_dynamic-update-slice_fusion.1, bf16[256,1024]{1,0:T(8,128)(2,1)} %copy-done.5), kind=kLoop, calls=%fused_computation.10 | loop fusion | bytes 1048576 | tf_op jit(solution)/shard_map/concatenate | solution.py:419
  80.9 2.8 %collective-permute-start.14 = (bf16[512,1024]{1,0:T(8,128)(2,1)}, bf16[512,1024]{1,0:T(8,128)(2,1)S(1)}, u32[]{:S(2)}, u32[]{:S(2)}) collective-permute-start(bf16[512,1024]{1,0:T(8,128)(2,1)} %constant_dynamic-update-slice_fusion.refs_12_), channel_id=1, source_target_pairs={{0,2},{1,7},{2,4},{3,1},{4,6},{5,3},{6,0},{7,5},{8,10},{9,15},{10,... | collective-permute-start | bytes 3145736 | tf_op jit(solution)/shard_map/ppermute | solution.py:340
  83.7 1.3 collective-permute-start.21
  85.0 3.3 %collective-permute-done.17.refs_2_ = bf16[64,5120]{1,0:T(8,128)(2,1)S(1)} collective-permute-done((bf16[64,5120]{1,0:T(8,128)(2,1)S(1)}, bf16[64,5120]{1,0:T(8,128)(2,1)S(1)}, u32[]{:S(2)}, u32[]{:S(2)}) %collective-permute-start.17) | collective-permute-done | bytes 655392 | tf_op jit(solution)/shard_map/ppermute | solution.py:340
  88.2 0.8 copy-done.3
  89.1 6.2 %shard_map.113 = (bf16[128,640]{1,0:T(8,128)(2,1)}, bf16[64,640]{1,0:T(8,128)(2,1)}) custom-call(s32[6]{0:T(128)} %stack.27.place_ref.refs_0_.refs_3_, bf16[128,5120]{1,0:T(8,128)(2,1)} %collective-permute-done.10.refs_1_, bf16[64,5120]{1,0:T(8,128)(2,1)} %copy-done.3, bf16[640,5120]{1,0:T(8,128)(2,1)} %shard_map.110.refs_3_.refs_2_), custom_call_target="tpu_custom_call" | custom-call | flops 1258291200 | bytes 8519680 | tf_op jit(solution)/shard_map/pallas_call | solution.py:171
  95.3 4.7 %collective-permute-start.19 = (bf16[64,640]{1,0:T(8,128)(2,1)}, bf16[64,640]{1,0:T(8,128)(2,1)}, u32[]{:S(2)}, u32[]{:S(2)}) collective-permute-start(bf16[64,640]{1,0:T(8,128)(2,1)} %get-tuple-element.70), channel_id=1, source_target_pairs={{0,64},{1,65},{16,80},{17,81},{32,96},{33,97},{48,112},{49,113},{6... | collective-permute-start | bytes 245768 | tf_op jit(solution)/shard_map/ppermute | solution.py:340
  100.0 8.1 %collective-permute-done.19.refs_19_ = bf16[64,640]{1,0:T(8,128)(2,1)} collective-permute-done((bf16[64,640]{1,0:T(8,128)(2,1)}, bf16[64,640]{1,0:T(8,128)(2,1)}, u32[]{:S(2)}, u32[]{:S(2)}) %collective-permute-start.19) | collective-permute-done | bytes 81952 | tf_op jit(solution)/shard_map/ppermute | solution.py:340
  108.2 4.5 %collective-permute-start.20 = (bf16[128,640]{1,0:T(8,128)(2,1)S(1)}, bf16[128,640]{1,0:T(8,128)(2,1)S(1)}, u32[]{:S(2)}, u32[]{:S(2)}) collective-permute-start(bf16[128,640]{1,0:T(8,128)(2,1)S(1)} %collective-permute-done.13.refs_20_), channel_id=1, source_target_pairs={{0,1},{1,0},{2,3},{3,2},{4,5},{5,4},{6,7},{7,6},{8,9},{9,8},{10,11... | collective-permute-start | bytes 491528 | tf_op jit(solution)/shard_map/ppermute | solution.py:332
  115.3 14.7 %shard_map.114.kept_ref = bf16[64,4096]{1,0:T(8,128)(2,1)} custom-call(s32[8]{0:T(128)} %get-tuple-element.57.refs_0_, s32[8]{0:T(128)} %copy-done.14, s32[16]{0:T(128)} %reshape.159.refs_2_, s32[6]{0:T(128)} %stack.27.place_ref.refs_0_.refs_3_, f32[64,128]{1,0:T(8,128)} %get-tuple-element.60.refs_4_, f32[64,128]{1,0:T(8,128)} %get-tuple-element.61.refs_5_, ...), custom_call_target="tpu_custom_call" | custom-call | flops 687865856 | bytes 13631488 | tf_op jit(solution)/shard_map/pallas_call | solution.py:309
  130.0 1.5 %collective-permute-start.24 = (bf16[64,4096]{1,0:T(8,128)(2,1)}, bf16[64,4096]{1,0:T(8,128)(2,1)S(1)}, u32[]{:S(2)}, u32[]{:S(2)}) collective-permute-start(bf16[64,4096]{1,0:T(8,128)(2,1)} %shard_map.114.kept_ref), channel_id=1, source_target_pairs={{0,1},{1,0},{2,3},{3,2},{4,5},{5,4},{6,7},{7,6},{8,9},{9,8},{10,11... | collective-permute-start | bytes 1572872 | tf_op jit(solution)/shard_map/ppermute | solution.py:332
  131.5 1.7 %collective-permute-done.24.got_ref = bf16[64,4096]{1,0:T(8,128)(2,1)S(1)} collective-permute-done((bf16[64,4096]{1,0:T(8,128)(2,1)}, bf16[64,4096]{1,0:T(8,128)(2,1)S(1)}, u32[]{:S(2)}, u32[]{:S(2)}) %collective-permute-start.24) | collective-permute-done | bytes 524320 | tf_op jit(solution)/shard_map/ppermute | solution.py:332
  134.1 2.6 %shard_map.115 = bf16[64,4096]{1,0:T(8,128)(2,1)} custom-call(s32[6]{0:T(128)} %stack.27.place_ref.refs_0_.refs_3_, s32[1,16]{1,0:T(1,128)} %slots_ref.3, bf16[64,4096]{1,0:T(8,128)(2,1)} %shard_map.114.kept_ref, bf16[64,4096]{1,0:T(8,128)(2,1)} %copy-done.6), custom_call_target="tpu_custom_call" | custom-call | flops 67108864 | bytes 1048576 | tf_op jit(solution)/shard_map/pallas_call | solution.py:94
  (79 shorter events, 12.1 us)
Async XLA Ops:
  0.0 5.2 %collective-permute-start = (bf16[64,5120]{1,0:T(8,128)(2,1)}, bf16[64,5120]{1,0:T(8,128)(2,1)S(1)}, u32[]{:S(2)}, u32[]{:S(2)}) collective-permute-start(bf16[64,5120]{1,0:T(8,128)(2,1)} %bitcast.24), channel_id=1, source_target_pairs={{0,1},{1,0},{2,3},{3,2},{4,5},{5,4},{6,7},{7,6},{8,9},{9,8},{10,11... | collective-permute-start | bytes 1966088 | tf_op jit(solution)/shard_map/ppermute | solution.py:332
  3.2 7.8 %collective-permute-start.1 = (s32[16,1]{0,1:T(1,128)}, s32[16,1]{0,1:T(1,128)S(1)}, u32[]{:S(2)}, u32[]{:S(2)}) collective-permute-start(s32[16,1]{0,1:T(1,128)} %param.21), channel_id=1, source_target_pairs={{0,1},{1,0},{2,3},{3,2},{4,5},{5,4},{6,7},{7,6},{8,9},{9,8},{10,11... | collective-permute-start | bytes 200 | tf_op jit(solution)/shard_map/ppermute | solution.py:332
  6.0 38.1 %copy-start.15 = (s32[16,1]{0,1:T(1,128)S(1)}, s32[16,1]{0,1:T(1,128)}, u32[]{:S(2)}) copy-start(s32[16,1]{0,1:T(1,128)} %param.21) | copy-start | bytes 196
  11.0 21.9 %collective-permute-start.5 = (bf16[16,128,1024]{2,1,0:T(8,128)(2,1)}, bf16[16,128,1024]{2,1,0:T(8,128)(2,1)}, u32[]{:S(2)}, u32[]{:S(2)}) collective-permute-start(bf16[16,128,1024]{2,1,0:T(8,128)(2,1)} %bitcast.21), channel_id=1, source_target_pairs={{0,1},{1,0},{2,3},{3,2},{4,5},{5,4},{6,7},{7,6},{8,9},{9,8},{10,11... | collective-permute-start | bytes 12582920 | tf_op jit(solution)/shard_map/ppermute | solution.py:332
  11.5 21.4 %collective-permute-start.3 = (bf16[320,2560]{1,0:T(8,128)(2,1)}, bf16[320,2560]{1,0:T(8,128)(2,1)S(1)}, u32[]{:S(2)}, u32[]{:S(2)}) collective-permute-start(bf16[320,2560]{1,0:T(8,128)(2,1)} %get-tuple-element.44), channel_id=1, source_target_pairs={{0,128},{1,137},{8,136},{9,129},{128,0},{129,9},{136,8},{137,1},{2... | collective-permute-start | bytes 4915208 | tf_op jit(solution)/shard_map/ppermute | solution.py:349
  12.5 20.4 %collective-permute-start.2 = (bf16[128,5120]{1,0:T(8,128)(2,1)}, bf16[128,5120]{1,0:T(8,128)(2,1)}, u32[]{:S(2)}, u32[]{:S(2)}) collective-permute-start(bf16[128,5120]{1,0:T(8,128)(2,1)} %get-tuple-element.43.refs_1_), channel_id=1, source_target_pairs={{0,16},{1,113},{16,32},{17,1},{32,48},{33,17},{48,64},{49,33},{64,... | collective-permute-start | bytes 3932168 | tf_op jit(solution)/shard_map/ppermute | solution.py:340
  18.1 14.5 %collective-permute-start.4 = (bf16[512,1024]{1,0:T(8,128)(2,1)}, bf16[512,1024]{1,0:T(8,128)(2,1)}, u32[]{:S(2)}, u32[]{:S(2)}) collective-permute-start(bf16[512,1024]{1,0:T(8,128)(2,1)} %get-tuple-element.52.refs_8_), channel_id=1, source_target_pairs={{0,2},{1,7},{2,4},{3,1},{4,6},{5,3},{6,0},{7,5},{8,10},{9,15},{10,... | collective-permute-start | bytes 3145736 | tf_op jit(solution)/shard_map/ppermute | solution.py:340
  32.9 11.2 %copy-start.1 = (bf16[320,2560]{1,0:T(8,128)(2,1)}, bf16[320,2560]{1,0:T(8,128)(2,1)S(1)}, u32[]{:S(2)}) copy-start(bf16[320,2560]{1,0:T(8,128)(2,1)S(1)} %collective-permute-done.3.near) | copy-start | bytes 4915204
  32.9 11.2 %collective-permute-start.8 = (bf16[320,2560]{1,0:T(8,128)(2,1)S(1)}, bf16[320,2560]{1,0:T(8,128)(2,1)}, u32[]{:S(2)}, u32[]{:S(2)}) collective-permute-start(bf16[320,2560]{1,0:T(8,128)(2,1)S(1)} %collective-permute-done.3.near), channel_id=1, source_target_pairs={{0,1},{1,0},{2,3},{3,2},{4,5},{5,4},{6,7},{7,6},{8,9},{9,8},{10,11... | collective-permute-start | bytes 4915208 | tf_op jit(solution)/shard_map/ppermute | solution.py:332
  33.3 23.7 %collective-permute-start.6 = (bf16[128,5120]{1,0:T(8,128)(2,1)}, bf16[128,5120]{1,0:T(8,128)(2,1)}, u32[]{:S(2)}, u32[]{:S(2)}) collective-permute-start(bf16[128,5120]{1,0:T(8,128)(2,1)} %collective-permute-done.2.refs_2_), channel_id=1, source_target_pairs={{0,16},{1,113},{16,32},{17,1},{32,48},{33,17},{48,64},{49,33},{64,... | collective-permute-start | bytes 3932168 | tf_op jit(solution)/shard_map/ppermute | solution.py:340
  36.9 20.1 %collective-permute-start.7 = (bf16[512,1024]{1,0:T(8,128)(2,1)}, bf16[512,1024]{1,0:T(8,128)(2,1)}, u32[]{:S(2)}, u32[]{:S(2)}) collective-permute-start(bf16[512,1024]{1,0:T(8,128)(2,1)} %collective-permute-done.4.refs_9_), channel_id=1, source_target_pairs={{0,2},{1,7},{2,4},{3,1},{4,6},{5,3},{6,0},{7,5},{8,10},{9,15},{10,... | collective-permute-start | bytes 3145736 | tf_op jit(solution)/shard_map/ppermute | solution.py:340
  41.2 15.8 %collective-permute-start.9 = (bf16[256,1024]{1,0:T(8,128)(2,1)}, bf16[256,1024]{1,0:T(8,128)(2,1)}, u32[]{:S(2)}, u32[]{:S(2)}) collective-permute-start(bf16[256,1024]{1,0:T(8,128)(2,1)} %slice.6), channel_id=1, source_target_pairs={{0,8},{8,0},{1,9},{9,1},{2,10},{10,2},{3,11},{11,3},{4,12},{12,4},... | collective-permute-start | bytes 1572872 | tf_op jit(solution)/shard_map/ppermute | solution.py:332
  50.5 7.4 %copy-start = (bf16[512,1024]{1,0:T(8,128)(2,1)S(1)}, bf16[512,1024]{1,0:T(8,128)(2,1)}, u32[]{:S(2)}) copy-start(bf16[512,1024]{1,0:T(8,128)(2,1)} %get-tuple-element.52.refs_8_) | copy-start | bytes 3145732
  50.5 7.4 %copy-start.13 = (s32[1,16]{1,0:T(1,128)S(1)}, s32[1,16]{1,0:T(1,128)}, u32[]{:S(2)}) copy-start(s32[1,16]{1,0:T(1,128)} %slots_ref.3) | copy-start | bytes 196
  50.5 7.4 %copy-start.16 = (s32[1,16]{1,0:T(1,128)S(1)}, s32[1,16]{1,0:T(1,128)}, u32[]{:S(2)}) copy-start(s32[1,16]{1,0:T(1,128)} %param.19) | copy-start | bytes 196
  57.0 19.4 %collective-permute-start.10 = (bf16[128,5120]{1,0:T(8,128)(2,1)}, bf16[128,5120]{1,0:T(8,128)(2,1)}, u32[]{:S(2)}, u32[]{:S(2)}) collective-permute-start(bf16[128,5120]{1,0:T(8,128)(2,1)} %collective-permute-done.6.refs_1_), channel_id=1, source_target_pairs={{0,16},{1,113},{16,32},{17,1},{32,48},{33,17},{48,64},{49,33},{64,... | collective-permute-start | bytes 3932168 | tf_op jit(solution)/shard_map/ppermute | solution.py:340
  57.8 18.6 %collective-permute-start.11 = (bf16[512,1024]{1,0:T(8,128)(2,1)S(1)}, bf16[512,1024]{1,0:T(8,128)(2,1)}, u32[]{:S(2)}, u32[]{:S(2)}) collective-permute-start(bf16[512,1024]{1,0:T(8,128)(2,1)S(1)} %copy-done), channel_id=1, source_target_pairs={{0,6},{1,3},{2,0},{3,5},{4,2},{5,7},{6,4},{7,1},{8,14},{9,11},{10,... | collective-permute-start | bytes 3145736 | tf_op jit(solution)/shard_map/ppermute | solution.py:340
  60.6 15.7 %collective-permute-start.12 = (bf16[256,1024]{1,0:T(8,128)(2,1)}, bf16[256,1024]{1,0:T(8,128)(2,1)S(1)}, u32[]{:S(2)}, u32[]{:S(2)}) collective-permute-start(bf16[256,1024]{1,0:T(8,128)(2,1)} %slice.7), channel_id=1, source_target_pairs={{0,8},{8,0},{1,9},{9,1},{2,10},{10,2},{3,11},{11,3},{4,12},{12,4},... | collective-permute-start | bytes 1572872 | tf_op jit(solution)/shard_map/ppermute | solution.py:332
  62.0 10.9 %collective-permute-start.13 = (bf16[128,640]{1,0:T(8,128)(2,1)}, bf16[128,640]{1,0:T(8,128)(2,1)S(1)}, u32[]{:S(2)}, u32[]{:S(2)}) collective-permute-start(bf16[128,640]{1,0:T(8,128)(2,1)} %get-tuple-element.54), channel_id=1, source_target_pairs={{0,112},{1,17},{16,0},{17,33},{32,16},{33,49},{48,32},{49,65},{64,... | collective-permute-start | bytes 491528 | tf_op jit(solution)/shard_map/ppermute | solution.py:340
  62.0 50.7 %collective-permute-start.16 = (bf16[512,1024]{1,0:T(8,128)(2,1)}, bf16[512,1024]{1,0:T(8,128)(2,1)}, u32[]{:S(2)}, u32[]{:S(2)}) collective-permute-start(bf16[512,1024]{1,0:T(8,128)(2,1)} %collective-permute-done.7.refs_11_), channel_id=1, source_target_pairs={{0,8},{8,0},{1,9},{9,1},{2,10},{10,2},{3,11},{11,3},{4,12},{12,4},... | collective-permute-start | bytes 3145736 | tf_op jit(solution)/shard_map/ppermute | solution.py:332
  73.0 35.2 %copy-start.7 = (bf16[128,640]{1,0:T(8,128)(2,1)}, bf16[128,640]{1,0:T(8,128)(2,1)S(1)}, u32[]{:S(2)}) copy-start(bf16[128,640]{1,0:T(8,128)(2,1)S(1)} %collective-permute-done.13.refs_20_) | copy-start | bytes 491524
  78.3 9.9 %collective-permute-start.17 = (bf16[64,5120]{1,0:T(8,128)(2,1)S(1)}, bf16[64,5120]{1,0:T(8,128)(2,1)S(1)}, u32[]{:S(2)}, u32[]{:S(2)}) collective-permute-start(bf16[64,5120]{1,0:T(8,128)(2,1)S(1)} %constant_dynamic-slice_fusion), channel_id=1, source_target_pairs={{0,16},{1,113},{16,32},{17,1},{32,48},{33,17},{48,64},{49,33},{64,... | collective-permute-start | bytes 1966088 | tf_op jit(solution)/shard_map/ppermute | solution.py:340
  80.9 33.4 %collective-permute-start.14 = (bf16[512,1024]{1,0:T(8,128)(2,1)}, bf16[512,1024]{1,0:T(8,128)(2,1)S(1)}, u32[]{:S(2)}, u32[]{:S(2)}) collective-permute-start(bf16[512,1024]{1,0:T(8,128)(2,1)} %constant_dynamic-update-slice_fusion.refs_12_), channel_id=1, source_target_pairs={{0,2},{1,7},{2,4},{3,1},{4,6},{5,3},{6,0},{7,5},{8,10},{9,15},{10,... | collective-permute-start | bytes 3145736 | tf_op jit(solution)/shard_map/ppermute | solution.py:340
  83.7 30.6 %collective-permute-start.15 = (bf16[512,1024]{1,0:T(8,128)(2,1)}, bf16[512,1024]{1,0:T(8,128)(2,1)}, u32[]{:S(2)}, u32[]{:S(2)}) collective-permute-start(bf16[512,1024]{1,0:T(8,128)(2,1)} %constant_dynamic-update-slice_fusion.refs_12_), channel_id=1, source_target_pairs={{0,6},{1,3},{2,0},{3,5},{4,2},{5,7},{6,4},{7,1},{8,14},{9,11},{10,... | collective-permute-start | bytes 3145736 | tf_op jit(solution)/shard_map/ppermute | solution.py:340
  83.7 11.6 %collective-permute-start.21 = (bf16[128,640]{1,0:T(8,128)(2,1)}, bf16[128,640]{1,0:T(8,128)(2,1)S(1)}, u32[]{:S(2)}, u32[]{:S(2)}) collective-permute-start(bf16[128,640]{1,0:T(8,128)(2,1)} %shard_map.112), channel_id=1, source_target_pairs={{0,96},{1,33},{16,112},{17,49},{32,0},{33,65},{48,16},{49,81},{64,... | collective-permute-start | bytes 491528 | tf_op jit(solution)/shard_map/ppermute | solution.py:340
  95.3 17.4 %collective-permute-start.18 = (bf16[128,640]{1,0:T(8,128)(2,1)}, bf16[128,640]{1,0:T(8,128)(2,1)S(1)}, u32[]{:S(2)}, u32[]{:S(2)}) collective-permute-start(bf16[128,640]{1,0:T(8,128)(2,1)} %get-tuple-element.69), channel_id=1, source_target_pairs={{0,80},{1,49},{16,96},{17,65},{32,112},{33,81},{48,0},{49,97},{64,... | collective-permute-start | bytes 491528 | tf_op jit(solution)/shard_map/ppermute | solution.py:340
  95.3 19.0 %copy-start.8 = (bf16[128,640]{1,0:T(8,128)(2,1)}, bf16[128,640]{1,0:T(8,128)(2,1)S(1)}, u32[]{:S(2)}) copy-start(bf16[128,640]{1,0:T(8,128)(2,1)S(1)} %collective-permute-done.21.refs_22_) | copy-start | bytes 491524
  95.3 12.8 %collective-permute-start.19 = (bf16[64,640]{1,0:T(8,128)(2,1)}, bf16[64,640]{1,0:T(8,128)(2,1)}, u32[]{:S(2)}, u32[]{:S(2)}) collective-permute-start(bf16[64,640]{1,0:T(8,128)(2,1)} %get-tuple-element.70), channel_id=1, source_target_pairs={{0,64},{1,65},{16,80},{17,81},{32,96},{33,97},{48,112},{49,113},{6... | collective-permute-start | bytes 245768 | tf_op jit(solution)/shard_map/ppermute | solution.py:340
  108.2 5.5 %collective-permute-start.20 = (bf16[128,640]{1,0:T(8,128)(2,1)S(1)}, bf16[128,640]{1,0:T(8,128)(2,1)S(1)}, u32[]{:S(2)}, u32[]{:S(2)}) collective-permute-start(bf16[128,640]{1,0:T(8,128)(2,1)S(1)} %collective-permute-done.13.refs_20_), channel_id=1, source_target_pairs={{0,1},{1,0},{2,3},{3,2},{4,5},{5,4},{6,7},{7,6},{8,9},{9,8},{10,11... | collective-permute-start | bytes 491528 | tf_op jit(solution)/shard_map/ppermute | solution.py:332
  112.6 1.4 %collective-permute-start.22 = (bf16[128,640]{1,0:T(8,128)(2,1)S(1)}, bf16[128,640]{1,0:T(8,128)(2,1)S(1)}, u32[]{:S(2)}, u32[]{:S(2)}) collective-permute-start(bf16[128,640]{1,0:T(8,128)(2,1)S(1)} %collective-permute-done.21.refs_22_), channel_id=1, source_target_pairs={{0,1},{1,0},{2,3},{3,2},{4,5},{5,4},{6,7},{7,6},{8,9},{9,8},{10,11... | collective-permute-start | bytes 491528 | tf_op jit(solution)/shard_map/ppermute | solution.py:332
  112.7 1.5 %collective-permute-start.23 = (bf16[128,640]{1,0:T(8,128)(2,1)S(1)}, bf16[128,640]{1,0:T(8,128)(2,1)S(1)}, u32[]{:S(2)}, u32[]{:S(2)}) collective-permute-start(bf16[128,640]{1,0:T(8,128)(2,1)S(1)} %collective-permute-done.18.refs_24_), channel_id=1, source_target_pairs={{0,1},{1,0},{2,3},{3,2},{4,5},{5,4},{6,7},{7,6},{8,9},{9,8},{10,11... | collective-permute-start | bytes 491528 | tf_op jit(solution)/shard_map/ppermute | solution.py:332
  130.0 3.3 %collective-permute-start.24 = (bf16[64,4096]{1,0:T(8,128)(2,1)}, bf16[64,4096]{1,0:T(8,128)(2,1)S(1)}, u32[]{:S(2)}, u32[]{:S(2)}) collective-permute-start(bf16[64,4096]{1,0:T(8,128)(2,1)} %shard_map.114.kept_ref), channel_id=1, source_target_pairs={{0,1},{1,0},{2,3},{3,2},{4,5},{5,4},{6,7},{7,6},{8,9},{9,8},{10,11... | collective-permute-start | bytes 1572872 | tf_op jit(solution)/shard_map/ppermute | solution.py:332
  (10 other events, 9.1 us)

commit v4 on v3

--- a/solution.py
+++ b/solution.py
@@ -70,7 +70,7 @@
         in_specs=[smem, smem, vmem, vmem, vmem, vmem, hbm, hbm],
         out_specs=(vmem, vmem, vmem),
         scratch_shapes=[pltpu.SemaphoreType.DMA((9,))],
-        compiler_params=pltpu.CompilerParams(vmem_limit_bytes=62 * 2**20),
+        compiler_params=pltpu.CompilerParams(vmem_limit_bytes=255 * 2**18),
         cost_estimate=pl.CostEstimate(flops=8 * ROWS * ROWS * D, bytes_accessed=8 * 2**20, transcendentals=0),
     )(place, table, slots, gain, mine, mate, weights, pool)
 
@@ -96,7 +96,7 @@
         out_shape=jax.ShapeDtypeStruct((ROWS, QD), jnp.bfloat16),
         in_specs=[pl.BlockSpec(memory_space=pltpu.SMEM), vmem, vmem, vmem],
         out_specs=vmem,
-        compiler_params=pltpu.CompilerParams(vmem_limit_bytes=62 * 2**20),
+        compiler_params=pltpu.CompilerParams(vmem_limit_bytes=255 * 2**18),
         cost_estimate=pl.CostEstimate(flops=4 * ROWS * ROWS * QD, bytes_accessed=4 * ROWS * QD, transcendentals=0),
     )(place, slots, kept, got)
 
@@ -135,7 +135,7 @@
         in_specs=[pl.BlockSpec(memory_space=pltpu.SMEM), hbm, hbm, hbm],
         out_specs=pl.BlockSpec(memory_space=pltpu.VMEM),
         scratch_shapes=[pltpu.SemaphoreType.DMA((6,))],
-        compiler_params=pltpu.CompilerParams(vmem_limit_bytes=62 * 2**20),
+        compiler_params=pltpu.CompilerParams(vmem_limit_bytes=255 * 2**18),
         cost_estimate=pl.CostEstimate(flops=0, bytes_accessed=8 * D * own_w.shape[0], transcendentals=0),
     )(place, own_w, near, far)
 
@@ -179,7 +179,7 @@
             out_specs=[pl.BlockSpec((height, width), lambda step, _: (0, 0)) for height in heights],
             scratch_shapes=[pltpu.VMEM((sum(heights), width), jnp.float32)],
         ),
-        compiler_params=pltpu.CompilerParams(vmem_limit_bytes=62 * 2**20),
+        compiler_params=pltpu.CompilerParams(vmem_limit_bytes=255 * 2**18),
         cost_estimate=pl.CostEstimate(
             flops=2 * sum(heights) * width * D, bytes_accessed=2 * D * (sum(heights) + width), transcendentals=0
         ),
@@ -275,14 +275,19 @@
         share = 1.0 / (jnp.sum(w_p, axis=0, keepdims=True) + jnp.sum(w_r, axis=0, keepdims=True))
         w_p = (w_p * share).astype(jnp.bfloat16)
         w_r = (w_r * share).astype(jnp.bfloat16)
-        mix = lax.dot_general(w_p, kv[j, :, KVD:], down, preferred_element_type=jnp.float32)
-        mix_r = [
-            lax.dot_general(w_r, rkv[2 * j + a, :, KVD:], down, preferred_element_type=jnp.float32) for a in range(2)
-        ]
-        for k in range(KV_HEADS):
-            block = (slice(k * wide, (k + 1) * wide), slice(k * HD, (k + 1) * HD))
-            one = mix[block] + jnp.where(first_row, mix_r[0][block], mix_r[1][block])
-            mixed[k * GROUP : (k + 1) * GROUP, rows, :] = one.reshape(GROUP, 2 * STEPS, HD)
+        for pair in range(2):
+            lanes = slice(pair * 2 * wide, (pair + 1) * 2 * wide)
+            feats = slice(KVD + pair * 2 * HD, KVD + (pair + 1) * 2 * HD)
+            mix = lax.dot_general(w_p[:, lanes], kv[j, :, feats], down, preferred_element_type=jnp.float32)
+            mix_r = [
+                lax.dot_general(w_r[:, lanes], rkv[2 * j + a, :, feats], down, preferred_element_type=jnp.float32)
+                for a in range(2)
+            ]
+            for n in range(2):
+                k = 2 * pair + n
+                block = (slice(n * wide, (n + 1) * wide), slice(n * HD, (n + 1) * HD))
+                one = mix[block] + jnp.where(first_row, mix_r[0][block], mix_r[1][block])
+                mixed[k * GROUP : (k + 1) * GROUP, rows, :] = one.reshape(GROUP, 2 * STEPS, HD)
 
     def some_slots(i, carry):
         for n in range(BATCH):
@@ -321,7 +326,7 @@
             pltpu.SemaphoreType.DMA((HELD,)),
             pltpu.SemaphoreType.DMA((HELD,)),
         ],
-        compiler_params=pltpu.CompilerParams(vmem_limit_bytes=62 * 2**20),
+        compiler_params=pltpu.CompilerParams(vmem_limit_bytes=255 * 2**18),
         cost_estimate=pl.CostEstimate(
             flops=4 * ROWS * QD * (PLEN + RK), bytes_accessed=13 * 2**20, transcendentals=ROWS * HEADS * (PLEN + RK)
         ),

time: 139 us -> 137 us (0.986)
  local copies, waits for them, and re-layouts: 13.5 us -> 12 us
    unnamed x35 -> x21, local copies, waits for them, and re-layouts: 6.14 us -> 3.81 us
  transfers between devices with their start and end apart: 25 -> 25, of which waited for: 10 -> 9; matrix products, arithmetic and copies ran while one was open for 8% -> 9% of each run, Pallas kernels for 22% -> 22%
where the time goes in v4:
time: 137 us; the launch traced here: 134 us
  Pallas kernels  45.8 us (33%)
  starting transfers between devices  43.5 us (32%)
  waiting for transfers between devices  30.9 us (23%)
  local copies, waits for them, and re-layouts  12 us (9%)
  other arithmetic  1.95 us (1%)
    ppermute x13, starting transfers between devices, turn(): return lax.ppermute(array, (axis, 'c'), pairs)  24.4 us
    ppermute x13, waiting for transfers between devices, turn(): return lax.ppermute(array, (axis, 'c'), pairs)  23 us
    pallas_call x3, Pallas kernels, project(): pl.pallas_call(functools.partial(project_kernel, len(arrays), own_rows),...  18.5 us
    ppermute x11, starting transfers between devices, shift(): lax.ppermute(array, axis, [(i, (i + by) % size) for i in range(size)])  18.2 us
    pallas_call x1, Pallas kernels, attend_all(): pl.pallas_call(attend_kernel, out_shape=jax.ShapeDtypeStruct((ROWS, QD),...  13.4 us
    ppermute x11, waiting for transfers between devices, shift(): lax.ppermute(array, axis, [(i, (i + by) % size) for i in range(size)])  7.86 us
    pallas_call x1, Pallas kernels, join_weights(): pl.pallas_call(join_kernel, out_shape=jax.ShapeDtypeStruct((2 * own_w.sha...  6.27 us
    pallas_call x1, Pallas kernels, prepare(): pl.pallas_call(prepare_kernel, out_shape=(jax.ShapeDtypeStruct((2 * ROWS,...  5.06 us
  transfers between devices with their start and end apart: 25, of which 9 were waited for; matrix products, arithmetic and copies ran while one was open for 9% of the time, Pallas kernels for 22%

profile of v4, /device:TPU:1, one launch (start us, length us, event | category | flops | bytes accessed | tf_op | source)
XLA Modules:
  0.0 134.3 jit_solution(145640652926631395)
XLA Ops:
  0.0 3.2 %collective-permute-start = (bf16[64,5120]{1,0:T(8,128)(2,1)}, bf16[64,5120]{1,0:T(8,128)(2,1)}, u32[]{:S(2)}, u32[]{:S(2)}) collective-permute-start(bf16[64,5120]{1,0:T(8,128)(2,1)} %bitcast.24), channel_id=1, source_target_pairs={{0,1},{1,0},{2,3},{3,2},{4,5},{5,4},{6,7},{7,6},{8,9},{9,8},{10,11... | collective-permute-start | bytes 1966088 | tf_op jit(solution)/shard_map/ppermute | solution.py:337
  3.8 1.5 %collective-permute-done.mate_ref = bf16[64,5120]{1,0:T(8,128)(2,1)} collective-permute-done((bf16[64,5120]{1,0:T(8,128)(2,1)}, bf16[64,5120]{1,0:T(8,128)(2,1)}, u32[]{:S(2)}, u32[]{:S(2)}) %collective-permute-start) | collective-permute-done | bytes 655392 | tf_op jit(solution)/shard_map/ppermute | solution.py:337
  5.3 5.1 %shard_map.109 = (bf16[128,5120]{1,0:T(8,128)(2,1)}, bf16[320,2560]{1,0:T(8,128)(2,1)}, bf16[512,1024]{1,0:T(8,128)(2,1)}) custom-call(s32[6]{0:T(128)} %stack.27.place_ref.refs_0_.refs_3_, s32[8]{0:T(128)} %bitcast.31, s32[1,16]{1,0:T(1,128)} %slots_ref.3, f32[1,5120]{1,0:T(1,128)} %bitcast.26, bf16[64,5120]{1,0:T(8,128)(2,1)} %bitcast.25, ...), custom_call_target="tpu_custom_call" | custom-call | flops 167772160 | bytes 8388608 | tf_op jit(solution)/shard_map/pallas_call | solution.py:63
  11.9 5.6 %collective-permute-start.2 = (bf16[128,5120]{1,0:T(8,128)(2,1)}, bf16[128,5120]{1,0:T(8,128)(2,1)}, u32[]{:S(2)}, u32[]{:S(2)}) collective-permute-start(bf16[128,5120]{1,0:T(8,128)(2,1)} %get-tuple-element.43.refs_1_), channel_id=1, source_target_pairs={{0,16},{1,113},{16,32},{17,1},{32,48},{33,17},{48,64},{49,33},{64,... | collective-permute-start | bytes 3932168 | tf_op jit(solution)/shard_map/ppermute | solution.py:345
  17.4 2.5 %collective-permute-start.4 = (bf16[512,1024]{1,0:T(8,128)(2,1)}, bf16[512,1024]{1,0:T(8,128)(2,1)}, u32[]{:S(2)}, u32[]{:S(2)}) collective-permute-start(bf16[512,1024]{1,0:T(8,128)(2,1)} %get-tuple-element.52.refs_8_), channel_id=1, source_target_pairs={{0,2},{1,7},{2,4},{3,1},{4,6},{5,3},{6,0},{7,5},{8,10},{9,15},{10,... | collective-permute-start | bytes 3145736 | tf_op jit(solution)/shard_map/ppermute | solution.py:345
  19.9 12.1 %collective-permute-done.4.refs_9_ = bf16[512,1024]{1,0:T(8,128)(2,1)} collective-permute-done((bf16[512,1024]{1,0:T(8,128)(2,1)}, bf16[512,1024]{1,0:T(8,128)(2,1)}, u32[]{:S(2)}, u32[]{:S(2)}) %collective-permute-start.4) | collective-permute-done | bytes 1048608 | tf_op jit(solution)/shard_map/ppermute | solution.py:345
  32.3 1.2 copy-done
  33.7 3.6 %collective-permute-start.6 = (bf16[128,5120]{1,0:T(8,128)(2,1)}, bf16[128,5120]{1,0:T(8,128)(2,1)}, u32[]{:S(2)}, u32[]{:S(2)}) collective-permute-start(bf16[128,5120]{1,0:T(8,128)(2,1)} %collective-permute-done.2.refs_2_), channel_id=1, source_target_pairs={{0,16},{1,113},{16,32},{17,1},{32,48},{33,17},{48,64},{49,33},{64,... | collective-permute-start | bytes 3932168 | tf_op jit(solution)/shard_map/ppermute | solution.py:345
  37.3 2.5 %collective-permute-start.7 = (bf16[512,1024]{1,0:T(8,128)(2,1)}, bf16[512,1024]{1,0:T(8,128)(2,1)}, u32[]{:S(2)}, u32[]{:S(2)}) collective-permute-start(bf16[512,1024]{1,0:T(8,128)(2,1)} %collective-permute-done.4.refs_9_), channel_id=1, source_target_pairs={{0,2},{1,7},{2,4},{3,1},{4,6},{5,3},{6,0},{7,5},{8,10},{9,15},{10,... | collective-permute-start | bytes 3145736 | tf_op jit(solution)/shard_map/ppermute | solution.py:345
  39.8 1.9 %slice.6 = bf16[256,1024]{1,0:T(8,128)(2,1)} slice(bf16[512,1024]{1,0:T(8,128)(2,1)} %get-tuple-element.52.refs_8_), slice={[0:256], [0:1024]} | slice | bytes 1048576 | tf_op jit(solution)/shard_map/slice | solution.py:392
  41.7 2.9 %collective-permute-start.9 = (bf16[256,1024]{1,0:T(8,128)(2,1)}, bf16[256,1024]{1,0:T(8,128)(2,1)}, u32[]{:S(2)}, u32[]{:S(2)}) collective-permute-start(bf16[256,1024]{1,0:T(8,128)(2,1)} %slice.6), channel_id=1, source_target_pairs={{0,8},{8,0},{1,9},{9,1},{2,10},{10,2},{3,11},{11,3},{4,12},{12,4},... | collective-permute-start | bytes 1572872 | tf_op jit(solution)/shard_map/ppermute | solution.py:337
  44.6 6.3 %shard_map.110.refs_3_.refs_2_ = bf16[640,5120]{1,0:T(8,128)(2,1)} custom-call(s32[6]{0:T(128)} %stack.27.place_ref.refs_0_.refs_3_, bf16[320,5120]{1,0:T(8,128)(2,1)} %bitcast.20, bf16[320,2560]{1,0:T(8,128)(2,1)} %copy-done, bf16[320,2560]{1,0:T(8,128)(2,1)} %collective-permute-done.8.far), custom_call_target="tpu_custom_call" | custom-call | bytes 13107200 | tf_op jit(solution)/shard_map/pallas_call | solution.py:132
  50.9 6.5 %shard_map.111 = (bf16[64,640]{1,0:T(8,128)(2,1)}, bf16[128,640]{1,0:T(8,128)(2,1)}) custom-call(s32[6]{0:T(128)} %stack.27.place_ref.refs_0_.refs_3_, bf16[128,5120]{1,0:T(8,128)(2,1)} %get-tuple-element.43.refs_1_, bf16[128,5120]{1,0:T(8,128)(2,1)} %collective-permute-done.2.refs_2_, bf16[640,5120]{1,0:T(8,128)(2,1)} %shard_map.110.refs_3_.refs_2_), custom_call_target="tpu_custom_call" | custom-call | flops 1258291200 | bytes 8519680 | tf_op jit(solution)/shard_map/pallas_call | solution.py:171
  59.2 1.9 %slice.7 = bf16[256,1024]{1,0:T(8,128)(2,1)} slice(bf16[512,1024]{1,0:T(8,128)(2,1)} %get-tuple-element.52.refs_8_), slice={[256:512], [0:1024]} | slice | bytes 1048576 | tf_op jit(solution)/shard_map/slice | solution.py:399
  62.0 1.3 collective-permute-start.12
  63.3 2.4 %collective-permute-start.16 = (bf16[512,1024]{1,0:T(8,128)(2,1)}, bf16[512,1024]{1,0:T(8,128)(2,1)}, u32[]{:S(2)}, u32[]{:S(2)}) collective-permute-start(bf16[512,1024]{1,0:T(8,128)(2,1)} %collective-permute-done.7.refs_11_), channel_id=1, source_target_pairs={{0,8},{8,0},{1,9},{9,1},{2,10},{10,2},{3,11},{11,3},{4,12},{12,4},... | collective-permute-start | bytes 3145736 | tf_op jit(solution)/shard_map/ppermute | solution.py:337
  65.7 5.8 %shard_map.112 = bf16[128,640]{1,0:T(8,128)(2,1)} custom-call(s32[6]{0:T(128)} %stack.27.place_ref.refs_0_.refs_3_, bf16[128,5120]{1,0:T(8,128)(2,1)} %collective-permute-done.6.refs_1_, bf16[640,5120]{1,0:T(8,128)(2,1)} %shard_map.110.refs_3_.refs_2_), custom_call_target="tpu_custom_call" | custom-call | flops 838860800 | bytes 7864320 | tf_op jit(solution)/shard_map/pallas_call | solution.py:171
  72.5 1.9 %constant_dynamic-update-slice_fusion.1 = bf16[512,1024]{1,0:T(8,128)(2,1)} fusion(bf16[256,1024]{1,0:T(8,128)(2,1)} %collective-permute-done.9), kind=kLoop, calls=%fused_computation.11 | loop fusion | bytes 1048576
  74.4 3.4 %collective-permute-done.12 = bf16[256,1024]{1,0:T(8,128)(2,1)} collective-permute-done((bf16[256,1024]{1,0:T(8,128)(2,1)}, bf16[256,1024]{1,0:T(8,128)(2,1)}, u32[]{:S(2)}, u32[]{:S(2)}) %collective-permute-start.12) | collective-permute-done | bytes 524320 | tf_op jit(solution)/shard_map/ppermute | solution.py:337
  77.8 1.1 constant_dynamic-slice_fusion
  79.5 1.9 %constant_dynamic-update-slice_fusion.refs_12_ = bf16[512,1024]{1,0:T(8,128)(2,1)} fusion(bf16[512,1024]{1,0:T(8,128)(2,1)} %constant_dynamic-update-slice_fusion.1, bf16[256,1024]{1,0:T(8,128)(2,1)} %collective-permute-done.12), kind=kLoop, calls=%fused_computation.10 | loop fusion | bytes 1048576 | tf_op jit(solution)/shard_map/concatenate | solution.py:424
  81.4 2.9 %collective-permute-start.14 = (bf16[512,1024]{1,0:T(8,128)(2,1)}, bf16[512,1024]{1,0:T(8,128)(2,1)}, u32[]{:S(2)}, u32[]{:S(2)}) collective-permute-start(bf16[512,1024]{1,0:T(8,128)(2,1)} %constant_dynamic-update-slice_fusion.refs_12_), channel_id=1, source_target_pairs={{0,2},{1,7},{2,4},{3,1},{4,6},{5,3},{6,0},{7,5},{8,10},{9,15},{10,... | collective-permute-start | bytes 3145736 | tf_op jit(solution)/shard_map/ppermute | solution.py:345
  84.3 1.3 collective-permute-start.21
  85.5 3.3 %collective-permute-done.17.refs_2_ = bf16[64,5120]{1,0:T(8,128)(2,1)} collective-permute-done((bf16[64,5120]{1,0:T(8,128)(2,1)S(1)}, bf16[64,5120]{1,0:T(8,128)(2,1)}, u32[]{:S(2)}, u32[]{:S(2)}) %collective-permute-start.17) | collective-permute-done | bytes 655392 | tf_op jit(solution)/shard_map/ppermute | solution.py:345
  88.8 6.2 %shard_map.113 = (bf16[128,640]{1,0:T(8,128)(2,1)}, bf16[64,640]{1,0:T(8,128)(2,1)}) custom-call(s32[6]{0:T(128)} %stack.27.place_ref.refs_0_.refs_3_, bf16[128,5120]{1,0:T(8,128)(2,1)} %collective-permute-done.10.refs_1_, bf16[64,5120]{1,0:T(8,128)(2,1)} %collective-permute-done.17.refs_2_, bf16[640,5120]{1,0:T(8,128)(2,1)} %shard_map.110.refs_3_.refs_2_), custom_call_target="tpu_custom_call" | custom-call | flops 1258291200 | bytes 8519680 | tf_op jit(solution)/shard_map/pallas_call | solution.py:171
  95.0 4.7 %collective-permute-start.19 = (bf16[64,640]{1,0:T(8,128)(2,1)}, bf16[64,640]{1,0:T(8,128)(2,1)}, u32[]{:S(2)}, u32[]{:S(2)}) collective-permute-start(bf16[64,640]{1,0:T(8,128)(2,1)} %get-tuple-element.70), channel_id=1, source_target_pairs={{0,64},{1,65},{16,80},{17,81},{32,96},{33,97},{48,112},{49,113},{6... | collective-permute-start | bytes 245768 | tf_op jit(solution)/shard_map/ppermute | solution.py:345
  99.7 7.3 %collective-permute-done.19.refs_19_ = bf16[64,640]{1,0:T(8,128)(2,1)} collective-permute-done((bf16[64,640]{1,0:T(8,128)(2,1)}, bf16[64,640]{1,0:T(8,128)(2,1)}, u32[]{:S(2)}, u32[]{:S(2)}) %collective-permute-start.19) | collective-permute-done | bytes 81952 | tf_op jit(solution)/shard_map/ppermute | solution.py:345
  107.1 5.4 %collective-permute-start.20 = (bf16[128,640]{1,0:T(8,128)(2,1)S(1)}, bf16[128,640]{1,0:T(8,128)(2,1)S(1)}, u32[]{:S(2)}, u32[]{:S(2)}) collective-permute-start(bf16[128,640]{1,0:T(8,128)(2,1)S(1)} %collective-permute-done.13.refs_20_), channel_id=1, source_target_pairs={{0,1},{1,0},{2,3},{3,2},{4,5},{5,4},{6,7},{7,6},{8,9},{9,8},{10,11... | collective-permute-start | bytes 491528 | tf_op jit(solution)/shard_map/ppermute | solution.py:337
  114.9 13.4 %shard_map.114.kept_ref = bf16[64,4096]{1,0:T(8,128)(2,1)} custom-call(s32[8]{0:T(128)} %get-tuple-element.57.refs_0_, s32[8]{0:T(128)} %copy-done.7, s32[16]{0:T(128)} %reshape.159.refs_2_, s32[6]{0:T(128)} %stack.27.place_ref.refs_0_.refs_3_, f32[64,128]{1,0:T(8,128)} %get-tuple-element.60.refs_4_, f32[64,128]{1,0:T(8,128)} %get-tuple-element.61.refs_5_, ...), custom_call_target="tpu_custom_call" | custom-call | flops 687865856 | bytes 13631488 | tf_op jit(solution)/shard_map/pallas_call | solution.py:314
  128.3 1.6 %collective-permute-start.24 = (bf16[64,4096]{1,0:T(8,128)(2,1)}, bf16[64,4096]{1,0:T(8,128)(2,1)}, u32[]{:S(2)}, u32[]{:S(2)}) collective-permute-start(bf16[64,4096]{1,0:T(8,128)(2,1)} %shard_map.114.kept_ref), channel_id=1, source_target_pairs={{0,1},{1,0},{2,3},{3,2},{4,5},{5,4},{6,7},{7,6},{8,9},{9,8},{10,11... | collective-permute-start | bytes 1572872 | tf_op jit(solution)/shard_map/ppermute | solution.py:337
  129.9 1.9 %collective-permute-done.24.got_ref = bf16[64,4096]{1,0:T(8,128)(2,1)} collective-permute-done((bf16[64,4096]{1,0:T(8,128)(2,1)}, bf16[64,4096]{1,0:T(8,128)(2,1)}, u32[]{:S(2)}, u32[]{:S(2)}) %collective-permute-start.24) | collective-permute-done | bytes 524320 | tf_op jit(solution)/shard_map/ppermute | solution.py:337
  131.7 2.6 %shard_map.115 = bf16[64,4096]{1,0:T(8,128)(2,1)} custom-call(s32[6]{0:T(128)} %stack.27.place_ref.refs_0_.refs_3_, s32[1,16]{1,0:T(1,128)} %slots_ref.3, bf16[64,4096]{1,0:T(8,128)(2,1)} %shard_map.114.kept_ref, bf16[64,4096]{1,0:T(8,128)(2,1)} %collective-permute-done.24.got_ref), custom_call_target="tpu_custom_call" | custom-call | flops 67108864 | bytes 1048576 | tf_op jit(solution)/shard_map/pallas_call | solution.py:94
  (65 shorter events, 9.3 us)
Async XLA Ops:
  0.0 5.3 %collective-permute-start = (bf16[64,5120]{1,0:T(8,128)(2,1)}, bf16[64,5120]{1,0:T(8,128)(2,1)}, u32[]{:S(2)}, u32[]{:S(2)}) collective-permute-start(bf16[64,5120]{1,0:T(8,128)(2,1)} %bitcast.24), channel_id=1, source_target_pairs={{0,1},{1,0},{2,3},{3,2},{4,5},{5,4},{6,7},{7,6},{8,9},{9,8},{10,11... | collective-permute-start | bytes 1966088 | tf_op jit(solution)/shard_map/ppermute | solution.py:337
  3.2 7.1 %collective-permute-start.1 = (s32[16,1]{0,1:T(1,128)}, s32[16,1]{0,1:T(1,128)S(1)}, u32[]{:S(2)}, u32[]{:S(2)}) collective-permute-start(s32[16,1]{0,1:T(1,128)} %param.21), channel_id=1, source_target_pairs={{0,1},{1,0},{2,3},{3,2},{4,5},{5,4},{6,7},{7,6},{8,9},{9,8},{10,11... | collective-permute-start | bytes 200 | tf_op jit(solution)/shard_map/ppermute | solution.py:337
  5.3 39.3 %copy-start.8 = (s32[16,1]{0,1:T(1,128)S(1)}, s32[16,1]{0,1:T(1,128)}, u32[]{:S(2)}) copy-start(s32[16,1]{0,1:T(1,128)} %param.21) | copy-start | bytes 196
  10.4 21.9 %collective-permute-start.5 = (bf16[16,128,1024]{2,1,0:T(8,128)(2,1)}, bf16[16,128,1024]{2,1,0:T(8,128)(2,1)}, u32[]{:S(2)}, u32[]{:S(2)}) collective-permute-start(bf16[16,128,1024]{2,1,0:T(8,128)(2,1)} %bitcast.21), channel_id=1, source_target_pairs={{0,1},{1,0},{2,3},{3,2},{4,5},{5,4},{6,7},{7,6},{8,9},{9,8},{10,11... | collective-permute-start | bytes 12582920 | tf_op jit(solution)/shard_map/ppermute | solution.py:337
  10.9 21.4 %collective-permute-start.3 = (bf16[320,2560]{1,0:T(8,128)(2,1)}, bf16[320,2560]{1,0:T(8,128)(2,1)S(1)}, u32[]{:S(2)}, u32[]{:S(2)}) collective-permute-start(bf16[320,2560]{1,0:T(8,128)(2,1)} %get-tuple-element.44), channel_id=1, source_target_pairs={{0,128},{1,137},{8,136},{9,129},{128,0},{129,9},{136,8},{137,1},{2... | collective-permute-start | bytes 4915208 | tf_op jit(solution)/shard_map/ppermute | solution.py:354
  11.9 20.4 %collective-permute-start.2 = (bf16[128,5120]{1,0:T(8,128)(2,1)}, bf16[128,5120]{1,0:T(8,128)(2,1)}, u32[]{:S(2)}, u32[]{:S(2)}) collective-permute-start(bf16[128,5120]{1,0:T(8,128)(2,1)} %get-tuple-element.43.refs_1_), channel_id=1, source_target_pairs={{0,16},{1,113},{16,32},{17,1},{32,48},{33,17},{48,64},{49,33},{64,... | collective-permute-start | bytes 3932168 | tf_op jit(solution)/shard_map/ppermute | solution.py:345
  17.4 14.5 %collective-permute-start.4 = (bf16[512,1024]{1,0:T(8,128)(2,1)}, bf16[512,1024]{1,0:T(8,128)(2,1)}, u32[]{:S(2)}, u32[]{:S(2)}) collective-permute-start(bf16[512,1024]{1,0:T(8,128)(2,1)} %get-tuple-element.52.refs_8_), channel_id=1, source_target_pairs={{0,2},{1,7},{2,4},{3,1},{4,6},{5,3},{6,0},{7,5},{8,10},{9,15},{10,... | collective-permute-start | bytes 3145736 | tf_op jit(solution)/shard_map/ppermute | solution.py:345
  32.3 1.2 copy-start
  33.5 11.2 %collective-permute-start.8 = (bf16[320,2560]{1,0:T(8,128)(2,1)S(1)}, bf16[320,2560]{1,0:T(8,128)(2,1)}, u32[]{:S(2)}, u32[]{:S(2)}) collective-permute-start(bf16[320,2560]{1,0:T(8,128)(2,1)S(1)} %collective-permute-done.3.near), channel_id=1, source_target_pairs={{0,1},{1,0},{2,3},{3,2},{4,5},{5,4},{6,7},{7,6},{8,9},{9,8},{10,11... | collective-permute-start | bytes 4915208 | tf_op jit(solution)/shard_map/ppermute | solution.py:337
  33.7 23.7 %collective-permute-start.6 = (bf16[128,5120]{1,0:T(8,128)(2,1)}, bf16[128,5120]{1,0:T(8,128)(2,1)}, u32[]{:S(2)}, u32[]{:S(2)}) collective-permute-start(bf16[128,5120]{1,0:T(8,128)(2,1)} %collective-permute-done.2.refs_2_), channel_id=1, source_target_pairs={{0,16},{1,113},{16,32},{17,1},{32,48},{33,17},{48,64},{49,33},{64,... | collective-permute-start | bytes 3932168 | tf_op jit(solution)/shard_map/ppermute | solution.py:345
  37.3 20.1 %collective-permute-start.7 = (bf16[512,1024]{1,0:T(8,128)(2,1)}, bf16[512,1024]{1,0:T(8,128)(2,1)}, u32[]{:S(2)}, u32[]{:S(2)}) collective-permute-start(bf16[512,1024]{1,0:T(8,128)(2,1)} %collective-permute-done.4.refs_9_), channel_id=1, source_target_pairs={{0,2},{1,7},{2,4},{3,1},{4,6},{5,3},{6,0},{7,5},{8,10},{9,15},{10,... | collective-permute-start | bytes 3145736 | tf_op jit(solution)/shard_map/ppermute | solution.py:345
  41.7 15.8 %collective-permute-start.9 = (bf16[256,1024]{1,0:T(8,128)(2,1)}, bf16[256,1024]{1,0:T(8,128)(2,1)}, u32[]{:S(2)}, u32[]{:S(2)}) collective-permute-start(bf16[256,1024]{1,0:T(8,128)(2,1)} %slice.6), channel_id=1, source_target_pairs={{0,8},{8,0},{1,9},{9,1},{2,10},{10,2},{3,11},{11,3},{4,12},{12,4},... | collective-permute-start | bytes 1572872 | tf_op jit(solution)/shard_map/ppermute | solution.py:337
  50.9 7.3 %copy-start.6 = (s32[1,16]{1,0:T(1,128)S(1)}, s32[1,16]{1,0:T(1,128)}, u32[]{:S(2)}) copy-start(s32[1,16]{1,0:T(1,128)} %slots_ref.3) | copy-start | bytes 196
  50.9 7.3 %copy-start.9 = (s32[1,16]{1,0:T(1,128)S(1)}, s32[1,16]{1,0:T(1,128)}, u32[]{:S(2)}) copy-start(s32[1,16]{1,0:T(1,128)} %param.19) | copy-start | bytes 196
  57.5 20.3 %collective-permute-start.10 = (bf16[128,5120]{1,0:T(8,128)(2,1)}, bf16[128,5120]{1,0:T(8,128)(2,1)}, u32[]{:S(2)}, u32[]{:S(2)}) collective-permute-start(bf16[128,5120]{1,0:T(8,128)(2,1)} %collective-permute-done.6.refs_1_), channel_id=1, source_target_pairs={{0,16},{1,113},{16,32},{17,1},{32,48},{33,17},{48,64},{49,33},{64,... | collective-permute-start | bytes 3932168 | tf_op jit(solution)/shard_map/ppermute | solution.py:345
  58.3 19.5 %collective-permute-start.11 = (bf16[512,1024]{1,0:T(8,128)(2,1)}, bf16[512,1024]{1,0:T(8,128)(2,1)}, u32[]{:S(2)}, u32[]{:S(2)}) collective-permute-start(bf16[512,1024]{1,0:T(8,128)(2,1)} %get-tuple-element.52.refs_8_), channel_id=1, source_target_pairs={{0,6},{1,3},{2,0},{3,5},{4,2},{5,7},{6,4},{7,1},{8,14},{9,11},{10,... | collective-permute-start | bytes 3145736 | tf_op jit(solution)/shard_map/ppermute | solution.py:345
  59.0 12.6 %copy-start.7 = (s32[8]{0:T(128)}, s32[8]{0:T(128)S(1)}, u32[]{:S(2)}) copy-start(s32[8]{0:T(128)S(1)} %get-tuple-element.58.refs_1_) | copy-start | bytes 100
  62.0 15.8 %collective-permute-start.12 = (bf16[256,1024]{1,0:T(8,128)(2,1)}, bf16[256,1024]{1,0:T(8,128)(2,1)}, u32[]{:S(2)}, u32[]{:S(2)}) collective-permute-start(bf16[256,1024]{1,0:T(8,128)(2,1)} %slice.7), channel_id=1, source_target_pairs={{0,8},{8,0},{1,9},{9,1},{2,10},{10,2},{3,11},{11,3},{4,12},{12,4},... | collective-permute-start | bytes 1572872 | tf_op jit(solution)/shard_map/ppermute | solution.py:337
  63.3 11.1 %collective-permute-start.13 = (bf16[128,640]{1,0:T(8,128)(2,1)}, bf16[128,640]{1,0:T(8,128)(2,1)S(1)}, u32[]{:S(2)}, u32[]{:S(2)}) collective-permute-start(bf16[128,640]{1,0:T(8,128)(2,1)} %get-tuple-element.54), channel_id=1, source_target_pairs={{0,112},{1,17},{16,0},{17,33},{32,16},{33,49},{48,32},{49,65},{64,... | collective-permute-start | bytes 491528 | tf_op jit(solution)/shard_map/ppermute | solution.py:345
  63.3 49.3 %collective-permute-start.16 = (bf16[512,1024]{1,0:T(8,128)(2,1)}, bf16[512,1024]{1,0:T(8,128)(2,1)}, u32[]{:S(2)}, u32[]{:S(2)}) collective-permute-start(bf16[512,1024]{1,0:T(8,128)(2,1)} %collective-permute-done.7.refs_11_), channel_id=1, source_target_pairs={{0,8},{8,0},{1,9},{9,1},{2,10},{10,2},{3,11},{11,3},{4,12},{12,4},... | collective-permute-start | bytes 3145736 | tf_op jit(solution)/shard_map/ppermute | solution.py:337
  74.4 32.7 %copy-start.1 = (bf16[128,640]{1,0:T(8,128)(2,1)}, bf16[128,640]{1,0:T(8,128)(2,1)S(1)}, u32[]{:S(2)}) copy-start(bf16[128,640]{1,0:T(8,128)(2,1)S(1)} %collective-permute-done.13.refs_20_) | copy-start | bytes 491524
  78.9 9.9 %collective-permute-start.17 = (bf16[64,5120]{1,0:T(8,128)(2,1)S(1)}, bf16[64,5120]{1,0:T(8,128)(2,1)}, u32[]{:S(2)}, u32[]{:S(2)}) collective-permute-start(bf16[64,5120]{1,0:T(8,128)(2,1)S(1)} %constant_dynamic-slice_fusion), channel_id=1, source_target_pairs={{0,16},{1,113},{16,32},{17,1},{32,48},{33,17},{48,64},{49,33},{64,... | collective-permute-start | bytes 1966088 | tf_op jit(solution)/shard_map/ppermute | solution.py:345
  81.4 32.8 %collective-permute-start.14 = (bf16[512,1024]{1,0:T(8,128)(2,1)}, bf16[512,1024]{1,0:T(8,128)(2,1)}, u32[]{:S(2)}, u32[]{:S(2)}) collective-permute-start(bf16[512,1024]{1,0:T(8,128)(2,1)} %constant_dynamic-update-slice_fusion.refs_12_), channel_id=1, source_target_pairs={{0,2},{1,7},{2,4},{3,1},{4,6},{5,3},{6,0},{7,5},{8,10},{9,15},{10,... | collective-permute-start | bytes 3145736 | tf_op jit(solution)/shard_map/ppermute | solution.py:345
  84.3 30.5 %collective-permute-start.15 = (bf16[512,1024]{1,0:T(8,128)(2,1)}, bf16[512,1024]{1,0:T(8,128)(2,1)}, u32[]{:S(2)}, u32[]{:S(2)}) collective-permute-start(bf16[512,1024]{1,0:T(8,128)(2,1)} %constant_dynamic-update-slice_fusion.refs_12_), channel_id=1, source_target_pairs={{0,6},{1,3},{2,0},{3,5},{4,2},{5,7},{6,4},{7,1},{8,14},{9,11},{10,... | collective-permute-start | bytes 3145736 | tf_op jit(solution)/shard_map/ppermute | solution.py:345
  84.3 10.8 %collective-permute-start.21 = (bf16[128,640]{1,0:T(8,128)(2,1)}, bf16[128,640]{1,0:T(8,128)(2,1)}, u32[]{:S(2)}, u32[]{:S(2)}) collective-permute-start(bf16[128,640]{1,0:T(8,128)(2,1)} %shard_map.112), channel_id=1, source_target_pairs={{0,96},{1,33},{16,112},{17,49},{32,0},{33,65},{48,16},{49,81},{64,... | collective-permute-start | bytes 491528 | tf_op jit(solution)/shard_map/ppermute | solution.py:345
  95.0 17.5 %collective-permute-start.18 = (bf16[128,640]{1,0:T(8,128)(2,1)}, bf16[128,640]{1,0:T(8,128)(2,1)S(1)}, u32[]{:S(2)}, u32[]{:S(2)}) collective-permute-start(bf16[128,640]{1,0:T(8,128)(2,1)} %get-tuple-element.69), channel_id=1, source_target_pairs={{0,80},{1,49},{16,96},{17,65},{32,112},{33,81},{48,0},{49,97},{64,... | collective-permute-start | bytes 491528 | tf_op jit(solution)/shard_map/ppermute | solution.py:345
  95.0 12.0 %collective-permute-start.19 = (bf16[64,640]{1,0:T(8,128)(2,1)}, bf16[64,640]{1,0:T(8,128)(2,1)}, u32[]{:S(2)}, u32[]{:S(2)}) collective-permute-start(bf16[64,640]{1,0:T(8,128)(2,1)} %get-tuple-element.70), channel_id=1, source_target_pairs={{0,64},{1,65},{16,80},{17,81},{32,96},{33,97},{48,112},{49,113},{6... | collective-permute-start | bytes 245768 | tf_op jit(solution)/shard_map/ppermute | solution.py:345
  107.1 6.5 %collective-permute-start.20 = (bf16[128,640]{1,0:T(8,128)(2,1)S(1)}, bf16[128,640]{1,0:T(8,128)(2,1)S(1)}, u32[]{:S(2)}, u32[]{:S(2)}) collective-permute-start(bf16[128,640]{1,0:T(8,128)(2,1)S(1)} %collective-permute-done.13.refs_20_), channel_id=1, source_target_pairs={{0,1},{1,0},{2,3},{3,2},{4,5},{5,4},{6,7},{7,6},{8,9},{9,8},{10,11... | collective-permute-start | bytes 491528 | tf_op jit(solution)/shard_map/ppermute | solution.py:337
  112.5 1.0 copy-start.2
  112.5 1.6 %collective-permute-start.22 = (bf16[128,640]{1,0:T(8,128)(2,1)}, bf16[128,640]{1,0:T(8,128)(2,1)S(1)}, u32[]{:S(2)}, u32[]{:S(2)}) collective-permute-start(bf16[128,640]{1,0:T(8,128)(2,1)} %collective-permute-done.21.refs_22_), channel_id=1, source_target_pairs={{0,1},{1,0},{2,3},{3,2},{4,5},{5,4},{6,7},{7,6},{8,9},{9,8},{10,11... | collective-permute-start | bytes 491528 | tf_op jit(solution)/shard_map/ppermute | solution.py:337
  112.6 1.5 %collective-permute-start.23 = (bf16[128,640]{1,0:T(8,128)(2,1)S(1)}, bf16[128,640]{1,0:T(8,128)(2,1)S(1)}, u32[]{:S(2)}, u32[]{:S(2)}) collective-permute-start(bf16[128,640]{1,0:T(8,128)(2,1)S(1)} %collective-permute-done.18.refs_24_), channel_id=1, source_target_pairs={{0,1},{1,0},{2,3},{3,2},{4,5},{5,4},{6,7},{7,6},{8,9},{9,8},{10,11... | collective-permute-start | bytes 491528 | tf_op jit(solution)/shard_map/ppermute | solution.py:337
  128.3 3.5 %collective-permute-start.24 = (bf16[64,4096]{1,0:T(8,128)(2,1)}, bf16[64,4096]{1,0:T(8,128)(2,1)}, u32[]{:S(2)}, u32[]{:S(2)}) collective-permute-start(bf16[64,4096]{1,0:T(8,128)(2,1)} %shard_map.114.kept_ref), channel_id=1, source_target_pairs={{0,1},{1,0},{2,3},{3,2},{4,5},{5,4},{6,7},{7,6},{8,9},{9,8},{10,11... | collective-permute-start | bytes 1572872 | tf_op jit(solution)/shard_map/ppermute | solution.py:337
  (3 other events, 2.0 us)

commit v5 on v4

--- a/solution.py
+++ b/solution.py
@@ -135,7 +135,7 @@
         in_specs=[pl.BlockSpec(memory_space=pltpu.SMEM), hbm, hbm, hbm],
         out_specs=pl.BlockSpec(memory_space=pltpu.VMEM),
         scratch_shapes=[pltpu.SemaphoreType.DMA((6,))],
-        compiler_params=pltpu.CompilerParams(vmem_limit_bytes=255 * 2**18),
+        compiler_params=pltpu.CompilerParams(vmem_limit_bytes=62 * 2**20),
         cost_estimate=pl.CostEstimate(flops=0, bytes_accessed=8 * D * own_w.shape[0], transcendentals=0),
     )(place, own_w, near, far)
 
@@ -179,7 +179,7 @@
             out_specs=[pl.BlockSpec((height, width), lambda step, _: (0, 0)) for height in heights],
             scratch_shapes=[pltpu.VMEM((sum(heights), width), jnp.float32)],
         ),
-        compiler_params=pltpu.CompilerParams(vmem_limit_bytes=255 * 2**18),
+        compiler_params=pltpu.CompilerParams(vmem_limit_bytes=62 * 2**20),
         cost_estimate=pl.CostEstimate(
             flops=2 * sum(heights) * width * D, bytes_accessed=2 * D * (sum(heights) + width), transcendentals=0
         ),
@@ -326,7 +326,7 @@
             pltpu.SemaphoreType.DMA((HELD,)),
             pltpu.SemaphoreType.DMA((HELD,)),
         ],
-        compiler_params=pltpu.CompilerParams(vmem_limit_bytes=255 * 2**18),
+        compiler_params=pltpu.CompilerParams(vmem_limit_bytes=62 * 2**20),
         cost_estimate=pl.CostEstimate(
             flops=4 * ROWS * QD * (PLEN + RK), bytes_accessed=13 * 2**20, transcendentals=ROWS * HEADS * (PLEN + RK)
         ),

time: 137 us -> 136 us (level)
    unnamed x21 -> x31, local copies, waits for them, and re-layouts: 3.81 us -> 4.53 us
  transfers between devices with their start and end apart: 25 -> 25, of which waited for: 9 -> 10; matrix products, arithmetic and copies ran while one was open for 9% -> 8% of each run, Pallas kernels for 22% -> 22%
where the time goes in v5:
time: 136 us; the launch traced here: 134 us
  Pallas kernels  45.8 us (34%)
  starting transfers between devices  42.6 us (31%)
  waiting for transfers between devices  31.6 us (23%)
  local copies, waits for them, and re-layouts  11.8 us (9%)
  other arithmetic  2 us (1%)
    ppermute x13, starting transfers between devices, turn(): return lax.ppermute(array, (axis, 'c'), pairs)  24.4 us
    ppermute x13, waiting for transfers between devices, turn(): return lax.ppermute(array, (axis, 'c'), pairs)  23.7 us
    pallas_call x3, Pallas kernels, project(): pl.pallas_call(functools.partial(project_kernel, len(arrays), own_rows),...  18.5 us
    ppermute x11, starting transfers between devices, shift(): lax.ppermute(array, axis, [(i, (i + by) % size) for i in range(size)])  17.2 us
    pallas_call x1, Pallas kernels, attend_all(): pl.pallas_call(attend_kernel, out_shape=jax.ShapeDtypeStruct((ROWS, QD),...  13.4 us
    ppermute x11, waiting for transfers between devices, shift(): lax.ppermute(array, axis, [(i, (i + by) % size) for i in range(size)])  7.88 us
    pallas_call x1, Pallas kernels, join_weights(): pl.pallas_call(join_kernel, out_shape=jax.ShapeDtypeStruct((2 * own_w.sha...  6.31 us
    pallas_call x1, Pallas kernels, prepare(): pl.pallas_call(prepare_kernel, out_shape=(jax.ShapeDtypeStruct((2 * ROWS,...  5.02 us
  transfers between devices with their start and end apart: 25, of which 10 were waited for; matrix products, arithmetic and copies ran while one was open for 8% of the time, Pallas kernels for 22%

profile of v5, /device:TPU:1, one launch (start us, length us, event | category | flops | bytes accessed | tf_op | source)
XLA Modules:
  0.0 134.0 jit_solution(17476999029189705506)
XLA Ops:
  0.0 3.2 %collective-permute-start = (bf16[64,5120]{1,0:T(8,128)(2,1)}, bf16[64,5120]{1,0:T(8,128)(2,1)}, u32[]{:S(2)}, u32[]{:S(2)}) collective-permute-start(bf16[64,5120]{1,0:T(8,128)(2,1)} %bitcast.24), channel_id=1, source_target_pairs={{0,1},{1,0},{2,3},{3,2},{4,5},{5,4},{6,7},{7,6},{8,9},{9,8},{10,11... | collective-permute-start | bytes 1966088 | tf_op jit(solution)/shard_map/ppermute | solution.py:337
  3.9 1.4 %collective-permute-done.mate_ref = bf16[64,5120]{1,0:T(8,128)(2,1)} collective-permute-done((bf16[64,5120]{1,0:T(8,128)(2,1)}, bf16[64,5120]{1,0:T(8,128)(2,1)}, u32[]{:S(2)}, u32[]{:S(2)}) %collective-permute-start) | collective-permute-done | bytes 655392 | tf_op jit(solution)/shard_map/ppermute | solution.py:337
  5.3 5.0 %shard_map.109 = (bf16[128,5120]{1,0:T(8,128)(2,1)}, bf16[320,2560]{1,0:T(8,128)(2,1)}, bf16[512,1024]{1,0:T(8,128)(2,1)}) custom-call(s32[6]{0:T(128)} %stack.27.place_ref.refs_0_.refs_3_, s32[8]{0:T(128)} %bitcast.31, s32[1,16]{1,0:T(1,128)} %slots_ref.3, f32[1,5120]{1,0:T(1,128)} %bitcast.26, bf16[64,5120]{1,0:T(8,128)(2,1)} %bitcast.25, ...), custom_call_target="tpu_custom_call" | custom-call | flops 167772160 | bytes 8388608 | tf_op jit(solution)/shard_map/pallas_call | solution.py:63
  10.8 1.0 collective-permute-start.3
  11.8 5.6 %collective-permute-start.2 = (bf16[128,5120]{1,0:T(8,128)(2,1)}, bf16[128,5120]{1,0:T(8,128)(2,1)}, u32[]{:S(2)}, u32[]{:S(2)}) collective-permute-start(bf16[128,5120]{1,0:T(8,128)(2,1)} %get-tuple-element.43.refs_1_), channel_id=1, source_target_pairs={{0,16},{1,113},{16,32},{17,1},{32,48},{33,17},{48,64},{49,33},{64,... | collective-permute-start | bytes 3932168 | tf_op jit(solution)/shard_map/ppermute | solution.py:345
  17.4 2.5 %collective-permute-start.4 = (bf16[512,1024]{1,0:T(8,128)(2,1)}, bf16[512,1024]{1,0:T(8,128)(2,1)}, u32[]{:S(2)}, u32[]{:S(2)}) collective-permute-start(bf16[512,1024]{1,0:T(8,128)(2,1)} %get-tuple-element.52.refs_8_), channel_id=1, source_target_pairs={{0,2},{1,7},{2,4},{3,1},{4,6},{5,3},{6,0},{7,5},{8,10},{9,15},{10,... | collective-permute-start | bytes 3145736 | tf_op jit(solution)/shard_map/ppermute | solution.py:345
  19.9 12.1 %collective-permute-done.4.refs_9_ = bf16[512,1024]{1,0:T(8,128)(2,1)} collective-permute-done((bf16[512,1024]{1,0:T(8,128)(2,1)}, bf16[512,1024]{1,0:T(8,128)(2,1)}, u32[]{:S(2)}, u32[]{:S(2)}) %collective-permute-start.4) | collective-permute-done | bytes 1048608 | tf_op jit(solution)/shard_map/ppermute | solution.py:345
  32.6 3.5 %collective-permute-start.6 = (bf16[128,5120]{1,0:T(8,128)(2,1)}, bf16[128,5120]{1,0:T(8,128)(2,1)}, u32[]{:S(2)}, u32[]{:S(2)}) collective-permute-start(bf16[128,5120]{1,0:T(8,128)(2,1)} %collective-permute-done.2.refs_2_), channel_id=1, source_target_pairs={{0,16},{1,113},{16,32},{17,1},{32,48},{33,17},{48,64},{49,33},{64,... | collective-permute-start | bytes 3932168 | tf_op jit(solution)/shard_map/ppermute | solution.py:345
  36.2 2.5 %collective-permute-start.7 = (bf16[512,1024]{1,0:T(8,128)(2,1)}, bf16[512,1024]{1,0:T(8,128)(2,1)}, u32[]{:S(2)}, u32[]{:S(2)}) collective-permute-start(bf16[512,1024]{1,0:T(8,128)(2,1)} %collective-permute-done.4.refs_9_), channel_id=1, source_target_pairs={{0,2},{1,7},{2,4},{3,1},{4,6},{5,3},{6,0},{7,5},{8,10},{9,15},{10,... | collective-permute-start | bytes 3145736 | tf_op jit(solution)/shard_map/ppermute | solution.py:345
  38.7 1.9 %slice.6 = bf16[256,1024]{1,0:T(8,128)(2,1)} slice(bf16[512,1024]{1,0:T(8,128)(2,1)} %get-tuple-element.52.refs_8_), slice={[0:256], [0:1024]} | slice | bytes 1048576 | tf_op jit(solution)/shard_map/slice | solution.py:392
  40.5 2.8 %collective-permute-start.9 = (bf16[256,1024]{1,0:T(8,128)(2,1)}, bf16[256,1024]{1,0:T(8,128)(2,1)}, u32[]{:S(2)}, u32[]{:S(2)}) collective-permute-start(bf16[256,1024]{1,0:T(8,128)(2,1)} %slice.6), channel_id=1, source_target_pairs={{0,8},{8,0},{1,9},{9,1},{2,10},{10,2},{3,11},{11,3},{4,12},{12,4},... | collective-permute-start | bytes 1572872 | tf_op jit(solution)/shard_map/ppermute | solution.py:337
  43.5 6.3 %shard_map.110.refs_3_.refs_2_ = bf16[640,5120]{1,0:T(8,128)(2,1)} custom-call(s32[6]{0:T(128)} %stack.27.place_ref.refs_0_.refs_3_, bf16[320,5120]{1,0:T(8,128)(2,1)} %bitcast.20, bf16[320,2560]{1,0:T(8,128)(2,1)} %copy-done.1, bf16[320,2560]{1,0:T(8,128)(2,1)} %collective-permute-done.8.far), custom_call_target="tpu_custom_call" | custom-call | bytes 13107200 | tf_op jit(solution)/shard_map/pallas_call | solution.py:132
  49.8 6.5 %shard_map.111 = (bf16[64,640]{1,0:T(8,128)(2,1)}, bf16[128,640]{1,0:T(8,128)(2,1)}) custom-call(s32[6]{0:T(128)} %stack.27.place_ref.refs_0_.refs_3_, bf16[128,5120]{1,0:T(8,128)(2,1)} %get-tuple-element.43.refs_1_, bf16[128,5120]{1,0:T(8,128)(2,1)} %collective-permute-done.2.refs_2_, bf16[640,5120]{1,0:T(8,128)(2,1)} %shard_map.110.refs_3_.refs_2_), custom_call_target="tpu_custom_call" | custom-call | flops 1258291200 | bytes 8519680 | tf_op jit(solution)/shard_map/pallas_call | solution.py:171
  60.0 1.4 %collective-permute-start.12 = (bf16[256,1024]{1,0:T(8,128)(2,1)}, bf16[256,1024]{1,0:T(8,128)(2,1)S(1)}, u32[]{:S(2)}, u32[]{:S(2)}) collective-permute-start(bf16[256,1024]{1,0:T(8,128)(2,1)} %slice.7), channel_id=1, source_target_pairs={{0,8},{8,0},{1,9},{9,1},{2,10},{10,2},{3,11},{11,3},{4,12},{12,4},... | collective-permute-start | bytes 1572872 | tf_op jit(solution)/shard_map/ppermute | solution.py:337
  61.4 2.3 %collective-permute-start.16 = (bf16[512,1024]{1,0:T(8,128)(2,1)}, bf16[512,1024]{1,0:T(8,128)(2,1)}, u32[]{:S(2)}, u32[]{:S(2)}) collective-permute-start(bf16[512,1024]{1,0:T(8,128)(2,1)} %collective-permute-done.7.refs_11_), channel_id=1, source_target_pairs={{0,8},{8,0},{1,9},{9,1},{2,10},{10,2},{3,11},{11,3},{4,12},{12,4},... | collective-permute-start | bytes 3145736 | tf_op jit(solution)/shard_map/ppermute | solution.py:337
  63.7 5.8 %shard_map.112 = bf16[128,640]{1,0:T(8,128)(2,1)} custom-call(s32[6]{0:T(128)} %stack.27.place_ref.refs_0_.refs_3_, bf16[128,5120]{1,0:T(8,128)(2,1)} %collective-permute-done.6.refs_1_, bf16[640,5120]{1,0:T(8,128)(2,1)} %shard_map.110.refs_3_.refs_2_), custom_call_target="tpu_custom_call" | custom-call | flops 838860800 | bytes 7864320 | tf_op jit(solution)/shard_map/pallas_call | solution.py:171
  70.4 1.9 %constant_dynamic-update-slice_fusion.1 = bf16[512,1024]{1,0:T(8,128)(2,1)} fusion(bf16[256,1024]{1,0:T(8,128)(2,1)} %collective-permute-done.9), kind=kLoop, calls=%fused_computation.11 | loop fusion | bytes 1048576
  72.3 3.4 %collective-permute-done.12 = bf16[256,1024]{1,0:T(8,128)(2,1)S(1)} collective-permute-done((bf16[256,1024]{1,0:T(8,128)(2,1)}, bf16[256,1024]{1,0:T(8,128)(2,1)S(1)}, u32[]{:S(2)}, u32[]{:S(2)}) %collective-permute-start.12) | collective-permute-done | bytes 524320 | tf_op jit(solution)/shard_map/ppermute | solution.py:337
  76.5 1.1 constant_dynamic-slice_fusion
  78.3 1.9 %constant_dynamic-update-slice_fusion.refs_12_ = bf16[512,1024]{1,0:T(8,128)(2,1)} fusion(bf16[512,1024]{1,0:T(8,128)(2,1)} %constant_dynamic-update-slice_fusion.1, bf16[256,1024]{1,0:T(8,128)(2,1)} %copy-done.4), kind=kLoop, calls=%fused_computation.10 | loop fusion | bytes 1048576 | tf_op jit(solution)/shard_map/concatenate | solution.py:424
  80.2 2.9 %collective-permute-start.14 = (bf16[512,1024]{1,0:T(8,128)(2,1)}, bf16[512,1024]{1,0:T(8,128)(2,1)S(1)}, u32[]{:S(2)}, u32[]{:S(2)}) collective-permute-start(bf16[512,1024]{1,0:T(8,128)(2,1)} %constant_dynamic-update-slice_fusion.refs_12_), channel_id=1, source_target_pairs={{0,2},{1,7},{2,4},{3,1},{4,6},{5,3},{6,0},{7,5},{8,10},{9,15},{10,... | collective-permute-start | bytes 3145736 | tf_op jit(solution)/shard_map/ppermute | solution.py:345
  83.1 1.3 collective-permute-start.21
  84.3 3.2 %collective-permute-done.17.refs_2_ = bf16[64,5120]{1,0:T(8,128)(2,1)S(1)} collective-permute-done((bf16[64,5120]{1,0:T(8,128)(2,1)S(1)}, bf16[64,5120]{1,0:T(8,128)(2,1)S(1)}, u32[]{:S(2)}, u32[]{:S(2)}) %collective-permute-start.17) | collective-permute-done | bytes 655392 | tf_op jit(solution)/shard_map/ppermute | solution.py:345
  87.6 0.9 copy-done.3
  88.4 6.2 %shard_map.113 = (bf16[128,640]{1,0:T(8,128)(2,1)}, bf16[64,640]{1,0:T(8,128)(2,1)}) custom-call(s32[6]{0:T(128)} %stack.27.place_ref.refs_0_.refs_3_, bf16[128,5120]{1,0:T(8,128)(2,1)} %collective-permute-done.10.refs_1_, bf16[64,5120]{1,0:T(8,128)(2,1)} %copy-done.3, bf16[640,5120]{1,0:T(8,128)(2,1)} %shard_map.110.refs_3_.refs_2_), custom_call_target="tpu_custom_call" | custom-call | flops 1258291200 | bytes 8519680 | tf_op jit(solution)/shard_map/pallas_call | solution.py:171
  94.6 4.7 %collective-permute-start.19 = (bf16[64,640]{1,0:T(8,128)(2,1)}, bf16[64,640]{1,0:T(8,128)(2,1)}, u32[]{:S(2)}, u32[]{:S(2)}) collective-permute-start(bf16[64,640]{1,0:T(8,128)(2,1)} %get-tuple-element.70), channel_id=1, source_target_pairs={{0,64},{1,65},{16,80},{17,81},{32,96},{33,97},{48,112},{49,113},{6... | collective-permute-start | bytes 245768 | tf_op jit(solution)/shard_map/ppermute | solution.py:345
  99.4 8.1 %collective-permute-done.19.refs_19_ = bf16[64,640]{1,0:T(8,128)(2,1)} collective-permute-done((bf16[64,640]{1,0:T(8,128)(2,1)}, bf16[64,640]{1,0:T(8,128)(2,1)}, u32[]{:S(2)}, u32[]{:S(2)}) %collective-permute-start.19) | collective-permute-done | bytes 81952 | tf_op jit(solution)/shard_map/ppermute | solution.py:345
  107.4 4.5 %collective-permute-start.20 = (bf16[128,640]{1,0:T(8,128)(2,1)S(1)}, bf16[128,640]{1,0:T(8,128)(2,1)S(1)}, u32[]{:S(2)}, u32[]{:S(2)}) collective-permute-start(bf16[128,640]{1,0:T(8,128)(2,1)S(1)} %collective-permute-done.13.refs_20_), channel_id=1, source_target_pairs={{0,1},{1,0},{2,3},{3,2},{4,5},{5,4},{6,7},{7,6},{8,9},{9,8},{10,11... | collective-permute-start | bytes 491528 | tf_op jit(solution)/shard_map/ppermute | solution.py:337
  114.6 13.4 %shard_map.114.kept_ref = bf16[64,4096]{1,0:T(8,128)(2,1)} custom-call(s32[8]{0:T(128)} %get-tuple-element.57.refs_0_, s32[8]{0:T(128)} %copy-done.12, s32[16]{0:T(128)} %reshape.159.refs_2_, s32[6]{0:T(128)} %stack.27.place_ref.refs_0_.refs_3_, f32[64,128]{1,0:T(8,128)} %get-tuple-element.60.refs_4_, f32[64,128]{1,0:T(8,128)} %get-tuple-element.61.refs_5_, ...), custom_call_target="tpu_custom_call" | custom-call | flops 687865856 | bytes 13631488 | tf_op jit(solution)/shard_map/pallas_call | solution.py:314
  128.0 1.5 %collective-permute-start.24 = (bf16[64,4096]{1,0:T(8,128)(2,1)}, bf16[64,4096]{1,0:T(8,128)(2,1)}, u32[]{:S(2)}, u32[]{:S(2)}) collective-permute-start(bf16[64,4096]{1,0:T(8,128)(2,1)} %shard_map.114.kept_ref), channel_id=1, source_target_pairs={{0,1},{1,0},{2,3},{3,2},{4,5},{5,4},{6,7},{7,6},{8,9},{9,8},{10,11... | collective-permute-start | bytes 1572872 | tf_op jit(solution)/shard_map/ppermute | solution.py:337
  129.6 1.9 %collective-permute-done.24.got_ref = bf16[64,4096]{1,0:T(8,128)(2,1)} collective-permute-done((bf16[64,4096]{1,0:T(8,128)(2,1)}, bf16[64,4096]{1,0:T(8,128)(2,1)}, u32[]{:S(2)}, u32[]{:S(2)}) %collective-permute-start.24) | collective-permute-done | bytes 524320 | tf_op jit(solution)/shard_map/ppermute | solution.py:337
  131.4 2.6 %shard_map.115 = bf16[64,4096]{1,0:T(8,128)(2,1)} custom-call(s32[6]{0:T(128)} %stack.27.place_ref.refs_0_.refs_3_, s32[1,16]{1,0:T(1,128)} %slots_ref.3, bf16[64,4096]{1,0:T(8,128)(2,1)} %shard_map.114.kept_ref, bf16[64,4096]{1,0:T(8,128)(2,1)} %collective-permute-done.24.got_ref), custom_call_target="tpu_custom_call" | custom-call | flops 67108864 | bytes 1048576 | tf_op jit(solution)/shard_map/pallas_call | solution.py:94
  (75 shorter events, 10.5 us)
Async XLA Ops:
  0.0 5.3 %collective-permute-start = (bf16[64,5120]{1,0:T(8,128)(2,1)}, bf16[64,5120]{1,0:T(8,128)(2,1)}, u32[]{:S(2)}, u32[]{:S(2)}) collective-permute-start(bf16[64,5120]{1,0:T(8,128)(2,1)} %bitcast.24), channel_id=1, source_target_pairs={{0,1},{1,0},{2,3},{3,2},{4,5},{5,4},{6,7},{7,6},{8,9},{9,8},{10,11... | collective-permute-start | bytes 1966088 | tf_op jit(solution)/shard_map/ppermute | solution.py:337
  3.2 7.1 %collective-permute-start.1 = (s32[16,1]{0,1:T(1,128)}, s32[16,1]{0,1:T(1,128)S(1)}, u32[]{:S(2)}, u32[]{:S(2)}) collective-permute-start(s32[16,1]{0,1:T(1,128)} %param.21), channel_id=1, source_target_pairs={{0,1},{1,0},{2,3},{3,2},{4,5},{5,4},{6,7},{7,6},{8,9},{9,8},{10,11... | collective-permute-start | bytes 200 | tf_op jit(solution)/shard_map/ppermute | solution.py:337
  5.3 38.1 %copy-start.13 = (s32[16,1]{0,1:T(1,128)S(1)}, s32[16,1]{0,1:T(1,128)}, u32[]{:S(2)}) copy-start(s32[16,1]{0,1:T(1,128)} %param.21) | copy-start | bytes 196
  10.3 21.9 %collective-permute-start.5 = (bf16[16,128,1024]{2,1,0:T(8,128)(2,1)}, bf16[16,128,1024]{2,1,0:T(8,128)(2,1)}, u32[]{:S(2)}, u32[]{:S(2)}) collective-permute-start(bf16[16,128,1024]{2,1,0:T(8,128)(2,1)} %bitcast.21), channel_id=1, source_target_pairs={{0,1},{1,0},{2,3},{3,2},{4,5},{5,4},{6,7},{7,6},{8,9},{9,8},{10,11... | collective-permute-start | bytes 12582920 | tf_op jit(solution)/shard_map/ppermute | solution.py:337
  10.8 21.4 %collective-permute-start.3 = (bf16[320,2560]{1,0:T(8,128)(2,1)}, bf16[320,2560]{1,0:T(8,128)(2,1)S(1)}, u32[]{:S(2)}, u32[]{:S(2)}) collective-permute-start(bf16[320,2560]{1,0:T(8,128)(2,1)} %get-tuple-element.44), channel_id=1, source_target_pairs={{0,128},{1,137},{8,136},{9,129},{128,0},{129,9},{136,8},{137,1},{2... | collective-permute-start | bytes 4915208 | tf_op jit(solution)/shard_map/ppermute | solution.py:354
  11.8 20.4 %collective-permute-start.2 = (bf16[128,5120]{1,0:T(8,128)(2,1)}, bf16[128,5120]{1,0:T(8,128)(2,1)}, u32[]{:S(2)}, u32[]{:S(2)}) collective-permute-start(bf16[128,5120]{1,0:T(8,128)(2,1)} %get-tuple-element.43.refs_1_), channel_id=1, source_target_pairs={{0,16},{1,113},{16,32},{17,1},{32,48},{33,17},{48,64},{49,33},{64,... | collective-permute-start | bytes 3932168 | tf_op jit(solution)/shard_map/ppermute | solution.py:345
  17.4 14.5 %collective-permute-start.4 = (bf16[512,1024]{1,0:T(8,128)(2,1)}, bf16[512,1024]{1,0:T(8,128)(2,1)}, u32[]{:S(2)}, u32[]{:S(2)}) collective-permute-start(bf16[512,1024]{1,0:T(8,128)(2,1)} %get-tuple-element.52.refs_8_), channel_id=1, source_target_pairs={{0,2},{1,7},{2,4},{3,1},{4,6},{5,3},{6,0},{7,5},{8,10},{9,15},{10,... | collective-permute-start | bytes 3145736 | tf_op jit(solution)/shard_map/ppermute | solution.py:345
  32.3 11.2 %copy-start.1 = (bf16[320,2560]{1,0:T(8,128)(2,1)}, bf16[320,2560]{1,0:T(8,128)(2,1)S(1)}, u32[]{:S(2)}) copy-start(bf16[320,2560]{1,0:T(8,128)(2,1)S(1)} %collective-permute-done.3.near) | copy-start | bytes 4915204
  32.3 11.2 %collective-permute-start.8 = (bf16[320,2560]{1,0:T(8,128)(2,1)S(1)}, bf16[320,2560]{1,0:T(8,128)(2,1)}, u32[]{:S(2)}, u32[]{:S(2)}) collective-permute-start(bf16[320,2560]{1,0:T(8,128)(2,1)S(1)} %collective-permute-done.3.near), channel_id=1, source_target_pairs={{0,1},{1,0},{2,3},{3,2},{4,5},{5,4},{6,7},{7,6},{8,9},{9,8},{10,11... | collective-permute-start | bytes 4915208 | tf_op jit(solution)/shard_map/ppermute | solution.py:337
  32.6 23.7 %collective-permute-start.6 = (bf16[128,5120]{1,0:T(8,128)(2,1)}, bf16[128,5120]{1,0:T(8,128)(2,1)}, u32[]{:S(2)}, u32[]{:S(2)}) collective-permute-start(bf16[128,5120]{1,0:T(8,128)(2,1)} %collective-permute-done.2.refs_2_), channel_id=1, source_target_pairs={{0,16},{1,113},{16,32},{17,1},{32,48},{33,17},{48,64},{49,33},{64,... | collective-permute-start | bytes 3932168 | tf_op jit(solution)/shard_map/ppermute | solution.py:345
  36.2 20.1 %collective-permute-start.7 = (bf16[512,1024]{1,0:T(8,128)(2,1)}, bf16[512,1024]{1,0:T(8,128)(2,1)}, u32[]{:S(2)}, u32[]{:S(2)}) collective-permute-start(bf16[512,1024]{1,0:T(8,128)(2,1)} %collective-permute-done.4.refs_9_), channel_id=1, source_target_pairs={{0,2},{1,7},{2,4},{3,1},{4,6},{5,3},{6,0},{7,5},{8,10},{9,15},{10,... | collective-permute-start | bytes 3145736 | tf_op jit(solution)/shard_map/ppermute | solution.py:345
  40.5 15.8 %collective-permute-start.9 = (bf16[256,1024]{1,0:T(8,128)(2,1)}, bf16[256,1024]{1,0:T(8,128)(2,1)}, u32[]{:S(2)}, u32[]{:S(2)}) collective-permute-start(bf16[256,1024]{1,0:T(8,128)(2,1)} %slice.6), channel_id=1, source_target_pairs={{0,8},{8,0},{1,9},{9,1},{2,10},{10,2},{3,11},{11,3},{4,12},{12,4},... | collective-permute-start | bytes 1572872 | tf_op jit(solution)/shard_map/ppermute | solution.py:337
  49.8 7.4 %copy-start = (bf16[512,1024]{1,0:T(8,128)(2,1)S(1)}, bf16[512,1024]{1,0:T(8,128)(2,1)}, u32[]{:S(2)}) copy-start(bf16[512,1024]{1,0:T(8,128)(2,1)} %get-tuple-element.52.refs_8_) | copy-start | bytes 3145732
  49.8 7.3 %copy-start.11 = (s32[1,16]{1,0:T(1,128)S(1)}, s32[1,16]{1,0:T(1,128)}, u32[]{:S(2)}) copy-start(s32[1,16]{1,0:T(1,128)} %slots_ref.3) | copy-start | bytes 196
  49.8 7.3 %copy-start.14 = (s32[1,16]{1,0:T(1,128)S(1)}, s32[1,16]{1,0:T(1,128)}, u32[]{:S(2)}) copy-start(s32[1,16]{1,0:T(1,128)} %param.19) | copy-start | bytes 196
  56.3 19.4 %collective-permute-start.10 = (bf16[128,5120]{1,0:T(8,128)(2,1)}, bf16[128,5120]{1,0:T(8,128)(2,1)}, u32[]{:S(2)}, u32[]{:S(2)}) collective-permute-start(bf16[128,5120]{1,0:T(8,128)(2,1)} %collective-permute-done.6.refs_1_), channel_id=1, source_target_pairs={{0,16},{1,113},{16,32},{17,1},{32,48},{33,17},{48,64},{49,33},{64,... | collective-permute-start | bytes 3932168 | tf_op jit(solution)/shard_map/ppermute | solution.py:345
  57.1 18.6 %collective-permute-start.11 = (bf16[512,1024]{1,0:T(8,128)(2,1)S(1)}, bf16[512,1024]{1,0:T(8,128)(2,1)}, u32[]{:S(2)}, u32[]{:S(2)}) collective-permute-start(bf16[512,1024]{1,0:T(8,128)(2,1)S(1)} %copy-done), channel_id=1, source_target_pairs={{0,6},{1,3},{2,0},{3,5},{4,2},{5,7},{6,4},{7,1},{8,14},{9,11},{10,... | collective-permute-start | bytes 3145736 | tf_op jit(solution)/shard_map/ppermute | solution.py:345
  60.0 15.7 %collective-permute-start.12 = (bf16[256,1024]{1,0:T(8,128)(2,1)}, bf16[256,1024]{1,0:T(8,128)(2,1)S(1)}, u32[]{:S(2)}, u32[]{:S(2)}) collective-permute-start(bf16[256,1024]{1,0:T(8,128)(2,1)} %slice.7), channel_id=1, source_target_pairs={{0,8},{8,0},{1,9},{9,1},{2,10},{10,2},{3,11},{11,3},{4,12},{12,4},... | collective-permute-start | bytes 1572872 | tf_op jit(solution)/shard_map/ppermute | solution.py:337
  61.4 10.9 %collective-permute-start.13 = (bf16[128,640]{1,0:T(8,128)(2,1)}, bf16[128,640]{1,0:T(8,128)(2,1)S(1)}, u32[]{:S(2)}, u32[]{:S(2)}) collective-permute-start(bf16[128,640]{1,0:T(8,128)(2,1)} %get-tuple-element.54), channel_id=1, source_target_pairs={{0,112},{1,17},{16,0},{17,33},{32,16},{33,49},{48,32},{49,65},{64,... | collective-permute-start | bytes 491528 | tf_op jit(solution)/shard_map/ppermute | solution.py:345
  61.4 50.7 %collective-permute-start.16 = (bf16[512,1024]{1,0:T(8,128)(2,1)}, bf16[512,1024]{1,0:T(8,128)(2,1)}, u32[]{:S(2)}, u32[]{:S(2)}) collective-permute-start(bf16[512,1024]{1,0:T(8,128)(2,1)} %collective-permute-done.7.refs_11_), channel_id=1, source_target_pairs={{0,8},{8,0},{1,9},{9,1},{2,10},{10,2},{3,11},{11,3},{4,12},{12,4},... | collective-permute-start | bytes 3145736 | tf_op jit(solution)/shard_map/ppermute | solution.py:337
  72.3 35.1 %copy-start.5 = (bf16[128,640]{1,0:T(8,128)(2,1)}, bf16[128,640]{1,0:T(8,128)(2,1)S(1)}, u32[]{:S(2)}) copy-start(bf16[128,640]{1,0:T(8,128)(2,1)S(1)} %collective-permute-done.13.refs_20_) | copy-start | bytes 491524
  77.6 9.9 %collective-permute-start.17 = (bf16[64,5120]{1,0:T(8,128)(2,1)S(1)}, bf16[64,5120]{1,0:T(8,128)(2,1)S(1)}, u32[]{:S(2)}, u32[]{:S(2)}) collective-permute-start(bf16[64,5120]{1,0:T(8,128)(2,1)S(1)} %constant_dynamic-slice_fusion), channel_id=1, source_target_pairs={{0,16},{1,113},{16,32},{17,1},{32,48},{33,17},{48,64},{49,33},{64,... | collective-permute-start | bytes 1966088 | tf_op jit(solution)/shard_map/ppermute | solution.py:345
  80.2 33.4 %collective-permute-start.14 = (bf16[512,1024]{1,0:T(8,128)(2,1)}, bf16[512,1024]{1,0:T(8,128)(2,1)S(1)}, u32[]{:S(2)}, u32[]{:S(2)}) collective-permute-start(bf16[512,1024]{1,0:T(8,128)(2,1)} %constant_dynamic-update-slice_fusion.refs_12_), channel_id=1, source_target_pairs={{0,2},{1,7},{2,4},{3,1},{4,6},{5,3},{6,0},{7,5},{8,10},{9,15},{10,... | collective-permute-start | bytes 3145736 | tf_op jit(solution)/shard_map/ppermute | solution.py:345
  83.0 30.6 %collective-permute-start.15 = (bf16[512,1024]{1,0:T(8,128)(2,1)}, bf16[512,1024]{1,0:T(8,128)(2,1)}, u32[]{:S(2)}, u32[]{:S(2)}) collective-permute-start(bf16[512,1024]{1,0:T(8,128)(2,1)} %constant_dynamic-update-slice_fusion.refs_12_), channel_id=1, source_target_pairs={{0,6},{1,3},{2,0},{3,5},{4,2},{5,7},{6,4},{7,1},{8,14},{9,11},{10,... | collective-permute-start | bytes 3145736 | tf_op jit(solution)/shard_map/ppermute | solution.py:345
  83.1 11.6 %collective-permute-start.21 = (bf16[128,640]{1,0:T(8,128)(2,1)}, bf16[128,640]{1,0:T(8,128)(2,1)S(1)}, u32[]{:S(2)}, u32[]{:S(2)}) collective-permute-start(bf16[128,640]{1,0:T(8,128)(2,1)} %shard_map.112), channel_id=1, source_target_pairs={{0,96},{1,33},{16,112},{17,49},{32,0},{33,65},{48,16},{49,81},{64,... | collective-permute-start | bytes 491528 | tf_op jit(solution)/shard_map/ppermute | solution.py:345
  94.6 17.3 %collective-permute-start.18 = (bf16[128,640]{1,0:T(8,128)(2,1)}, bf16[128,640]{1,0:T(8,128)(2,1)S(1)}, u32[]{:S(2)}, u32[]{:S(2)}) collective-permute-start(bf16[128,640]{1,0:T(8,128)(2,1)} %get-tuple-element.69), channel_id=1, source_target_pairs={{0,80},{1,49},{16,96},{17,65},{32,112},{33,81},{48,0},{49,97},{64,... | collective-permute-start | bytes 491528 | tf_op jit(solution)/shard_map/ppermute | solution.py:345
  94.6 19.0 %copy-start.6 = (bf16[128,640]{1,0:T(8,128)(2,1)}, bf16[128,640]{1,0:T(8,128)(2,1)S(1)}, u32[]{:S(2)}) copy-start(bf16[128,640]{1,0:T(8,128)(2,1)S(1)} %collective-permute-done.21.refs_22_) | copy-start | bytes 491524
  94.6 12.8 %collective-permute-start.19 = (bf16[64,640]{1,0:T(8,128)(2,1)}, bf16[64,640]{1,0:T(8,128)(2,1)}, u32[]{:S(2)}, u32[]{:S(2)}) collective-permute-start(bf16[64,640]{1,0:T(8,128)(2,1)} %get-tuple-element.70), channel_id=1, source_target_pairs={{0,64},{1,65},{16,80},{17,81},{32,96},{33,97},{48,112},{49,113},{6... | collective-permute-start | bytes 245768 | tf_op jit(solution)/shard_map/ppermute | solution.py:345
  107.4 5.6 %collective-permute-start.20 = (bf16[128,640]{1,0:T(8,128)(2,1)S(1)}, bf16[128,640]{1,0:T(8,128)(2,1)S(1)}, u32[]{:S(2)}, u32[]{:S(2)}) collective-permute-start(bf16[128,640]{1,0:T(8,128)(2,1)S(1)} %collective-permute-done.13.refs_20_), channel_id=1, source_target_pairs={{0,1},{1,0},{2,3},{3,2},{4,5},{5,4},{6,7},{7,6},{8,9},{9,8},{10,11... | collective-permute-start | bytes 491528 | tf_op jit(solution)/shard_map/ppermute | solution.py:337
  112.0 1.4 %collective-permute-start.22 = (bf16[128,640]{1,0:T(8,128)(2,1)S(1)}, bf16[128,640]{1,0:T(8,128)(2,1)S(1)}, u32[]{:S(2)}, u32[]{:S(2)}) collective-permute-start(bf16[128,640]{1,0:T(8,128)(2,1)S(1)} %collective-permute-done.21.refs_22_), channel_id=1, source_target_pairs={{0,1},{1,0},{2,3},{3,2},{4,5},{5,4},{6,7},{7,6},{8,9},{9,8},{10,11... | collective-permute-start | bytes 491528 | tf_op jit(solution)/shard_map/ppermute | solution.py:337
  112.1 1.5 %collective-permute-start.23 = (bf16[128,640]{1,0:T(8,128)(2,1)S(1)}, bf16[128,640]{1,0:T(8,128)(2,1)S(1)}, u32[]{:S(2)}, u32[]{:S(2)}) collective-permute-start(bf16[128,640]{1,0:T(8,128)(2,1)S(1)} %collective-permute-done.18.refs_24_), channel_id=1, source_target_pairs={{0,1},{1,0},{2,3},{3,2},{4,5},{5,4},{6,7},{7,6},{8,9},{9,8},{10,11... | collective-permute-start | bytes 491528 | tf_op jit(solution)/shard_map/ppermute | solution.py:337
  128.0 3.4 %collective-permute-start.24 = (bf16[64,4096]{1,0:T(8,128)(2,1)}, bf16[64,4096]{1,0:T(8,128)(2,1)}, u32[]{:S(2)}, u32[]{:S(2)}) collective-permute-start(bf16[64,4096]{1,0:T(8,128)(2,1)} %shard_map.114.kept_ref), channel_id=1, source_target_pairs={{0,1},{1,0},{2,3},{3,2},{4,5},{5,4},{6,7},{7,6},{8,9},{9,8},{10,11... | collective-permute-start | bytes 1572872 | tf_op jit(solution)/shard_map/ppermute | solution.py:337
  (8 other events, 7.4 us)
